TPU v7x, 32 devices: a whole 2x2x4 slice. The times are simulated.
32 devices in a mesh: rep: 8 (over z, x), shard: 4 (over y, core).
Axes of the slice: x: 2, y: 2, z: 4, core: 2. Of those that a mesh axis runs over, the one named last changes fastest.
Arguments:
- x_in: bfloat16 [4096, 2048], P(('rep', 'shard')), may hold values from -6 to 6
- cotangent: bfloat16 [4096, 2048], P(('rep', 'shard')), may hold values from -6 to 6
- seq_lengths: int32 [8, 4], P('rep'), may hold values from 1 to 256, 512 in all within a row
- seq_order: int32 [8, 4], P('rep'), may hold values from 0 to 3, each once within a row
- valid: int32 [4096], P(('rep', 'shard')), may hold values 0 or 1
- norm_gain: float32 [2048], replicated, may hold values from 0.5 to 1.5
- w_in: bfloat16 [2048, 8512], P('shard'), may hold values from -0.125 to 0.125
- conv_w: float32 [4, 4352], replicated, may hold values from -3 to 3
- conv_b: float32 [4352], replicated, may hold values from -2 to 2
- dt_bias: float32 [64], replicated, may hold values from -9 to -3
- a_log: float32 [64], replicated, may hold values from 0 to 2
- d_skip: float32 [64], replicated, may hold values from 0.5 to 1.5
- gated_gain: float32 [4096], replicated, may hold values from 0.5 to 1.5
- w_out: bfloat16 [4096, 2048], P('shard'), may hold values from -0.09375 to 0.09375
Outputs:
- block_out: bfloat16 [4096, 2048], P(('rep', 'shard'))
- grad_in: bfloat16 [4096, 2048], P(('rep', 'shard'))
- grad_norm_gain: float32 [2048], replicated
- grad_w_in: float32 [2048, 8512], P('shard')
- grad_conv_w: float32 [4, 4352], replicated
- grad_conv_b: float32 [4352], replicated
- grad_dt_bias: float32 [64], replicated
- grad_a_log: float32 [64], replicated
- grad_d_skip: float32 [64], replicated
- grad_gated_gain: float32 [4096], replicated
- grad_w_out: float32 [4096, 2048], P('shard')
- rms_residual: float32 [], replicated
- rms_mixer: float32 [], replicated
Inputs may be any that keep to these rules, and one draw needn't show every extreme that they name: `seq_lengths`: each row holds the lengths of one group's 4 sequences; they sum to 512 and the longest is exactly 256. `seq_order`: each row is a permutation of 0 to 3.
All inputs are finite; a program needn't handle non-finite values. No bound on the sum of `valid` on one device may be relied on, other than what follows from the above.
Results may differ from a plain program's by a relative error of at most 0.0097.
Values may be sent and summed in bfloat16 or wider, within the bound.
A program may use at most 448 MiB of HBM per device.

v0:
```python
import jax
import jax.numpy as jnp
from jax import lax
from jax.sharding import PartitionSpec as P

D = 2048
H = 64
P_SIZE = 64
N = 128
KW = 4
SPAN = 128
DI = 4096
CONVW = 4352


EPSILON = 1e-05
HIGHEST = lax.Precision.HIGHEST


def from_behind(block, axis, distance):
    devices = range(lax.axis_size(axis))
    route = [(i - distance, i) for i in devices if i - distance in devices]
    return lax.ppermute(block, axis, route)


def prefix(value, axis, join, neutral, backward):
    count, mine = (lax.axis_size(axis), lax.axis_index(axis))
    pieces = jax.tree.map(lambda part: lax.all_gather(part, axis), value)
    if backward:
        pieces = jax.tree.map(lambda part: part[::-1], pieces)
        mine = count - 1 - mine
    running = jax.tree.map(
        lambda part, zero: jnp.full_like(part, 0) + jnp.asarray(zero, part.dtype), value, neutral
    )

    def lap(position, running):
        longer = join(running, jax.tree.map(lambda part: part[position], pieces))
        return jax.tree.map(lambda new, old: jnp.where(position < mine, new, old), longer, running)

    return lax.fori_loop(0, count - 1, lap, running)


def slot_tables(seq_lengths, seq_order, slot_ids):
    seq_count = seq_lengths.shape[0]
    numbers = jnp.arange(seq_count, dtype=jnp.int32)
    chosen = (seq_order[:, None] == numbers[None, :]).astype(jnp.int32)
    given_start = jnp.cumsum(seq_lengths) - seq_lengths
    owner_length = jnp.sum(chosen * seq_lengths[None, :], axis=1)
    owner_start = jnp.cumsum(owner_length) - owner_length
    owner_from = jnp.sum(chosen * given_start[None, :], axis=1)
    placed_at = jnp.sum(chosen * owner_start[:, None], axis=0)
    column = slot_ids[:, None]
    within = (column >= owner_start[None, :]) & (column < (owner_start + owner_length)[None, :])
    offset = column - owner_start[None, :]
    source = jnp.sum(jnp.where(within, offset + owner_from[None, :], 0), axis=1)
    position = jnp.sum(jnp.where(within, offset, 0), axis=1)
    given_within = (column >= given_start[None, :]) & (
        column < (given_start + seq_lengths)[None, :]
    )
    target = jnp.sum(
        jnp.where(given_within, column - given_start[None, :] + placed_at[None, :], 0), axis=1
    )
    return (source, target, position)


def norm_apply(rows_in, gain_row):
    inverse_rms = lax.rsqrt(jnp.mean(rows_in * rows_in, axis=1, keepdims=True) + EPSILON)
    return rows_in * inverse_rms * gain_row[None, :]


def gated_norm(mixed, gate_rows, gain_row):
    product = mixed * jax.nn.silu(gate_rows)
    inverse_rms = lax.rsqrt(jnp.mean(product * product, axis=1, keepdims=True) + EPSILON)
    return product * inverse_rms * gain_row[None, :]


def conv_apply(extended, conv_w, conv_b, position):
    row_count = extended.shape[0] - (KW - 1)
    result = jnp.zeros((row_count, extended.shape[1]), jnp.float32) + conv_b[None, :]
    for column in range(KW):
        reach = (position >= KW - 1 - column).astype(jnp.float32)[:, None]
        result = result + conv_w[column][None, :] * extended[column : column + row_count] * reach
    return jax.nn.silu(result)


def split_mixer(activated, dt_raw, dt_bias, a_log):
    row_count = activated.shape[0]
    values = activated[:, :DI].reshape(row_count, H, P_SIZE)
    input_map = activated[:, DI : DI + N]
    output_map = activated[:, DI + N : DI + 2 * N]
    step_size = jax.nn.softplus(dt_raw + dt_bias[None, :])
    log_decay = -step_size * jnp.exp(a_log)[None, :]
    return (values, input_map, output_map, log_decay, step_size)


def scan_block(carry_state, pieces, d_skip, with_output):
    values, input_map, output_map, log_decay, step_size, position = pieces
    length = log_decay.shape[0]
    final_row = length - 1
    local = jnp.arange(length, dtype=jnp.int32)
    running = jnp.cumsum(log_decay, axis=0)
    scaled = values * step_size[:, :, None]
    begins = local - position
    reach_end = local >= begins[final_row]
    to_end = jnp.where(reach_end[:, None], running[final_row][None, :] - running, 0.0)
    tail_weight = jnp.exp(to_end) * reach_end[:, None].astype(jnp.float32)
    fresh = jnp.einsum(
        "jhp,jn->hpn", scaled * tail_weight[:, :, None], input_map, precision=HIGHEST
    )
    carried = jnp.where(position[final_row] >= length, jnp.exp(running[final_row]), 0.0)
    next_state = carried[:, None, None] * carry_state + fresh
    if not with_output:
        return (next_state, carried)
    causal = (local[None, :] <= local[:, None]) & (local[None, :] >= begins[:, None])
    heads_first = running.T
    spread = heads_first[:, :, None] - heads_first[:, None, :]
    decay_matrix = jnp.exp(jnp.where(causal[None], spread, 0.0)) * causal[None].astype(jnp.float32)
    pair_products = jnp.dot(output_map, input_map.T, precision=HIGHEST)
    diagonal_part = jnp.einsum(
        "hij,jhp->ihp", decay_matrix * pair_products[None], scaled, precision=HIGHEST
    )
    entering = jnp.where((position >= local + 1)[:, None], jnp.exp(running), 0.0)
    earlier_part = (
        jnp.einsum("in,hpn->ihp", output_map, carry_state, precision=HIGHEST) * entering[:, :, None]
    )
    outputs = diagonal_part + earlier_part + d_skip[None, :, None] * values
    return (next_state, outputs)


def to_blocks(pieces):
    return tuple(
        (member.reshape((member.shape[0] // SPAN, SPAN) + member.shape[1:]) for member in pieces)
    )


def ssd_run(activated, dt_raw, position, dt_bias, a_log, d_skip, start_state):
    blocks = to_blocks(split_mixer(activated, dt_raw, dt_bias, a_log) + (position,))

    def advance(state, block):
        return scan_block(state, block, d_skip, True)

    final_state, outputs = lax.scan(jax.checkpoint(advance), start_state, blocks)
    return (outputs.reshape(activated.shape[0], DI), final_state)


def ssd_summary(activated, dt_raw, position, dt_bias, a_log):
    blocks = to_blocks(split_mixer(activated, dt_raw, dt_bias, a_log) + (position,))

    def advance(carry, block):
        next_state, carried = scan_block(carry[0], block, None, False)
        return ((next_state, carry[1] * carried), None)

    start_value = (jnp.zeros((H, P_SIZE, N), jnp.float32), jnp.ones((H,), jnp.float32))
    (state, factor), unused = lax.scan(advance, start_value, blocks)
    return (state, factor)


def chain_states(earlier, later):
    return (earlier[0] * later[0], earlier[1] * later[0][:, None, None] + later[1])


def pick_rows(wanted, carry, piece):
    present = (wanted >= 0) & (wanted < piece.shape[0])
    rows_taken = jnp.take(piece, jnp.clip(wanted, 0, piece.shape[0] - 1), axis=0)
    return jnp.where(present[:, None], rows_taken, carry)


def on_device(
    x_in,
    cotangent,
    seq_lengths,
    seq_order,
    valid,
    norm_gain,
    w_in,
    conv_w,
    conv_b,
    dt_bias,
    a_log,
    d_skip,
    gated_gain,
    w_out,
):
    row_count = x_in.shape[0]
    slot_ids = lax.axis_index("shard") * row_count + jnp.arange(row_count, dtype=jnp.int32)
    source, target, position = slot_tables(seq_lengths[0], seq_order[0], slot_ids)
    arrived = pick_rows(
        source, jnp.zeros_like(x_in), lax.all_gather(x_in, "shard", axis=0, tiled=True)
    )
    resid = arrived.astype(jnp.float32)
    normed = norm_apply(resid, norm_gain).astype(jnp.bfloat16)
    columns = normed
    projected_sum = jnp.dot(
        columns,
        lax.all_gather(w_in, "shard", axis=0, tiled=True),
        preferred_element_type=jnp.float32,
    )
    projected = projected_sum.astype(jnp.bfloat16)
    gate_rows = projected[:, :DI].astype(jnp.float32)
    conv_in = projected[:, DI : DI + CONVW]
    dt_raw = projected[:, DI + CONVW :].astype(jnp.float32)
    rim_rows = from_behind(conv_in[row_count - (KW - 1) :], "shard", 1)
    extended = jnp.concatenate([rim_rows, conv_in], axis=0).astype(jnp.float32)
    activated = lax.optimization_barrier(
        conv_apply(extended, conv_w, conv_b, position).astype(jnp.bfloat16)
    ).astype(jnp.float32)
    end_state, end_factor = ssd_summary(activated, dt_raw, position, dt_bias, a_log)
    identity = (jnp.ones((H,), jnp.float32), jnp.zeros((H, P_SIZE, N), jnp.float32))
    unused_factor, start_state = prefix(
        (end_factor, end_state), "shard", chain_states, identity, False
    )

    def mixer_out(activated_in, dt_in, bias_in, decay_in, skip_in, state_in):
        return ssd_run(activated_in, dt_in, position, bias_in, decay_in, skip_in, state_in)[0]

    mixed, out_back = jax.vjp(mixer_out, activated, dt_raw, dt_bias, a_log, d_skip, start_state)
    normed_out = gated_norm(mixed, gate_rows, gated_gain).astype(jnp.bfloat16)
    columns = normed_out
    branch = jnp.dot(
        columns,
        lax.all_gather(w_out, "shard", axis=0, tiled=True),
        preferred_element_type=jnp.float32,
    )
    total_rows = resid + branch
    block_out = total_rows.astype(jnp.bfloat16)
    weights_valid = valid.astype(jnp.float32)
    square_total = jnp.sum(weights_valid * jnp.sum(total_rows * total_rows, axis=1))
    square_branch = jnp.sum(weights_valid * jnp.sum(branch * branch, axis=1))
    valid_count = jnp.sum(weights_valid)
    grad_branch = jnp.where(valid[:, None] > 0, cotangent, jnp.zeros_like(cotangent))
    columns = normed_out
    grad_w_out = lax.psum_scatter(
        lax.dot_general(
            columns, grad_branch, (((0,), (0,)), ((), ())), preferred_element_type=jnp.float32
        ),
        "shard",
        scatter_dimension=0,
        tiled=True,
    )
    grad_normed_out = lax.dot_general(
        grad_branch,
        lax.all_gather(w_out, "shard", axis=0, tiled=True),
        (((1,), (1,)), ((), ())),
        preferred_element_type=jnp.float32,
    )
    unused_gated, gated_back = jax.vjp(gated_norm, mixed, gate_rows, gated_gain)
    grad_mixed, grad_gate, grad_gated_gain = gated_back(grad_normed_out)
    grad_act_out, grad_dt_out, grad_bias_out, grad_decay_out, grad_d_skip, grad_start = out_back(
        grad_mixed
    )
    unused_product, later_grad = prefix(
        (end_factor, grad_start), "shard", chain_states, identity, True
    )
    grad_factor = jnp.sum(later_grad * start_state, axis=(1, 2))

    def mixer_summary(activated_in, dt_in, bias_in, decay_in):
        return ssd_summary(activated_in, dt_in, position, bias_in, decay_in)

    unused_summary, summary_back = jax.vjp(mixer_summary, activated, dt_raw, dt_bias, a_log)
    grad_act_sum, grad_dt_sum, grad_bias_sum, grad_decay_sum = summary_back(
        (later_grad, grad_factor)
    )
    grad_activated = grad_act_out + grad_act_sum

    def conv_local(extended_in, weight_in, bias_in):
        return conv_apply(extended_in, weight_in, bias_in, position)

    unused_conv, conv_back = jax.vjp(conv_local, extended, conv_w, conv_b)
    grad_extended, grad_conv_w, grad_conv_b = conv_back(grad_activated)
    rim_back = from_behind(grad_extended[: KW - 1].astype(jnp.bfloat16), "shard", -1).astype(
        jnp.float32
    )
    grad_conv_in = grad_extended[KW - 1 :] + jnp.pad(rim_back, ((row_count - (KW - 1), 0), (0, 0)))
    grad_projected = jnp.concatenate(
        [grad_gate, grad_conv_in, grad_dt_out + grad_dt_sum], axis=1
    ).astype(jnp.bfloat16)
    columns = normed
    grad_w_in = lax.psum_scatter(
        lax.dot_general(
            columns, grad_projected, (((0,), (0,)), ((), ())), preferred_element_type=jnp.float32
        ),
        "shard",
        scatter_dimension=0,
        tiled=True,
    )
    grad_normed = lax.dot_general(
        grad_projected,
        lax.all_gather(w_in, "shard", axis=0, tiled=True),
        (((1,), (1,)), ((), ())),
        preferred_element_type=jnp.float32,
    )
    unused_norm, norm_back = jax.vjp(norm_apply, resid, norm_gain)
    grad_resid, grad_norm_gain = norm_back(grad_normed)
    grad_rows = (grad_resid + grad_branch.astype(jnp.float32)).astype(jnp.bfloat16)
    grad_in = pick_rows(
        target, jnp.zeros_like(grad_rows), lax.all_gather(grad_rows, "shard", axis=0, tiled=True)
    )
    grad_w_in, grad_w_out = lax.psum((grad_w_in, grad_w_out), "rep")
    summed = lax.psum(
        (
            grad_norm_gain,
            grad_conv_w,
            grad_conv_b,
            grad_bias_out + grad_bias_sum,
            grad_decay_out + grad_decay_sum,
            grad_d_skip,
            grad_gated_gain,
            square_total,
            square_branch,
            valid_count,
        ),
        ("rep", "shard"),
    )
    count_all = jnp.maximum(summed[9], 1.0)
    rms_residual = jnp.sqrt(summed[7] / (count_all * D))
    rms_mixer = jnp.sqrt(summed[8] / (count_all * D))
    return (
        block_out,
        grad_in,
        summed[0],
        grad_w_in,
        summed[1],
        summed[2],
        summed[3],
        summed[4],
        summed[5],
        summed[6],
        grad_w_out,
        rms_residual,
        rms_mixer,
    )


def solution(mesh):
    in_specs = (
        P(("rep", "shard"), None),
        P(("rep", "shard"), None),
        P("rep", None),
        P("rep", None),
        P(("rep", "shard")),
        P(),
        P("shard", None),
        P(),
        P(),
        P(),
        P(),
        P(),
        P(),
        P("shard", None),
    )
    out_specs = (
        P(("rep", "shard"), None),
        P(("rep", "shard"), None),
        P(),
        P("shard", None),
        P(),
        P(),
        P(),
        P(),
        P(),
        P(),
        P("shard", None),
        P(),
        P(),
    )
    return jax.shard_map(
        on_device, mesh=mesh, in_specs=in_specs, out_specs=out_specs, check_vma=False
    )
```

profile of v0, /device:TPU:0, one launch (start us, length us, event | category | flops | bytes accessed | tf_op | source)
XLA Modules:
  0.0 2248.8 jit_solution(1582988732969053887)
XLA Ops:
  13.5 21.4 all-gather.10.cloned.1.call-done
  34.9 3.3 gather_fusion
  38.6 209.2 %all-gather.12.cloned.1.call-done = bf16[2048,8512]{0,1:T(8,128)(2,1)} async-done(((bf16[512,8512]{0,1:T(8,128)(2,1)}), bf16[2048,8512]{0,1:T(8,128)(2,1)}) %all-gather.12.cloned.1.call-update) | async-done | bytes 34865168 | tf_op jit(solution)/shard_map/all_gather | solution.py:195
  247.8 17.6 convolution_convert_fusion
  273.2 3.0 copy.235
  283.4 2.9 copy.238
  286.3 3.9 convolution_add_fusion
  291.1 5.2 all-gather.2
  299.2 3.2 copy.230
  304.2 44.6 %all-gather.18.cloned.1.call-done = f32[256,64,128]{2,1,0:T(8,128)} async-done(((f32[64,64,128]{2,1,0:T(8,128)}), f32[256,64,128]{2,1,0:T(8,128)}) %all-gather.18.cloned.1.call-update) | async-done | bytes 8388624 | tf_op jit(solution)/shard_map/all_gather | solution.py:28
  348.8 6.3 while.20
  357.2 9.8 fusion.26
  367.0 3.3 copy.240
  370.4 3.9 multiply_reduce_fusion.16
  374.3 81.8 %all-gather.14.cloned.1.call-done = bf16[4096,2048]{1,0:T(8,128)(2,1)} async-done(((bf16[1024,2048]{1,0:T(8,128)(2,1)}), bf16[4096,2048]{1,0:T(8,128)(2,1)}) %all-gather.14.cloned.1.call-update) | async-done | bytes 16777232 | tf_op jit(solution)/shard_map/all_gather | solution.py:221
  456.2 14.1 multiply_reduce_fusion.5
  470.3 6.1 fusion.22
  476.5 2.9 copy.242
  486.8 3.1 fusion.100
  494.6 4.0 multiply_reduce_fusion.13
  498.7 11.4 fusion.13
  510.2 7.1 multiply_reduce_fusion.6
  526.5 5.3 multiply_add_fusion.1
  532.5 17.7 fusion.141
  554.0 2.9 copy.248
  556.9 6.0 fusion.63
  563.8 3.5 fusion.69
  567.6 22.8 %all-gather.20.cloned.1.call-done = f32[256,64,128]{2,1,0:T(8,128)} async-done(((f32[64,64,128]{2,1,0:T(8,128)}), f32[256,64,128]{2,1,0:T(8,128)}) %all-gather.20.cloned.1.call-update) | async-done | bytes 8388624 | tf_op jit(solution)/shard_map/all_gather | solution.py:28
  590.3 8.5 rev.7
  598.8 15.7 while.21
  599.5 3.7 fusion.171
  603.9 4.9 fusion.171
  609.5 4.8 fusion.171
  614.6 6.1 multiply_reduce_fusion.7
  625.6 3.6 copy.250
  629.3 5.8 fusion.66
  635.2 5.4 multiply_reduce_fusion.4
  645.6 26.7 %fusion.87 = f32[2048,8512]{0,1:T(8,128)} fusion(bf16[128,64]{1,0:T(8,128)(2,1)S(1)} %add_convert_fusion, bf16[128,4352]{1,0:T(8,128)(2,1)S(1)} %fusion.16, bf16[128,4096]{1,0:T(8,128)(2,1)} %get-tuple-element.697, f32[2048]{0:T(1024)S(1)} %copy-done.17, f32[128]{0:T(128)S(1)} %copy-done.40, bf16[128,2048]{1,0:T(8,128)(2,1)S(1)} %gather_fusion, ...), kind=kOutput, calls=%fused_computation.131 | convolution fusion | flops 4470849536 | bytes 72442624 | tf_op jit(solution)/shard_map/dot_general | solution.py:279
  672.4 14.7 fusion.88
  687.2 9.6 multiply_reduce_fusion.17
  699.1 128.9 %reduce-scatter.5.cloned.1.call-done = f32[1024,2048]{1,0:T(8,128)} async-done(((f32[4096,2048]{1,0:T(8,128)}), f32[1024,2048]{1,0:T(8,128)}) %reduce-scatter.5.cloned.1.call-update) | async-done | bytes 8388624 | tf_op jit(solution)/shard_map/reduce_scatter | solution.py:232
  828.0 470.9 %reduce-scatter.3.cloned.1.call-done = f32[512,8512]{0,1:T(8,128)} async-done(((f32[2048,8512]{0,1:T(8,128)}), f32[512,8512]{0,1:T(8,128)}) %reduce-scatter.3.cloned.1.call-update) | async-done | bytes 17432592 | tf_op jit(solution)/shard_map/reduce_scatter | solution.py:278
  1300.3 40.8 %all-reduce.18 = (f32[2048]{0:T(1024)}, f32[4352]{0:T(1024)}, f32[64]{0:T(128)}, f32[64]{0:T(128)}, f32[64]{0:T(128)}, /*index=5*/f32[4096]{0:T(1024)}, f32[]{:T(128)}, f32[]{:T(128)}, f32[]{:T(128)}) all-reduce(f32[2048]{0:T(1024)S(1)} %get-tuple-element.640, ...), channel_id=1, replica_groups=mesh['rep'=8,'shard'=4] {'rep','shard'}, use_global_device_ids=true, to_apply=%region_35.38 | all-reduce | flops 10691 | bytes 85528 | tf_op jit(solution)/shard_map/psum | solution.py:299
  1343.3 3.3 gather_fusion.1
  1347.5 101.4 %all-reduce.23.cloned.1.call-done = f32[4,4352]{1,0:T(4,128)} async-done(((f32[4,4352]{1,0:T(4,128)}), f32[4,4352]{1,0:T(4,128)}) %all-reduce.23.cloned.1.call-update) | async-done | bytes 69648 | tf_op jit(solution)/shard_map/psum | solution.py:299
  1449.0 772.9 %all-reduce.25.cloned.1.call-done = (f32[512,8512]{0,1:T(8,128)}, f32[1024,2048]{1,0:T(8,128)}) async-done(((f32[512,8512]{0,1:T(8,128)}, f32[1024,2048]{1,0:T(8,128)}), (f32[512,8512]{0,1:T(8,128)}, f32[1024,2048]{1,0:T(8,128)})) %all-reduce.25.cloned.1.call-update) | async-done | bytes 25821200 | tf_op jit(solution)/shard_map/psum | solution.py:298
  2221.8 13.4 copy.274
  2235.9 3.4 copy.276
  (343 shorter events, 77.7 us)
Async XLA Ops:
  7.2 27.7 %all-gather.10.cloned.1.call-start = ((), (), s32[]{:S(2)}) async-start(), calls=%async_computation.2 | async-start | bytes 2621440 | tf_op jit(solution)/shard_map/all_gather | solution.py:188
  8.0 239.8 %all-gather.12.cloned.1.call-start = ((), (), s32[]{:S(2)}) async-start(), calls=%async_computation.3 | async-start | bytes 43581440 | tf_op jit(solution)/shard_map/all_gather | solution.py:195
  8.7 340.1 %all-gather.18.cloned.1.call-start = ((), (), s32[]{:S(2)}) async-start(), calls=%async_computation.9 | async-start | bytes 10485760 | tf_op jit(solution)/shard_map/all_gather | solution.py:28
  9.3 259.1 %copy-start.83 = (f32[64]{0:T(128)}, f32[64]{0:T(128)S(1)}, u32[]{:S(2)}) copy-start(f32[64]{0:T(128)S(1)} %exp.128) | copy-start | bytes 772
  10.2 28.0 %copy-start.88 = (s32[128]{0:T(128)}, s32[128]{0:T(128)S(1)}, u32[]{:S(2)}) copy-start(s32[128]{0:T(128)S(1)} %get-tuple-element.569) | copy-start | bytes 1540
  12.6 256.8 %copy-start.73 = (pred[128]{0:T(512)(128)(4,1)}, pred[128]{0:T(512)(128)(4,1)S(1)}, u32[]{:S(2)}) copy-start(pred[128]{0:T(512)(128)(4,1)S(1)} %get-tuple-element.734) | copy-start | bytes 388
  12.7 256.8 %copy-start.76 = (f32[128]{0:T(128)}, f32[128]{0:T(128)S(1)}, u32[]{:S(2)}) copy-start(f32[128]{0:T(128)S(1)} %get-tuple-element.735) | copy-start | bytes 1540
  13.2 234.6 %copy-start.37 = (pred[128]{0:T(512)(128)(4,1)}, pred[128]{0:T(512)(128)(4,1)S(1)}, u32[]{:S(2)}) copy-start(pred[128]{0:T(512)(128)(4,1)S(1)} %get-tuple-element.732) | copy-start | bytes 388
  13.4 263.1 %copy-start.28 = (f32[4352]{0:T(1024)}, f32[4352]{0:T(1024)S(1)}, u32[]{:S(2)}) copy-start(f32[4352]{0:T(1024)S(1)} %get-tuple-element.642) | copy-start | bytes 52228
  13.4 263.1 %copy-start.30 = (f32[4352]{0:T(1024)}, f32[4352]{0:T(1024)S(1)}, u32[]{:S(2)}) copy-start(f32[4352]{0:T(1024)S(1)} %get-tuple-element.643) | copy-start | bytes 52228
  13.4 263.1 %copy-start.32 = (f32[4352]{0:T(1024)}, f32[4352]{0:T(1024)S(1)}, u32[]{:S(2)}) copy-start(f32[4352]{0:T(1024)S(1)} %get-tuple-element.644) | copy-start | bytes 52228
  13.4 263.1 %copy-start.61 = (f32[128]{0:T(128)}, f32[128]{0:T(128)S(1)}, u32[]{:S(2)}) copy-start(f32[128]{0:T(128)S(1)} %get-tuple-element.726) | copy-start | bytes 1540
  13.4 263.1 %copy-start.63 = (f32[128]{0:T(128)}, f32[128]{0:T(128)S(1)}, u32[]{:S(2)}) copy-start(f32[128]{0:T(128)S(1)} %get-tuple-element.727) | copy-start | bytes 1540
  13.5 263.1 %copy-start.65 = (f32[128]{0:T(128)}, f32[128]{0:T(128)S(1)}, u32[]{:S(2)}) copy-start(f32[128]{0:T(128)S(1)} %get-tuple-element.728) | copy-start | bytes 1540
  13.5 263.1 %copy-start.67 = (f32[128]{0:T(128)}, f32[128]{0:T(128)S(1)}, u32[]{:S(2)}) copy-start(f32[128]{0:T(128)S(1)} %get-tuple-element.729) | copy-start | bytes 1540
  13.5 234.3 %copy-start.17 = (f32[2048]{0:T(1024)S(1)}, f32[2048]{0:T(1024)}, u32[]{:S(2)}) copy-start(f32[2048]{0:T(1024)} %param.26) | copy-start | bytes 24580
  38.5 226.8 %copy-start.92 = (f32[128]{0:T(128)}, f32[128]{0:T(128)S(1)}, u32[]{:S(2)}) copy-start(f32[128]{0:T(128)S(1)} %fusion.76) | copy-start | bytes 1540
  38.6 226.8 %copy-start.39 = (f32[128]{0:T(128)}, f32[128]{0:T(128)S(1)}, u32[]{:S(2)}) copy-start(f32[128]{0:T(128)S(1)} %fusion.132) | copy-start | bytes 1540
  38.6 229.9 %copy-start.81 = (f32[64]{0:T(128)S(1)}, f32[64]{0:T(128)}, u32[]{:S(2)}) copy-start(f32[64]{0:T(128)} %param.30) | copy-start | bytes 772
  266.3 10.0 collective-permute-start
  279.8 6.5 copy-start.9
  290.3 165.9 %all-gather.14.cloned.1.call-start = ((), (), s32[]{:S(2)}) async-start(), calls=%async_computation.4 | async-start | bytes 20971520 | tf_op jit(solution)/shard_map/all_gather | solution.py:221
  290.8 299.5 %all-gather.20.cloned.1.call-start = ((), (), s32[]{:S(2)}) async-start(), calls=%async_computation.10 | async-start | bytes 10485760 | tf_op jit(solution)/shard_map/all_gather | solution.py:28
  370.3 85.8 %copy-start.14 = (bf16[128,2048]{1,0:T(8,128)(2,1)S(1)}, bf16[128,2048]{1,0:T(8,128)(2,1)}, u32[]{:S(2)}) copy-start(bf16[128,2048]{1,0:T(8,128)(2,1)} %param.22) | copy-start | bytes 1572868
  370.3 85.8 %copy-start.18 = (f32[4096]{0:T(1024)S(1)}, f32[4096]{0:T(1024)}, u32[]{:S(2)}) copy-start(f32[4096]{0:T(1024)} %param.33) | copy-start | bytes 49156
  370.3 85.8 %copy-start.57 = (pred[128]{0:T(512)(128)(4,1)S(1)}, pred[128]{0:T(512)(128)(4,1)}, u32[]{:S(2)}) copy-start(pred[128]{0:T(512)(128)(4,1)} %get-tuple-element.736) | copy-start | bytes 388
  374.3 96.0 %copy-start.52 = (f32[128]{0:T(128)}, f32[128]{0:T(128)S(1)}, u32[]{:S(2)}) copy-start(f32[128]{0:T(128)S(1)} %fusion.133) | copy-start | bytes 1540
  498.6 11.5 copy-start.16
  498.7 11.5 copy-start.36
  498.7 11.5 copy-start.49
  498.7 11.5 copy-start.51
  498.7 11.5 copy-start.56
  498.7 11.5 copy-start.102
  531.9 296.2 %reduce-scatter.5.cloned.1.call-start = ((), (), s32[]{:S(2)}) async-start(), calls=%async_computation.8 | async-start | bytes 41943040 | tf_op jit(solution)/shard_map/reduce_scatter | solution.py:232
  550.2 748.8 %reduce-scatter.3.cloned.1.call-start = ((), (), s32[]{:S(2)}) async-start(), calls=%async_computation.6 | async-start | bytes 87162880 | tf_op jit(solution)/shard_map/reduce_scatter | solution.py:278
  556.9 6.9 copy-start.8
  598.8 15.7 copy-start.21
  642.2 3.1 collective-permute-start.1
  645.6 26.7 %copy-start.15 = (bf16[128,4352]{1,0:T(8,128)(2,1)}, bf16[128,4352]{1,0:T(8,128)(2,1)S(1)}, u32[]{:S(2)}) copy-start(bf16[128,4352]{1,0:T(8,128)(2,1)S(1)} %fusion.16) | copy-start | bytes 3342340
  672.3 14.8 copy-start.3
  672.3 14.8 copy-start.54
  672.3 670.9 %all-gather.16.cloned.1.call-start = ((), (), s32[]{:S(2)}) async-start(), calls=%async_computation.5 | async-start | bytes 2621440 | tf_op jit(solution)/shard_map/all_gather | solution.py:296
  687.1 9.7 copy-start.93
  687.1 9.7 copy-start.59
  698.1 750.8 %all-reduce.23.cloned.1.call-start = ((), (), s32[]{:S(2)}) async-start(), calls=%async_computation.7 | async-start | bytes 139264 | tf_op jit(solution)/shard_map/psum | solution.py:299
  699.0 1522.8 %all-reduce.25.cloned.1.call-start = ((), (), s32[]{:S(2)}) async-start(), calls=%async_computation.11 | async-start | bytes 51642368 | tf_op jit(solution)/shard_map/psum | solution.py:298
  2221.8 13.4 copy-start.46
  2221.8 14.1 copy-start.11
  (68 other events, 191.2 us)
Sparse Core Ops, SparseCore 0:
  9.6 25.2 all-gather.9
  36.5 211.2 all-gather.11
  290.4 58.3 all-gather.17
  350.2 105.9 all-gather.13
  532.0 58.2 all-gather.19
  592.7 235.2 reduce-scatter.4
  830.7 468.2 reduce-scatter.2
  1301.2 22.7 all-gather.15
  1331.1 117.8 all-reduce.22
  1453.9 767.9 all-reduce.24
where the time goes:
time: 2260 us; the launch traced here: 2250 us
  waiting for transfers between devices  1860 us (82%)
  matrix products  171 us (8%)
  local copies, waits for them, and re-layouts  82.4 us (4%)
  other arithmetic  66.1 us (3%)
  blocking collectives  46.1 us (2%)
    psum x1, waiting for transfers between devices, on_device(): grad_w_in, grad_w_out = lax.psum((grad_w_in, grad_w_out), 'rep')  773 us
    reduce_scatter x1, waiting for transfers between devices, on_device(): lax.psum_scatter(lax.dot_general(columns, grad_projected, (((0,), (0,)),...  471 us
    all_gather x1, waiting for transfers between devices, on_device(): lax.all_gather(w_in, 'shard', axis=0, tiled=True)  209 us
    reduce_scatter x1, waiting for transfers between devices, on_device(): lax.psum_scatter(lax.dot_general(columns, grad_branch, (((0,), (0,)), (()...  129 us
    psum x1, waiting for transfers between devices, on_device(): lax.psum((grad_norm_gain, grad_conv_w, grad_conv_b, grad_bias_out + grad_...  101 us
    all_gather x1, waiting for transfers between devices, on_device(): lax.all_gather(w_out, 'shard', axis=0, tiled=True)  81.8 us
    all_gather x2, waiting for transfers between devices, prefix(): pieces = jax.tree.map(lambda part: lax.all_gather(part, axis), value)  67.4 us
  transfers between devices with their start and end apart: 12, of which 10 were waited for; matrix products, arithmetic and copies ran while one was open for 9% of the time, Pallas kernels for 0%

commit v1 on v0

v1 whole, which is shorter than its diff:
```python
import functools

import jax
import jax.numpy as jnp
from jax import lax
from jax.experimental import pallas as pl
from jax.experimental.pallas import tpu as pltpu
from jax.sharding import PartitionSpec as P

D = 2048
H = 64
P_SIZE = 64
N = 128
KW = 4
SPAN = 128
DI = 4096
CONVW = 4352
PROJ = 8512
TAIL = PROJ - 2 * DI

EPSILON = 1e-05
ALL = ("rep", "shard")
VMEM_BYTES = 56 * 1024 * 1024
GATHER_BYTES = 32 * 1024 * 1024
BF = jnp.bfloat16
F32 = jnp.float32


def dot_nn(a, b):
    return lax.dot_general(a, b, (((1,), (0,)), ((), ())), preferred_element_type=F32)


def dot_nt(a, b):
    return lax.dot_general(a, b, (((1,), (1,)), ((), ())), preferred_element_type=F32)


def dot_tn(a, b):
    return lax.dot_general(a, b, (((0,), (0,)), ((), ())), preferred_element_type=F32)


def halves(a):
    high = a.astype(BF)
    return high, (a - high.astype(F32)).astype(BF)


def slot_tables(seq_lengths, seq_order, slot_ids):
    seq_count = seq_lengths.shape[0]
    numbers = jnp.arange(seq_count, dtype=jnp.int32)
    chosen = (seq_order[:, None] == numbers[None, :]).astype(jnp.int32)
    given_start = jnp.cumsum(seq_lengths) - seq_lengths
    owner_length = jnp.sum(chosen * seq_lengths[None, :], axis=1)
    owner_start = jnp.cumsum(owner_length) - owner_length
    owner_from = jnp.sum(chosen * given_start[None, :], axis=1)
    placed_at = jnp.sum(chosen * owner_start[:, None], axis=0)
    column = slot_ids[:, None]
    within = (column >= owner_start[None, :]) & (column < (owner_start + owner_length)[None, :])
    offset = column - owner_start[None, :]
    source = jnp.sum(jnp.where(within, offset + owner_from[None, :], 0), axis=1)
    position = jnp.sum(jnp.where(within, offset, 0), axis=1)
    given_within = (column >= given_start[None, :]) & (
        column < (given_start + seq_lengths)[None, :]
    )
    target = jnp.sum(
        jnp.where(given_within, column - given_start[None, :] + placed_at[None, :], 0), axis=1
    )
    return (source, target, position)


def sigmoid(v):
    return 1.0 / (1.0 + jnp.exp(-v))


def spread(column, lanes=128):
    return jnp.broadcast_to(column, (column.shape[0], lanes))


def conv_pre(x, conv_w, conv_b, place):
    pre = conv_b + conv_w[KW - 1 : KW] * x
    for back in range(1, KW):
        moved = pltpu.roll(x, back, 0)
        pre = pre + jnp.where(place >= back, conv_w[KW - 1 - back : KW - back] * moved, 0.0)
    return pre


def block_terms(row, position_ref, run_ref, run_t_ref):
    place = spread(position_ref[pl.ds(row, SPAN), :])
    local = lax.broadcasted_iota(jnp.int32, (SPAN, 128), 0)
    across = lax.broadcasted_iota(jnp.int32, (SPAN, 128), 1)
    begins = local - place
    causal = (across <= local) & (across >= begins)
    last_begin = begins[SPAN - 1 : SPAN, :]
    reach_end = local >= last_begin
    entered = place >= local + 1
    carries = place[SPAN - 1 : SPAN, :] >= SPAN
    return causal, reach_end, entered, carries


def pair_terms(pair, run, run_t, step, causal, reach_end, entered, carries):
    left = lax.broadcasted_iota(jnp.int32, (SPAN, 128), 1) < P_SIZE
    runs = [spread(run[:, 2 * pair + i : 2 * pair + i + 1]) for i in range(2)]
    decays = []
    for i in range(2):
        gap = runs[i] - run_t[2 * pair + i : 2 * pair + i + 1, :]
        decays.append(jnp.exp(jnp.where(causal, gap, -jnp.inf)))
    both = jnp.where(left, runs[0], runs[1])
    end = both[SPAN - 1 : SPAN, :]
    entering = jnp.where(entered, jnp.exp(both), 0.0)
    tail = jnp.where(reach_end, jnp.exp(jnp.where(reach_end, end - both, 0.0)), 0.0)
    carried = jnp.where(carries, jnp.exp(end), 0.0)
    size = jnp.where(
        left,
        spread(step[:, 2 * pair : 2 * pair + 1]),
        spread(step[:, 2 * pair + 1 : 2 * pair + 2]),
    )
    return left, decays, entering, tail, carried, size


def stacked(value, left):
    zero = jnp.zeros_like(value)
    return jnp.concatenate([jnp.where(left, value, zero), jnp.where(left, zero, value)], axis=0)


def step_and_run(dt_ref, dt_bias_ref, a_log_ref, run_ref, step_ref, length):
    step_ref[...] = jax.nn.softplus(dt_ref[...] + dt_bias_ref[...])
    lower = (
        lax.broadcasted_iota(jnp.int32, (SPAN, SPAN), 0)
        >= lax.broadcasted_iota(jnp.int32, (SPAN, SPAN), 1)
    ).astype(F32)

    def block(b, unused):
        rows = pl.ds(pl.multiple_of(b * SPAN, SPAN), SPAN)
        log_decay = -step_ref[rows, :] * jnp.exp(a_log_ref[...])
        run_ref[rows, :] = jnp.dot(
            lower, log_decay, precision=lax.Precision.HIGHEST, preferred_element_type=F32
        )
        return unused

    lax.fori_loop(0, length // SPAN, block, 0)


def forward_kernel(
    conv_in_ref,
    dt_ref,
    position_ref,
    conv_w_ref,
    conv_b_ref,
    dt_bias_ref,
    a_log_ref,
    d_skip_ref,
    mixed_ref,
    starts_ref,
    act_ref,
    step_ref,
    run_ref,
    state_ref,
):
    length, width = mixed_ref.shape
    place = spread(position_ref[...])
    for c in range((width + 2 * N) // 128):
        lanes = slice(128 * c, 128 * c + 128)
        pre = conv_pre(
            conv_in_ref[:, lanes].astype(F32), conv_w_ref[:, lanes], conv_b_ref[:, lanes], place
        )
        act_ref[:, lanes] = (pre * sigmoid(pre)).astype(BF)
    step_and_run(dt_ref, dt_bias_ref, a_log_ref, run_ref, step_ref, length)
    state_ref[...] = jnp.zeros_like(state_ref)

    def block(b, unused):
        row = pl.multiple_of(b * SPAN, SPAN)
        rows = pl.ds(row, SPAN)
        starts_ref[pl.ds(pl.multiple_of(b * N, N), N), :] = state_ref[...]
        run = run_ref[rows, :]
        run_t = run.T
        step = step_ref[rows, :]
        masks = block_terms(row, position_ref, run_ref, run_t)
        in_map = act_ref[rows, width : width + N]
        out_map = act_ref[rows, width + N : width + 2 * N]
        products = dot_nt(out_map, in_map)
        in_map_t = in_map.T
        for pair in range(width // 128):
            lanes = slice(128 * pair, 128 * pair + 128)
            left, decays, entering, tail, carried, size = pair_terms(
                pair, run, run_t, step, *masks
            )
            values = act_ref[rows, lanes].astype(F32)
            scaled = values * size
            weights = jnp.concatenate([(d * products).astype(BF) for d in decays], axis=1)
            out = dot_nn(weights, stacked(scaled.astype(BF), left))
            state = state_ref[:, lanes]
            high, low = halves(state)
            out += entering * (dot_nn(out_map, high) + dot_nn(out_map, low))
            mixed_ref[rows, lanes] = out + d_skip_ref[:, lanes] * values
            high, low = halves(tail * scaled)
            fresh = dot_nn(in_map_t, high) + dot_nn(in_map_t, low)
            state_ref[:, lanes] = carried * state + fresh
        return unused

    lax.fori_loop(0, length // SPAN, block, 0)


def backward_kernel(
    conv_in_ref,
    dt_ref,
    position_ref,
    conv_w_ref,
    conv_b_ref,
    dt_bias_ref,
    a_log_ref,
    d_skip_ref,
    mixed_ref,
    starts_ref,
    grad_ref,
    join_ref,
    grad_values_ref,
    grad_maps_ref,
    grad_dt_ref,
    grad_conv_w_ref,
    grad_conv_b_ref,
    grad_head_ref,
    grad_skip_ref,
    act_ref,
    pre_ref,
    step_ref,
    run_ref,
    state_ref,
    grad_act_ref,
    joined_ref,
):
    length, width = mixed_ref.shape
    blocks = length // SPAN
    place = spread(position_ref[...])
    for c in range((width + 2 * N) // 128):
        lanes = slice(128 * c, 128 * c + 128)
        pre = conv_pre(
            conv_in_ref[:, lanes].astype(F32), conv_w_ref[:, lanes], conv_b_ref[:, lanes], place
        )
        pre_ref[:, lanes] = pre
        act_ref[:, lanes] = (pre * sigmoid(pre)).astype(BF)
    step_and_run(dt_ref, dt_bias_ref, a_log_ref, run_ref, step_ref, length)
    state_ref[...] = jnp.zeros_like(state_ref)
    grad_head_ref[...] = jnp.zeros_like(grad_head_ref)
    grad_skip_ref[...] = jnp.zeros_like(grad_skip_ref)
    upper = (
        lax.broadcasted_iota(jnp.int32, (SPAN, SPAN), 0)
        <= lax.broadcasted_iota(jnp.int32, (SPAN, SPAN), 1)
    ).astype(F32)
    last_row = lax.broadcasted_iota(jnp.int32, (SPAN, 128), 0) == SPAN - 1

    def block(count, unused):
        b = blocks - 1 - count
        row = pl.multiple_of(b * SPAN, SPAN)
        rows = pl.ds(row, SPAN)
        start_rows = pl.ds(pl.multiple_of(b * N, N), N)
        run = run_ref[rows, :]
        run_t = run.T
        step = step_ref[rows, :]
        masks = block_terms(row, position_ref, run_ref, run_t)
        in_map = act_ref[rows, width : width + N]
        out_map = act_ref[rows, width + N : width + 2 * N]
        out_map_t = out_map.T
        products = dot_nt(out_map, in_map)
        grad_products = jnp.zeros((SPAN, SPAN), F32)
        grad_out_map = jnp.zeros((SPAN, N), F32)
        grad_in_map = jnp.zeros((SPAN, N), F32)
        for pair in range(width // 128):
            lanes = slice(128 * pair, 128 * pair + 128)
            left, decays, entering, tail, carried, size = pair_terms(
                pair, run, run_t, step, *masks
            )
            values = act_ref[rows, lanes].astype(F32)
            grad = grad_ref[rows, lanes]
            start = starts_ref[start_rows, lanes]
            later = state_ref[:, lanes]
            scaled = values * size
            scaled_low = scaled.astype(BF)
            grad_low = grad.astype(BF)
            weights = jnp.concatenate([(d * products).astype(BF) for d in decays], axis=0)
            grad_scaled = dot_tn(weights, stacked(grad_low, left))
            grad_pairs = dot_nt(grad_low, stacked(scaled_low, left))
            grad_products += (
                grad_pairs[:, :SPAN] * decays[0] + grad_pairs[:, SPAN:] * decays[1]
            )
            later_high, later_low = halves(later)
            from_later = tail * (dot_nn(in_map, later_high) + dot_nn(in_map, later_low))
            grad_scaled += from_later
            entering_grad = entering * grad
            entering_high, entering_low = halves(entering_grad)
            start_high = start.astype(BF)
            grad_out_map += dot_nt(entering_high, start_high)
            grad_in_map += dot_nt((tail * scaled).astype(BF), later_high)
            ending = jnp.sum(scaled * from_later, axis=0, keepdims=True) + carried * jnp.sum(
                start * later, axis=0, keepdims=True
            )
            state_ref[:, lanes] = (
                carried * later + dot_nn(out_map_t, entering_high) + dot_nn(out_map_t, entering_low)
            )
            skip = d_skip_ref[:, lanes]
            inner = mixed_ref[rows, lanes] - skip * values
            grad_run = (
                grad_low.astype(F32) * inner
                - scaled_low.astype(F32) * (grad_scaled - from_later)
                - scaled * from_later
                + jnp.where(last_row, ending, 0.0)
            )
            joined_ref[0:SPAN, lanes] = grad_run
            joined_ref[SPAN : 2 * SPAN, lanes] = grad_scaled * values
            grad_act_ref[rows, lanes] = grad_scaled * size + skip * grad
            grad_skip_ref[:, lanes] += jnp.sum(grad * values, axis=0, keepdims=True)
        grad_products = grad_products.astype(BF)
        grad_act_ref[rows, width : width + N] = grad_in_map + dot_tn(grad_products, out_map)
        grad_act_ref[rows, width + N : width + 2 * N] = grad_out_map + dot_nn(
            grad_products, in_map
        )
        joined = joined_ref[...]
        first = joined.astype(BF)
        rest = joined - first.astype(F32)
        second, third = halves(rest)
        join = join_ref[...]
        by_head = dot_nn(first, join) + dot_nn(second, join) + dot_nn(third, join)
        grad_log = jnp.dot(
            upper, by_head[:SPAN], precision=lax.Precision.HIGHEST, preferred_element_type=F32
        )
        rate = jnp.exp(a_log_ref[...])
        log_decay = -step * rate
        grad_step = by_head[SPAN:] - grad_log * rate
        grad_dt = grad_step * sigmoid(dt_ref[rows, :] + dt_bias_ref[...])
        grad_dt_ref[rows, :] = grad_dt
        grad_head_ref[0:1, :] += jnp.sum(grad_dt, axis=0, keepdims=True)
        grad_head_ref[1:2, :] += jnp.sum(grad_log * log_decay, axis=0, keepdims=True)
        return unused

    lax.fori_loop(0, blocks, block, 0)

    for c in range((width + 2 * N) // 128):
        lanes = slice(128 * c, 128 * c + 128)
        x = conv_in_ref[:, lanes].astype(F32)
        conv_w = conv_w_ref[:, lanes]
        pre = pre_ref[:, lanes]
        gain = sigmoid(pre)
        grad_pre = grad_act_ref[:, lanes] * (gain * (1.0 + pre * (1.0 - gain)))
        grad_conv_b_ref[:, lanes] = jnp.sum(grad_pre, axis=0, keepdims=True)
        grad_conv_w_ref[KW - 1 : KW, lanes] = jnp.sum(grad_pre * x, axis=0, keepdims=True)
        grad_x = conv_w[KW - 1 : KW] * grad_pre
        for back in range(1, KW):
            tap = KW - 1 - back
            kept = jnp.where(place >= back, grad_pre, 0.0)
            grad_conv_w_ref[tap : tap + 1, lanes] = jnp.sum(
                kept * pltpu.roll(x, back, 0), axis=0, keepdims=True
            )
            grad_x += conv_w[tap : tap + 1] * pltpu.roll(kept, length - back, 0)
        if c < width // 128:
            grad_values_ref[:, lanes] = grad_x.astype(BF)
        else:
            grad_maps_ref[:, 128 * c - width : 128 * c - width + 128] = grad_x


def params():
    return pltpu.CompilerParams(vmem_limit_bytes=VMEM_BYTES)


def run_forward(conv_in, dt, position, conv_w, conv_b, dt_bias, a_log, d_skip):
    length = conv_in.shape[0]
    width = conv_in.shape[1] - 2 * N
    blocks = length // SPAN
    return pl.pallas_call(
        forward_kernel,
        out_shape=(
            jax.ShapeDtypeStruct((length, width), F32),
            jax.ShapeDtypeStruct((blocks * N, width), F32),
        ),
        scratch_shapes=[
            pltpu.VMEM((length, width + 2 * N), BF),
            pltpu.VMEM((length, 128), F32),
            pltpu.VMEM((length, 128), F32),
            pltpu.VMEM((N, width), F32),
        ],
        compiler_params=params(),
        cost_estimate=pl.CostEstimate(
            flops=20 * length * width * 128, bytes_accessed=12 * length * width, transcendentals=0
        ),
        name="mixer_forward",
    )(conv_in, dt, position, conv_w, conv_b, dt_bias, a_log, d_skip)


def run_backward(
    conv_in, dt, position, conv_w, conv_b, dt_bias, a_log, d_skip, mixed, starts, grad, join
):
    length = conv_in.shape[0]
    width = conv_in.shape[1] - 2 * N
    return pl.pallas_call(
        backward_kernel,
        out_shape=(
            jax.ShapeDtypeStruct((length, width), BF),
            jax.ShapeDtypeStruct((length, 2 * N), F32),
            jax.ShapeDtypeStruct((length, 128), F32),
            jax.ShapeDtypeStruct((KW, width + 2 * N), F32),
            jax.ShapeDtypeStruct((1, width + 2 * N), F32),
            jax.ShapeDtypeStruct((8, 128), F32),
            jax.ShapeDtypeStruct((1, width), F32),
        ),
        scratch_shapes=[
            pltpu.VMEM((length, width + 2 * N), BF),
            pltpu.VMEM((length, width + 2 * N), F32),
            pltpu.VMEM((length, 128), F32),
            pltpu.VMEM((length, 128), F32),
            pltpu.VMEM((N, width), F32),
            pltpu.VMEM((length, width + 2 * N), F32),
            pltpu.VMEM((2 * SPAN, width), F32),
        ],
        compiler_params=params(),
        cost_estimate=pl.CostEstimate(
            flops=40 * length * width * 128, bytes_accessed=20 * length * width, transcendentals=0
        ),
        name="mixer_backward",
    )(conv_in, dt, position, conv_w, conv_b, dt_bias, a_log, d_skip, mixed, starts, grad, join)


def exchange(pieces, axis, mine):
    count = lax.axis_size(axis)
    own = pieces(mine)
    gathered = jnp.zeros((count,) + own.shape, own.dtype)
    gathered = lax.dynamic_update_index_in_dim(gathered, own, mine, 0)
    for other in range(1, count):
        arrived = lax.ppermute(
            pieces(mine ^ other), axis, [(i, i ^ other) for i in range(count)]
        )
        gathered = lax.dynamic_update_index_in_dim(gathered, arrived, mine ^ other, 0)
    return gathered


def columns_at(array, start, width):
    return lax.dynamic_slice_in_dim(array, start, width, axis=1)


def on_device(
    x_in,
    cotangent,
    seq_lengths,
    seq_order,
    valid,
    norm_gain,
    w_in,
    conv_w,
    conv_b,
    dt_bias,
    a_log,
    d_skip,
    gated_gain,
    w_out,
):
    shards, mine = lax.axis_size("shard"), lax.axis_index("shard")
    reps = lax.axis_size("rep")
    rows = x_in.shape[0]
    length = rows * shards
    depth = w_in.shape[0]
    heads = H // shards
    width = DI // shards

    w_tail = w_in[:, 2 * DI :]

    def conv_piece(d):
        return jnp.concatenate([columns_at(w_in, DI + d * width, width), w_tail], axis=1)

    def gate_piece(d):
        return columns_at(w_in, d * width, width)

    x_group = lax.all_gather(x_in, "shard", axis=0, tiled=True)
    w_conv = exchange(conv_piece, "shard", mine).reshape(D, width + TAIL)
    w_gate = exchange(gate_piece, "shard", mine).reshape(D, width)
    grad_branch = jnp.where(valid[:, None] > 0, cotangent, jnp.zeros_like(cotangent))
    grad_branch_group = lax.all_gather(grad_branch, "shard", axis=0, tiled=True)

    slot_ids = jnp.arange(length, dtype=jnp.int32)
    source, target, position = slot_tables(seq_lengths[0], seq_order[0], slot_ids)
    pick = (source[:, None] == slot_ids[None, :]).astype(BF)
    resid = dot_nn(pick, x_group)
    inverse_rms = lax.rsqrt(jnp.mean(resid * resid, axis=1, keepdims=True) + EPSILON)
    normed = (resid * inverse_rms * norm_gain[None, :]).astype(BF)
    normed_mine = lax.dynamic_slice_in_dim(normed, mine * rows, rows, axis=0)
    resid_mine = lax.dynamic_slice_in_dim(resid, mine * rows, rows, axis=0)
    few = reps * length * D * 2 <= GATHER_BYTES
    if few:
        normed_all = lax.all_gather(normed_mine, ALL, axis=0, tiled=True)

    projected = dot_nn(normed, w_conv).astype(BF)
    gate_low = dot_nn(normed, w_gate).astype(BF)
    conv_in = projected[:, : width + 2 * N]
    dt_all = projected[:, width + 2 * N :].astype(F32)

    def own_heads(row):
        picked = columns_at(row, mine * heads, heads)
        return jnp.pad(picked, ((0, 0), (0, 128 - heads)))

    dt = own_heads(dt_all)
    bias_row, decay_row = own_heads(dt_bias[None, :]), own_heads(a_log[None, :])
    skip_row = jnp.repeat(
        lax.dynamic_slice_in_dim(d_skip, mine * heads, heads), P_SIZE, total_repeat_length=width
    )[None, :]

    def own_conv(array):
        return jnp.concatenate([columns_at(array, mine * width, width), array[:, DI:]], axis=1)

    conv_w_own, conv_b_own = own_conv(conv_w), own_conv(conv_b[None, :])
    gain_row = lax.dynamic_slice_in_dim(gated_gain, mine * width, width)[None, :]
    place = position[:, None]

    mixed, starts = run_forward(
        conv_in, dt, place, conv_w_own, conv_b_own, bias_row, decay_row, skip_row
    )

    grad_normed_out = dot_nt(grad_branch_group, w_out)
    gate = gate_low.astype(F32)
    gate_gain = sigmoid(gate)
    product = mixed * (gate * gate_gain)
    weighted = grad_normed_out * gain_row
    partial_sums = jnp.stack(
        [jnp.sum(product * product, axis=1), jnp.sum(weighted * product, axis=1)]
    )
    row_sums = lax.psum(partial_sums, "shard") / DI
    inverse = lax.rsqrt(row_sums[0] + EPSILON)[:, None]
    normalized = product * inverse
    normed_out = (normalized * gain_row).astype(BF)
    grad_product = inverse * weighted - product * (inverse**3 * row_sums[1][:, None])
    grad_gated_gain = jnp.sum(grad_normed_out * normalized, axis=0)
    grad_mixed = grad_product * (gate * gate_gain)
    grad_gate = (
        grad_product * mixed * (gate_gain * (1.0 + gate * (1.0 - gate_gain)))
    ).astype(BF)

    branch = lax.psum_scatter(
        dot_nn(normed_out, w_out), "shard", scatter_dimension=0, tiled=True
    )
    total_rows = resid_mine + branch
    block_out = total_rows.astype(BF)
    weights_valid = valid.astype(F32)
    square_total = jnp.sum(weights_valid * jnp.sum(total_rows * total_rows, axis=1))
    square_branch = jnp.sum(weights_valid * jnp.sum(branch * branch, axis=1))
    valid_count = jnp.sum(weights_valid)

    grad_w_out = lax.psum(dot_tn(normed_out, grad_branch_group).astype(BF), "rep").astype(F32)

    def to_owners(columns):
        if not few:
            part = dot_tn(normed, columns).astype(BF).reshape(shards, depth, columns.shape[1])
            swapped = lax.all_to_all(part, "shard", split_axis=0, concat_axis=0, tiled=True)
            summed = lax.psum(swapped, "rep").astype(F32)
            return summed.transpose(1, 0, 2).reshape(depth, shards * columns.shape[1])
        share = columns.shape[1] // reps
        split = columns.reshape(length, reps, share).transpose(1, 0, 2)
        taken = lax.all_to_all(split, "rep", split_axis=0, concat_axis=0, tiled=True)
        summed = dot_tn(normed_all, taken.reshape(reps * length, share)).astype(BF)
        swapped = lax.all_to_all(
            summed.reshape(shards, depth, share), "shard", split_axis=0, concat_axis=0, tiled=True
        )
        whole = lax.all_gather(swapped, "rep")
        return whole.transpose(2, 1, 0, 3).reshape(depth, DI).astype(F32)

    grad_w_gate = to_owners(grad_gate)

    join = (
        jnp.arange(width, dtype=jnp.int32)[:, None] // P_SIZE
        == jnp.arange(128, dtype=jnp.int32)[None, :]
    ).astype(BF)
    grad_values, grad_maps, grad_dt, grad_conv_w, grad_conv_b, grad_head, grad_skip = run_backward(
        conv_in,
        dt,
        place,
        conv_w_own,
        conv_b_own,
        bias_row,
        decay_row,
        skip_row,
        mixed,
        starts,
        grad_mixed,
        join,
    )
    grad_maps = lax.psum_scatter(
        grad_maps, "shard", scatter_dimension=1, tiled=True
    ).astype(BF)
    grad_dt_low = grad_dt[:, :heads].astype(BF)
    share = 2 * N // shards
    grad_tail = jnp.concatenate([grad_maps, grad_dt_low], axis=1)

    back = (target[:, None] == slot_ids[None, :]).astype(BF)
    grad_own = jnp.concatenate([grad_gate, grad_values, grad_tail], axis=1)
    grad_given = dot_nn(back, grad_own).astype(BF)
    w_own = jnp.concatenate(
        [
            w_gate,
            w_conv[:, :width],
            columns_at(w_conv, width + mine * share, share),
            columns_at(w_conv, width + 2 * N + mine * heads, heads),
        ],
        axis=1,
    )
    grad_normed = lax.psum_scatter(
        dot_nt(grad_given, w_own), "shard", scatter_dimension=0, tiled=True
    )
    given = x_in.astype(F32)
    given_rms = lax.rsqrt(jnp.mean(given * given, axis=1, keepdims=True) + EPSILON)
    grad_norm_gain = jnp.sum(grad_normed * (given * given_rms), axis=0)
    scaled = grad_normed * norm_gain[None, :]
    grad_resid = scaled * given_rms - given * (
        given_rms**3 * jnp.mean(scaled * given, axis=1, keepdims=True)
    )
    back_mine = lax.dynamic_slice_in_dim(back, mine * rows, rows, axis=0)
    grad_in = (grad_resid + dot_nn(back_mine, grad_branch_group)).astype(BF)

    grad_w_values = to_owners(grad_values)
    if few:
        tails = lax.all_gather(grad_tail, ALL, axis=0, tiled=False)
        tails = tails.reshape(reps, shards, length, share + heads).transpose(0, 2, 1, 3)
        tails = jnp.concatenate(
            [
                tails[..., :share].reshape(reps * length, 2 * N),
                tails[..., share:].reshape(reps * length, H),
            ],
            axis=1,
        )
        grad_w_tail = dot_tn(columns_at(normed_all, mine * depth, depth), tails)
    else:
        parts = to_owners(grad_tail).reshape(depth, shards, share + heads)
        grad_w_tail = jnp.concatenate(
            [parts[..., :share].reshape(depth, 2 * N), parts[..., share:].reshape(depth, H)], axis=1
        )
    grad_w_in = jnp.concatenate([grad_w_gate, grad_w_values, grad_w_tail], axis=1)

    def placed(part, whole, start):
        return lax.dynamic_update_slice_in_dim(
            jnp.zeros(part.shape[:-1] + (whole,), F32), part, start, axis=part.ndim - 1
        )

    def placed_conv(part):
        return jnp.concatenate(
            [placed(part[:, :width], DI, mine * width), part[:, width:]], axis=1
        )

    grad_skip_heads = jnp.sum(grad_skip.reshape(heads, P_SIZE), axis=1)
    pieces = (
        grad_norm_gain,
        placed_conv(grad_conv_w).reshape(-1),
        placed_conv(grad_conv_b).reshape(-1),
        placed(grad_head[0, :heads], H, mine * heads),
        placed(grad_head[1, :heads], H, mine * heads),
        placed(grad_skip_heads, H, mine * heads),
        placed(grad_gated_gain, DI, mine * width),
        jnp.stack([square_total, square_branch, valid_count]),
    )
    summed = lax.psum(jnp.concatenate(pieces), ALL)
    results, at = [], 0
    for piece in pieces:
        results.append(summed[at : at + piece.shape[0]])
        at += piece.shape[0]
    count_all = jnp.maximum(results[7][2], 1.0)
    rms_residual = jnp.sqrt(results[7][0] / (count_all * D))
    rms_mixer = jnp.sqrt(results[7][1] / (count_all * D))
    return (
        block_out,
        grad_in,
        results[0],
        grad_w_in,
        results[1].reshape(KW, CONVW),
        results[2],
        results[3],
        results[4],
        results[5],
        results[6],
        grad_w_out,
        rms_residual,
        rms_mixer,
    )


def solution(mesh):
    in_specs = (
        P(ALL, None),
        P(ALL, None),
        P("rep", None),
        P("rep", None),
        P(ALL),
        P(),
        P("shard", None),
        P(),
        P(),
        P(),
        P(),
        P(),
        P(),
        P("shard", None),
    )
    out_specs = (
        P(ALL, None),
        P(ALL, None),
        P(),
        P("shard", None),
        P(),
        P(),
        P(),
        P(),
        P(),
        P(),
        P("shard", None),
        P(),
        P(),
    )
    return jax.shard_map(
        on_device, mesh=mesh, in_specs=in_specs, out_specs=out_specs, check_vma=False
    )
```

time: 2260 us -> 1050 us (0.46)
  waiting for transfers between devices: 1860 us -> 646 us
  matrix products: 171 us -> 71.8 us
  Pallas kernels: 0 us -> 37.6 us
  local copies, waits for them, and re-layouts: 82.4 us -> 116 us
  blocking collectives: 46.1 us -> 78.8 us
    psum x2, waiting for transfers between devices: 874 us -> 213 us  [the longest x1 115 us: on_device(): summed = lax.psum(jnp.concatenate(pieces), ALL)]
    reduce_scatter x2, waiting for transfers between devices: 600 us -> 76.8 us  [the longest x1 44.1 us: on_device(): lax.psum_scatter(dot_nt(grad_given, w_own), 'shard', scatter_dimension=0,...]
    all_gather x6, waiting for transfers between devices: 380 us -> 233 us  [the longest x2 120 us: to_owners(): whole = lax.all_gather(swapped, 'rep')]
    dot_general x22 -> x11, matrix products: 171 us -> 71.8 us  [the longest x4 28.6 us: dot_tn(): lax.dot_general(a, b, (((0,), (0,)), ((), ())), preferred_element_type=F32)]
    ppermute x2 -> x6, waiting for transfers between devices: 1.01 us -> 86.6 us  [exchange(): lax.ppermute(pieces(mine ^ other), axis, [(i, i ^ other) for i in range(c...]
    all_to_all x0 -> x2, blocking collectives: none -> 71.6 us  [the longest x1 59.5 us: to_owners(): lax.all_to_all(split, 'rep', split_axis=0, concat_axis=0, tiled=True)]
    pallas_call x0 -> x2, Pallas kernels: none -> 37.6 us  [the longest x1 24.9 us: run_backward(): pl.pallas_call(backward_kernel, out_shape=(jax.ShapeDtypeStruct((length,...]
    all_to_all x0 -> x2, waiting for transfers between devices: none -> 35.4 us  [the longest x1 35.4 us: to_owners(): lax.all_to_all(split, 'rep', split_axis=0, concat_axis=0, tiled=True)]
  transfers between devices with their start and end apart: 12 -> 19, of which waited for: 10 -> 11; matrix products, arithmetic and copies ran while one was open for 9% -> 19% of each run, Pallas kernels for 0% -> 1%
where the time goes in v1:
time: 1050 us
  waiting for transfers between devices  646 us (62%)
  local copies, waits for them, and re-layouts  116 us (11%)
  blocking collectives  78.8 us (8%)
  matrix products  71.8 us (7%)
  other arithmetic  65 us (6%)
  Pallas kernels  37.6 us (4%)
  between operations  19.1 us (2%)
  starting transfers between devices  15.2 us (1%)
    all_gather x2, waiting for transfers between devices, to_owners(): whole = lax.all_gather(swapped, 'rep')  120 us
    psum x1, waiting for transfers between devices, on_device(): summed = lax.psum(jnp.concatenate(pieces), ALL)  115 us
    psum x1, waiting for transfers between devices, on_device(): lax.psum(dot_tn(normed_out, grad_branch_group).astype(BF), 'rep')  97.3 us
    ppermute x6, waiting for transfers between devices, exchange(): lax.ppermute(pieces(mine ^ other), axis, [(i, i ^ other) for i in range(c...  86.6 us
    all_to_all x1, blocking collectives, to_owners(): lax.all_to_all(split, 'rep', split_axis=0, concat_axis=0, tiled=True)  59.5 us
    all_gather x1, waiting for transfers between devices, on_device(): tails = lax.all_gather(grad_tail, ALL, axis=0, tiled=False)  57.7 us
    all_gather x1, waiting for transfers between devices, on_device(): normed_all = lax.all_gather(normed_mine, ALL, axis=0, tiled=True)  55.1 us
    reduce_scatter x1, waiting for transfers between devices, on_device(): lax.psum_scatter(dot_nt(grad_given, w_own), 'shard', scatter_dimension=0,...  44.1 us
  transfers between devices with their start and end apart: 19, of which 11 were waited for; matrix products, arithmetic and copies ran while one was open for 19% of the time, Pallas kernels for 1%

profile of v1, /device:TPU:0, one launch (start us, length us, event | category | flops | bytes accessed | tf_op | source)
XLA Modules:
  0.0 1049.7 jit_solution(6916103170074567749)
XLA Ops:
  8.0 5.7 constant_dynamic-slice_fusion.3
  16.3 2.5 collective-permute-start.1
  28.7 4.5 compare_select_fusion.2
  34.0 5.8 select_select_fusion
  41.3 2.9 broadcast_in_dim.108
  51.7 2.5 broadcast_in_dim.118
  57.7 66.9 %collective-permute-done.4 = bf16[512,1024]{1,0:T(8,128)(2,1)} collective-permute-done((bf16[512,1024]{1,0:T(8,128)(2,1)}, bf16[512,1024]{1,0:T(8,128)(2,1)}, u32[]{:S(2)}, u32[]{:S(2)}) %collective-permute-start.4) | collective-permute-done | bytes 1048608 | tf_op jit(solution)/shard_map/ppermute | solution.py:424
  126.9 19.7 %collective-permute-done.5 = bf16[512,1024]{1,0:T(8,128)(2,1)S(1)} collective-permute-done((bf16[512,1024]{1,0:T(8,128)(2,1)S(1)}, bf16[512,1024]{1,0:T(8,128)(2,1)S(1)}, u32[]{:S(2)}, u32[]{:S(2)}) %collective-permute-start.5) | collective-permute-done | bytes 1048608 | tf_op jit(solution)/shard_map/ppermute | solution.py:424
  151.3 2.5 copy.65
  158.1 3.0 multiply_reduce_fusion
  163.0 6.0 convolution_convert_fusion.2
  171.2 12.8 %mixer_forward.1 = (f32[512,1024]{1,0:T(8,128)}, f32[512,1024]{1,0:T(8,128)}) custom-call(bf16[512,1280]{1,0:T(8,128)(2,1)} %slice.146.conv_in_ref, f32[512,128]{1,0:T(8,128)} %pad.14.dt_ref, s32[512,1]{1,0:T(8,128)} %copy.67.position_ref, f32[4,1280]{1,0:T(4,128)} %pad_maximum_fusion.7.conv_w_ref, f32[1,1280]{1,0:T(1,128)} %pad_maximum_fusion.8.conv_b_ref, ...), custom_call_target="tpu_custom_call" | custom-call | flops 1342177280 | bytes 6291456 | tf_op jit(solution)/shard_map/mixer_forward/pallas_call | solution.py:365
  183.9 5.3 fusion.46
  189.3 6.8 multiply_reduce_fusion.3
  196.1 7.1 psum.21
  203.2 4.5 fusion.19
  207.8 24.9 %mixer_backward.1 = (bf16[512,1024]{1,0:T(8,128)(2,1)}, f32[512,256]{1,0:T(8,128)}, f32[512,128]{1,0:T(8,128)}, f32[4,1280]{1,0:T(4,128)}, f32[1,1280]{1,0:T(1,1...) custom-call(bf16[512,1280]{1,0:T(8,128)(2,1)} %slice.146.conv_in_ref, f32[512,128]{1,0:T(8,128)} %pad.14.dt_ref, ...), custom_call_target="tpu_custom_call" | custom-call | flops 2684354560 | bytes 10485760 | tf_op jit(solution)/shard_map/mixer_backward/pallas_call | solution.py:390
  235.6 7.9 fusion.39
  244.3 4.6 slice.152
  251.5 14.3 %concatenate.54 = bf16[2048,2128]{1,0:T(8,128)(2,1)} concatenate(bf16[2048,1024]{1,0:T(8,128)(2,1)} %bitcast.42, bf16[2048,1024]{1,0:T(8,128)(2,1)} %slice.152, bf16[2048,64]{1,0:T(8,128)(2,1)S(1)} %constant_dynamic-slice_fusion.2, bf16[2048,16]{1,0:T(8,128)(2,1)S(1)} %constant_dynamic-slice_fusion.1), dimensions={1} | concatenate | bytes 17432576 | tf_op jit(solution)/shard_map/concatenate | solution.py:588
  266.9 3.0 concatenate.53
  269.8 12.7 %fusion.22 = f32[512,2048]{1,0:T(8,128)} fusion(bf16[2048,2128]{1,0:T(8,128)(2,1)} %concatenate.54, bf16[512,2128]{1,0:T(8,128)(2,1)} %concatenate.53, s32[512]{0:T(512)S(1)} %select_reduce_fusion), kind=kOutput, calls=%fused_computation.61 | convolution fusion | flops 5579776000 | bytes 15091712 | tf_op jit(solution)/shard_map/dot_general | solution.py:34
  283.7 6.9 convolution_convert_fusion.1
  292.7 5.9 all-to-all-start.2
  302.5 35.4 %all-to-all-done.2 = bf16[8,512,128]{2,1,0:T(8,128)(2,1)S(1)} async-done(((bf16[8,512,128]{2,1,0:T(8,128)(2,1)}), bf16[8,512,128]{2,1,0:T(8,128)(2,1)S(1)}, u32[]{:S(2)}, u32[]{:S(2)}) %all-to-all-start.2) | async-done | bytes 1048608 | tf_op jit(solution)/shard_map/all_to_all | solution.py:550
  337.9 55.1 %all-gather.14.cloned.1.call-done = bf16[4096,2048]{1,0:T(8,128)(2,1)} async-done(((bf16[128,2048]{1,0:T(8,128)(2,1)}), bf16[4096,2048]{1,0:T(8,128)(2,1)}) %all-gather.14.cloned.1.call-update) | async-done | bytes 16777232 | tf_op jit(solution)/shard_map/all_gather | solution.py:483
  392.9 9.2 convolution_convert_fusion.3
  402.1 3.6 all-to-all-start.3
  405.8 32.6 %reduce-scatter.6.cloned.1.call-done = f32[128,2048]{1,0:T(8,128)} async-done(((f32[512,2048]{1,0:T(8,128)}), f32[128,2048]{1,0:T(8,128)}) %reduce-scatter.6.cloned.1.call-update) | async-done | bytes 1048592 | tf_op jit(solution)/shard_map/reduce_scatter | solution.py:530
  438.4 2.5 multiply_reduce_fusion.4
  441.5 44.1 %reduce-scatter.8.cloned.1.call-done = f32[128,2048]{1,0:T(8,128)} async-done(((f32[512,2048]{1,0:T(8,128)}), f32[128,2048]{1,0:T(8,128)}) %reduce-scatter.8.cloned.1.call-update) | async-done | bytes 1048592 | tf_op jit(solution)/shard_map/reduce_scatter | solution.py:597
  487.3 2.7 concatenate.57
  491.1 59.5 %all_to_all.20 = bf16[8,512,128]{2,1,0:T(8,128)(2,1)S(1)} all-to-all(bf16[8,512,128]{2,1,0:T(8,128)(2,1)S(1)} %bitcast_bitcast_fusion.1), channel_id=1, replica_groups=mesh['rep'=8,'shard'=4] {'rep'}, dimensions={0} | all-to-all | bytes 2097152 | tf_op jit(solution)/shard_map/all_to_all | solution.py:550
  550.6 8.4 convolution_convert_fusion.4
  558.9 12.2 %all_to_all.21 = bf16[4,512,128]{2,1,0:T(8,128)(2,1)} all-to-all(bf16[4,512,128]{2,1,0:T(8,128)(2,1)S(1)} %bitcast.141), channel_id=1, replica_groups=mesh['rep'=8,'shard'=4] {'shard'}, dimensions={0} | all-to-all | bytes 1048576 | tf_op jit(solution)/shard_map/all_to_all | solution.py:552
  571.3 97.3 %all-reduce.8.cloned.1.call-done = bf16[1024,2048]{1,0:T(8,128)(2,1)} async-done(((bf16[1024,2048]{1,0:T(8,128)(2,1)}), bf16[1024,2048]{1,0:T(8,128)(2,1)}) %all-reduce.8.cloned.1.call-update) | async-done | bytes 4194320 | tf_op jit(solution)/shard_map/psum | solution.py:540
  668.6 6.7 convert_element_type.104
  675.3 57.7 %all-gather.20.cloned.1.call-done = bf16[16384,80]{1,0:T(8,128)(2,1)} async-done(((bf16[512,80]{1,0:T(8,128)(2,1)}), bf16[16384,80]{1,0:T(8,128)(2,1)}) %all-gather.20.cloned.1.call-update) | async-done | bytes 2621456 | tf_op jit(solution)/shard_map/all_gather | solution.py:612
  733.0 5.8 copy.77
  743.3 115.5 %all-reduce.6.cloned.1.call-done = f32[28099]{0:T(1024)} async-done(((f32[28099]{0:T(1024)}), f32[28099]{0:T(1024)}) %all-reduce.6.cloned.1.call-update) | async-done | bytes 112412 | tf_op jit(solution)/shard_map/psum | solution.py:650
  869.2 4.1 fusion
  873.3 61.8 %all-gather.18.cloned.1.call-done = bf16[32,512,128]{2,1,0:T(8,128)(2,1)} async-done(((bf16[4,512,128]{2,1,0:T(8,128)(2,1)}), bf16[32,512,128]{2,1,0:T(8,128)(2,1)}) %all-gather.18.cloned.1.call-update) | async-done | bytes 4194320 | tf_op jit(solution)/shard_map/all_gather | solution.py:555
  935.2 6.6 convert_bitcast_fusion
  941.7 8.8 copy.76
  950.6 58.6 %all-gather.16.cloned.1.call-done = bf16[32,512,128]{2,1,0:T(8,128)(2,1)} async-done(((bf16[4,512,128]{2,1,0:T(8,128)(2,1)}), bf16[32,512,128]{2,1,0:T(8,128)(2,1)}) %all-gather.16.cloned.1.call-update) | async-done | bytes 4194320 | tf_op jit(solution)/shard_map/all_gather | solution.py:555
  1009.2 6.6 convert_bitcast_fusion.1
  1015.8 8.7 copy.74
  1024.5 16.1 %pad_maximum_fusion = f32[512,8512]{0,1:T(8,128)} fusion(f32[512,320]{0,1:T(8,128)S(1)} %fusion, f32[512,4096]{0,1:T(8,128)} %bitcast.127, f32[512,4096]{0,1:T(8,128)} %bitcast.128), kind=kLoop, calls=%fused_computation | loop fusion | flops 8716288 | bytes 34865152 | tf_op jit(solution)/shard_map/concatenate | solution.py:627
  (204 shorter events, 72.2 us)
Async XLA Ops:
  7.2 150.9 %all-gather.10.cloned.1.call-start = ((), (), s32[]{:S(2)}) async-start(), calls=%async_computation.7 | async-start | bytes 2621440 | tf_op jit(solution)/shard_map/all_gather | solution.py:467
  7.9 176.0 %all-gather.12.cloned.1.call-start = ((), (), s32[]{:S(2)}) async-start(), calls=%async_computation.8 | async-start | bytes 2621440 | tf_op jit(solution)/shard_map/all_gather | solution.py:471
  8.0 5.7 slice-start
  15.9 131.8 %collective-permute-start = (bf16[512,1344]{0,1:T(8,128)(2,1)}, bf16[512,1344]{0,1:T(8,128)(2,1)}, u32[]{:S(2)}, u32[]{:S(2)}) collective-permute-start(bf16[512,1344]{0,1:T(8,128)(2,1)} %get-tuple-element.80), channel_id=1, source_target_pairs={{0,1},{1,0},{2,3},{3,2},{4,5},{5,4},{6,7},{7,6},{8,9},{9,8},{10,11... | collective-permute-start | bytes 4128776 | tf_op jit(solution)/shard_map/ppermute | solution.py:424
  16.3 133.1 %collective-permute-start.1 = (bf16[512,1344]{0,1:T(8,128)(2,1)}, bf16[512,1344]{0,1:T(8,128)(2,1)}, u32[]{:S(2)}, u32[]{:S(2)}) collective-permute-start(bf16[512,1344]{0,1:T(8,128)(2,1)} %get-tuple-element.81), channel_id=1, source_target_pairs={{0,2},{1,3},{2,0},{3,1},{4,6},{5,7},{6,4},{7,5},{8,10},{9,11},{10,... | collective-permute-start | bytes 4128776 | tf_op jit(solution)/shard_map/ppermute | solution.py:424
  18.8 132.5 %collective-permute-start.2 = (bf16[512,1344]{0,1:T(8,128)(2,1)}, bf16[512,1344]{0,1:T(8,128)(2,1)}, u32[]{:S(2)}, u32[]{:S(2)}) collective-permute-start(bf16[512,1344]{0,1:T(8,128)(2,1)} %get-tuple-element.79), channel_id=1, source_target_pairs={{0,3},{1,2},{2,1},{3,0},{4,7},{5,6},{6,5},{7,4},{8,11},{9,10},{10,... | collective-permute-start | bytes 4128776 | tf_op jit(solution)/shard_map/ppermute | solution.py:424
  19.0 5.7 copy-start.25
  19.0 5.7 copy-start.12
  21.3 4.6 copy-start.20
  21.3 4.6 copy-start.30
  21.3 29.7 %collective-permute-start.3 = (bf16[512,1024]{1,0:T(8,128)(2,1)}, bf16[512,1024]{1,0:T(8,128)(2,1)}, u32[]{:S(2)}, u32[]{:S(2)}) collective-permute-start(bf16[512,1024]{1,0:T(8,128)(2,1)} %copy.81), channel_id=1, source_target_pairs={{0,1},{1,0},{2,3},{3,2},{4,5},{5,4},{6,7},{7,6},{8,9},{9,8},{10,11... | collective-permute-start | bytes 3145736 | tf_op jit(solution)/shard_map/ppermute | solution.py:424
  22.8 101.8 %collective-permute-start.4 = (bf16[512,1024]{1,0:T(8,128)(2,1)}, bf16[512,1024]{1,0:T(8,128)(2,1)}, u32[]{:S(2)}, u32[]{:S(2)}) collective-permute-start(bf16[512,1024]{1,0:T(8,128)(2,1)} %copy.82), channel_id=1, source_target_pairs={{0,2},{1,3},{2,0},{3,1},{4,6},{5,7},{6,4},{7,5},{8,10},{9,11},{10,... | collective-permute-start | bytes 3145736 | tf_op jit(solution)/shard_map/ppermute | solution.py:424
  24.7 3.1 copy-start.16
  24.7 3.1 copy-start.29
  24.7 3.9 copy-start.18
  24.7 8.6 slice-start.1
  25.7 240.1 %reduce-scatter.10.cloned.1.call-start = ((), (), s32[]{:S(2)}) async-start(), calls=%async_computation.17 | async-start | bytes 655360
  27.0 14.3 %copy-start.23 = (s32[4,1]{0,1:T(1,128)}, s32[4,1]{0,1:T(1,128)S(1)}, u32[]{:S(2)}) copy-start(s32[4,1]{0,1:T(1,128)S(1)} %reduce-window.17) | copy-start | bytes 52
  44.2 1.4 copy-start.28
  44.2 1.5 copy-start.21
  44.3 1.5 copy-start.22
  44.3 4.0 copy-start.5
  44.3 4.5 copy-start.4
  51.1 95.5 %collective-permute-start.5 = (bf16[512,1024]{1,0:T(8,128)(2,1)S(1)}, bf16[512,1024]{1,0:T(8,128)(2,1)S(1)}, u32[]{:S(2)}, u32[]{:S(2)}) collective-permute-start(bf16[512,1024]{1,0:T(8,128)(2,1)S(1)} %copy.83), channel_id=1, source_target_pairs={{0,3},{1,2},{2,1},{3,0},{4,7},{5,6},{6,5},{7,4},{8,11},{9,10},{10,... | collective-permute-start | bytes 3145736 | tf_op jit(solution)/shard_map/ppermute | solution.py:424
  155.0 1.9 copy-start.2
  158.1 3.0 copy-start.13
  161.1 1.9 copy-start
  183.9 5.4 copy-start.7
  189.3 6.8 copy-start.8
  234.7 158.2 %all-gather.14.cloned.1.call-start = ((), (), s32[]{:S(2)}) async-start(), calls=%async_computation.12 | async-start | bytes 17301504 | tf_op jit(solution)/shard_map/all_gather | solution.py:483
  235.6 202.8 %reduce-scatter.6.cloned.1.call-start = ((), (), s32[]{:S(2)}) async-start(), calls=%async_computation.9 | async-start | bytes 5242880 | tf_op jit(solution)/shard_map/reduce_scatter | solution.py:530
  243.6 242.1 %reduce-scatter.8.cloned.1.call-start = ((), (), s32[]{:S(2)}) async-start(), calls=%async_computation.10 | async-start | bytes 5242880 | tf_op jit(solution)/shard_map/reduce_scatter | solution.py:597
  251.4 14.3 %copy-start.14 = (f32[512,128]{1,0:T(8,128)S(1)}, f32[512,128]{1,0:T(8,128)}, u32[]{:S(2)}) copy-start(f32[512,128]{1,0:T(8,128)} %get-tuple-element.38) | copy-start | bytes 786436
  251.5 15.4 %copy-start.6 = (bf16[512,1024]{1,0:T(8,128)(2,1)S(1)}, bf16[512,1024]{1,0:T(8,128)(2,1)}, u32[]{:S(2)}) copy-start(bf16[512,1024]{1,0:T(8,128)(2,1)} %get-tuple-element.36) | copy-start | bytes 3145732
  282.5 1.2 copy-start.11
  282.5 386.1 %all-reduce.8.cloned.1.call-start = ((), (), s32[]{:S(2)}) async-start(), calls=%async_computation.13 | async-start | bytes 8388608 | tf_op jit(solution)/shard_map/psum | solution.py:540
  290.7 442.3 %all-gather.20.cloned.1.call-start = ((), (), s32[]{:S(2)}) async-start(), calls=%async_computation.16 | async-start | bytes 4325376 | tf_op jit(solution)/shard_map/all_gather | solution.py:612
  291.5 7.1 copy-start.1
  291.5 7.3 copy-start.15
  291.6 7.4 copy-start.17
  291.6 7.9 copy-start.19
  292.7 45.1 %all-to-all-start.2 = ((bf16[8,512,128]{2,1,0:T(8,128)(2,1)}), bf16[8,512,128]{2,1,0:T(8,128)(2,1)S(1)}, u32[]{:S(2)}, u32[]{:S(2)}) async-start(bf16[8,512,128]{2,1,0:T(8,128)(2,1)} %bitcast_bitcast_fusion), calls=%async_computation.4 | async-start | bytes 2097152 | tf_op jit(solution)/shard_map/all_to_all | solution.py:550
  402.1 38.8 %copy-start.26 = (s32[128]{0:T(128)S(1)}, s32[128]{0:T(128)}, u32[]{:S(2)}) copy-start(s32[128]{0:T(128)} %param.20) | copy-start | bytes 1540
  402.1 87.9 %all-to-all-start.3 = ((bf16[4,512,128]{2,1,0:T(8,128)(2,1)}), bf16[4,512,128]{2,1,0:T(8,128)(2,1)S(1)}, u32[]{:S(2)}, u32[]{:S(2)}) async-start(bf16[4,512,128]{2,1,0:T(8,128)(2,1)} %bitcast.61), calls=%async_computation.5 | async-start | bytes 1048576 | tf_op jit(solution)/shard_map/all_to_all | solution.py:552
  405.7 453.1 %all-reduce.6.cloned.1.call-start = ((), (), s32[]{:S(2)}) async-start(), calls=%async_computation.11 | async-start | bytes 229376 | tf_op jit(solution)/shard_map/psum | solution.py:650
  490.0 445.2 %all-gather.18.cloned.1.call-start = ((), (), s32[]{:S(2)}) async-start(), calls=%async_computation.15 | async-start | bytes 4718592 | tf_op jit(solution)/shard_map/all_gather | solution.py:555
  490.8 518.4 %all-gather.16.cloned.1.call-start = ((), (), s32[]{:S(2)}) async-start(), calls=%async_computation.14 | async-start | bytes 4718592 | tf_op jit(solution)/shard_map/all_gather | solution.py:555
  740.0 1.9 copy-start.9
  (4 other events, 3.2 us)
Sparse Core Ops, SparseCore 0:
  9.6 36.6 all-gather.9
  48.4 33.7 all-gather.11
  234.8 21.9 reduce-scatter.9
  260.6 132.3 all-gather.13
  395.5 42.9 reduce-scatter.5
  441.4 44.2 reduce-scatter.7
  490.4 178.2 all-reduce.7
  671.9 61.0 all-gather.19
  739.5 119.2 all-reduce.5
  861.0 74.1 all-gather.17
  937.5 71.6 all-gather.15

commit v2 on v1

--- a/solution.py
+++ b/solution.py
@@ -21,7 +21,6 @@
 EPSILON = 1e-05
 ALL = ("rep", "shard")
 VMEM_BYTES = 56 * 1024 * 1024
-GATHER_BYTES = 32 * 1024 * 1024
 BF = jnp.bfloat16
 F32 = jnp.float32
 
@@ -415,6 +414,285 @@
     )(conv_in, dt, position, conv_w, conv_b, dt_bias, a_log, d_skip, mixed, starts, grad, join)
 
 
+MESH = pl.DeviceIdType.MESH
+LINE, PLANE = 4, 2
+
+
+def end_kernel(
+    gate_ref,
+    values_ref,
+    normed_ref,
+    out_ref,
+    taken,
+    stripes,
+    total,
+    low,
+    local_sem,
+    stripe_sem,
+    a2a_send,
+    a2a_recv,
+    swap_send,
+    swap_recv,
+    line_send,
+    line_recv,
+    side_send,
+    side_recv,
+):
+    reps, shards = LINE * PLANE, lax.axis_size("shard")
+    mine, rep = lax.axis_index("shard"), lax.axis_index("rep")
+    z, x = rep // PLANE, lax.rem(rep, PLANE)
+    beside = z * PLANE + (1 - x)
+    depth = out_ref.shape[3]
+    sources = (gate_ref, values_ref)
+
+    def other(step):
+        return lax.rem(z + step // PLANE, LINE) * PLANE + lax.rem(x + step % PLANE, PLANE)
+
+    def before(step):
+        return lax.rem(z + LINE - step // PLANE, LINE) * PLANE + lax.rem(
+            x + PLANE - step % PLANE, PLANE
+        )
+
+    barrier = pltpu.get_barrier_semaphore()
+    for step in range(1, reps):
+        pl.semaphore_signal(barrier, inc=1, device_id=(other(step), mine), device_id_type=MESH)
+    for step in range(1, shards):
+        pl.semaphore_signal(
+            barrier, inc=1, device_id=(rep, lax.rem(mine + step, shards)), device_id_type=MESH
+        )
+    pl.semaphore_wait(barrier, reps - 1 + shards - 1)
+
+    def share_copy(part, step):
+        peer = other(step)
+        return pltpu.make_async_remote_copy(
+            src_ref=sources[part].at[:, pl.ds(pl.multiple_of(peer * 128, 128), 128)],
+            dst_ref=taken.at[part, step],
+            send_sem=a2a_send.at[part, step],
+            recv_sem=a2a_recv.at[part, step],
+            device_id=(peer, mine),
+            device_id_type=MESH,
+        )
+
+    def own_copy(part):
+        return pltpu.make_async_copy(
+            sources[part].at[:, pl.ds(pl.multiple_of(rep * 128, 128), 128)],
+            taken.at[part, 0],
+            local_sem.at[part],
+        )
+
+    def stripe_copy(step, slot, shard):
+        group = before(step)
+        return pltpu.make_async_copy(
+            normed_ref.at[group, shard],
+            stripes.at[slot, :, pl.ds(128 * shard, 128)],
+            stripe_sem.at[slot, shard],
+        )
+
+    for part in range(2):
+        own_copy(part).start()
+        for step in range(1, reps):
+            share_copy(part, step).start()
+
+    def swap_copy(part, step):
+        peer = lax.rem(mine + step, shards)
+        return pltpu.make_async_remote_copy(
+            src_ref=low.at[part, pl.ds(pl.multiple_of(peer * depth, depth), depth)],
+            dst_ref=out_ref.at[rep, part, mine],
+            send_sem=swap_send.at[part, step],
+            recv_sem=swap_recv.at[part, step],
+            device_id=(rep, peer),
+            device_id_type=MESH,
+        )
+
+    def swap_own(part):
+        return pltpu.make_async_copy(
+            low.at[part, pl.ds(pl.multiple_of(mine * depth, depth), depth)],
+            out_ref.at[rep, part, mine],
+            local_sem.at[2 + part],
+        )
+
+    def line_copy(part, origin, toward, lane):
+        block = out_ref.at[origin * PLANE + x, part]
+        return pltpu.make_async_remote_copy(
+            src_ref=block,
+            dst_ref=block,
+            send_sem=line_send.at[part, lane, origin],
+            recv_sem=line_recv.at[part, origin],
+            device_id=((z + toward) * PLANE + x, mine),
+            device_id_type=MESH,
+        )
+
+    def side_copy(part, origin):
+        block = out_ref.at[origin * PLANE + x, part]
+        return pltpu.make_async_remote_copy(
+            src_ref=block,
+            dst_ref=block,
+            send_sem=side_send.at[part, origin],
+            recv_sem=side_recv.at[part, origin],
+            device_id=(beside, mine),
+            device_id_type=MESH,
+        )
+
+    def side_arrival(part, origin):
+        block = out_ref.at[origin * PLANE + (1 - x), part]
+        return pltpu.make_async_remote_copy(
+            src_ref=block,
+            dst_ref=block,
+            send_sem=side_send.at[part, origin],
+            recv_sem=side_recv.at[part, origin],
+            device_id=(beside, mine),
+            device_id_type=MESH,
+        )
+
+    for part in range(2):
+        for shard in range(shards):
+            stripe_copy(0, 0, shard).start()
+        for step in range(reps):
+            slot = step % 2
+            if step + 1 < reps:
+                for shard in range(shards):
+                    stripe_copy(step + 1, 1 - slot, shard).start()
+            if step == 0:
+                own_copy(part).wait()
+            else:
+                share_copy(part, step).wait_recv()
+            for shard in range(shards):
+                stripe_copy(step, slot, shard).wait()
+
+            def rows(i, unused, part=part, step=step, slot=slot):
+                span = pl.ds(pl.multiple_of(i * 256, 256), 256)
+                term = dot_nn(stripes[slot, span, :], taken[part, step])
+                if step == 0:
+                    total[span, :] = term
+                elif step < reps - 1:
+                    total[span, :] += term
+                else:
+                    low[part, span, :] = (total[span, :] + term).astype(BF)
+                return unused
+
+            lax.fori_loop(0, D // 256, rows, 0)
+        swap_own(part).start()
+        for step in range(1, shards):
+            swap_copy(part, step).start()
+        swap_own(part).wait()
+        for step in range(1, shards):
+            swap_copy(part, step).wait_recv()
+        side_copy(part, z).start()
+
+        @pl.when(z < LINE - 1)
+        def _(part=part):
+            line_copy(part, z, 1, 0).start()
+
+        @pl.when(z > 0)
+        def _(part=part):
+            line_copy(part, z, -1, 1).start()
+
+    for step in range(1, LINE):
+        for part in range(2):
+
+            @pl.when(z - step >= 0)
+            def _(part=part, step=step):
+                origin = z - step
+                line_copy(part, origin, 1, 0).wait_recv()
+                side_copy(part, origin).start()
+
+                @pl.when(z < LINE - 1)
+                def _():
+                    line_copy(part, origin, 1, 0).start()
+
+            @pl.when(z + step < LINE)
+            def _(part=part, step=step):
+                origin = z + step
+                line_copy(part, origin, -1, 1).wait_recv()
+                side_copy(part, origin).start()
+
+                @pl.when(z > 0)
+                def _():
+                    line_copy(part, origin, -1, 1).start()
+
+    for part in range(2):
+        for origin in range(LINE):
+            side_arrival(part, origin).wait_recv()
+            side_copy(part, origin).wait_send()
+
+            @pl.when((origin <= z) & (z < LINE - 1))
+            def _(part=part, origin=origin):
+                line_copy(part, origin, 1, 0).wait_send()
+
+            @pl.when((origin >= z) & (z > 0))
+            def _(part=part, origin=origin):
+                line_copy(part, origin, -1, 1).wait_send()
+
+        for step in range(1, shards):
+            swap_copy(part, step).wait_send()
+        for step in range(1, reps):
+            share_copy(part, step).wait_send()
+
+
+def run_end(gate, values, normed_stripes, shards):
+    reps = LINE * PLANE
+    length = gate.shape[0]
+    depth = D // shards
+    dma = pltpu.SemaphoreType.DMA
+    anywhere = pl.BlockSpec(memory_space=pl.ANY)
+    return pl.pallas_call(
+        end_kernel,
+        out_shape=jax.ShapeDtypeStruct((reps, 2, shards, depth, 128), BF),
+        in_specs=[anywhere] * 3,
+        out_specs=anywhere,
+        scratch_shapes=[
+            pltpu.VMEM((2, reps, length, 128), BF),
+            pltpu.VMEM((2, D, length), BF),
+            pltpu.VMEM((D, 128), F32),
+            pltpu.VMEM((2, D, 128), BF),
+            dma((4,)),
+            dma((2, shards)),
+            dma((2, reps)),
+            dma((2, reps)),
+            dma((2, shards)),
+            dma((2, shards)),
+            dma((2, 2, LINE)),
+            dma((2, LINE)),
+            dma((2, LINE)),
+            dma((2, LINE)),
+        ],
+        compiler_params=pltpu.CompilerParams(
+            vmem_limit_bytes=VMEM_BYTES, collective_id=1, has_side_effects=True
+        ),
+        cost_estimate=pl.CostEstimate(
+            flops=2 * reps * length * D * 256, bytes_accessed=64 << 20, transcendentals=0
+        ),
+        name="weight_gradient",
+    )(gate, values, normed_stripes)
+
+
+def assemble_kernel(parts_ref, tail_ref, out_ref):
+    reps, shards = parts_ref.shape[0], parts_ref.shape[2]
+    for part in range(2):
+        for shard in range(shards):
+            for rep in range(reps):
+                at = part * DI + (shard * reps + rep) * 128
+                out_ref[:, at : at + 128] = parts_ref[rep, part, shard].astype(F32)
+    out_ref[:, 2 * DI :] = tail_ref[...]
+
+
+def run_assemble(parts, tail):
+    reps, unused, shards, depth, unused2 = parts.shape
+    step = 64
+    return pl.pallas_call(
+        assemble_kernel,
+        grid=(depth // step,),
+        out_shape=jax.ShapeDtypeStruct((depth, PROJ), F32),
+        in_specs=[
+            pl.BlockSpec((reps, 2, shards, step, 128), lambda i: (0, 0, 0, i, 0)),
+            pl.BlockSpec((step, TAIL), lambda i: (i, 0)),
+        ],
+        out_specs=pl.BlockSpec((step, PROJ), lambda i: (i, 0)),
+        compiler_params=params(),
+        name="assemble",
+    )(parts, tail)
+
+
 def exchange(pieces, axis, mine):
     count = lax.axis_size(axis)
     own = pieces(mine)
@@ -478,9 +756,9 @@
     normed = (resid * inverse_rms * norm_gain[None, :]).astype(BF)
     normed_mine = lax.dynamic_slice_in_dim(normed, mine * rows, rows, axis=0)
     resid_mine = lax.dynamic_slice_in_dim(resid, mine * rows, rows, axis=0)
-    few = reps * length * D * 2 <= GATHER_BYTES
+    few = reps == LINE * PLANE and width == reps * 128 and rows == 128
     if few:
-        normed_all = lax.all_gather(normed_mine, ALL, axis=0, tiled=True)
+        stripes = lax.all_gather(normed_mine.T, ALL).reshape(reps, shards, D, rows)
 
     projected = dot_nn(normed, w_conv).astype(BF)
     gate_low = dot_nn(normed, w_gate).astype(BF)
@@ -540,22 +818,10 @@
     grad_w_out = lax.psum(dot_tn(normed_out, grad_branch_group).astype(BF), "rep").astype(F32)
 
     def to_owners(columns):
-        if not few:
-            part = dot_tn(normed, columns).astype(BF).reshape(shards, depth, columns.shape[1])
-            swapped = lax.all_to_all(part, "shard", split_axis=0, concat_axis=0, tiled=True)
-            summed = lax.psum(swapped, "rep").astype(F32)
-            return summed.transpose(1, 0, 2).reshape(depth, shards * columns.shape[1])
-        share = columns.shape[1] // reps
-        split = columns.reshape(length, reps, share).transpose(1, 0, 2)
-        taken = lax.all_to_all(split, "rep", split_axis=0, concat_axis=0, tiled=True)
-        summed = dot_tn(normed_all, taken.reshape(reps * length, share)).astype(BF)
-        swapped = lax.all_to_all(
-            summed.reshape(shards, depth, share), "shard", split_axis=0, concat_axis=0, tiled=True
-        )
-        whole = lax.all_gather(swapped, "rep")
-        return whole.transpose(2, 1, 0, 3).reshape(depth, DI).astype(F32)
-
-    grad_w_gate = to_owners(grad_gate)
+        part = dot_tn(normed, columns).astype(BF).reshape(shards, depth, columns.shape[1])
+        swapped = lax.all_to_all(part, "shard", split_axis=0, concat_axis=0, tiled=True)
+        summed = lax.psum(swapped, "rep").astype(F32)
+        return summed.transpose(1, 0, 2).reshape(depth, shards * columns.shape[1])
 
     join = (
         jnp.arange(width, dtype=jnp.int32)[:, None] // P_SIZE
@@ -607,24 +873,22 @@
     back_mine = lax.dynamic_slice_in_dim(back, mine * rows, rows, axis=0)
     grad_in = (grad_resid + dot_nn(back_mine, grad_branch_group)).astype(BF)
 
-    grad_w_values = to_owners(grad_values)
+    tails = lax.all_gather(grad_tail, "shard")
+    tails = jnp.concatenate(
+        [
+            tails[..., :share].transpose(1, 0, 2).reshape(length, 2 * N),
+            tails[..., share:].transpose(1, 0, 2).reshape(length, H),
+        ],
+        axis=1,
+    )
+    grad_w_tail = lax.psum(dot_tn(columns_at(normed, mine * depth, depth), tails), "rep")
     if few:
-        tails = lax.all_gather(grad_tail, ALL, axis=0, tiled=False)
-        tails = tails.reshape(reps, shards, length, share + heads).transpose(0, 2, 1, 3)
-        tails = jnp.concatenate(
-            [
-                tails[..., :share].reshape(reps * length, 2 * N),
-                tails[..., share:].reshape(reps * length, H),
-            ],
-            axis=1,
-        )
-        grad_w_tail = dot_tn(columns_at(normed_all, mine * depth, depth), tails)
+        parts = run_end(grad_gate, grad_values, stripes, shards)
+        grad_w_in = run_assemble(parts, grad_w_tail)
     else:
-        parts = to_owners(grad_tail).reshape(depth, shards, share + heads)
-        grad_w_tail = jnp.concatenate(
-            [parts[..., :share].reshape(depth, 2 * N), parts[..., share:].reshape(depth, H)], axis=1
-        )
-    grad_w_in = jnp.concatenate([grad_w_gate, grad_w_values, grad_w_tail], axis=1)
+        grad_w_in = jnp.concatenate(
+            [to_owners(grad_gate), to_owners(grad_values), grad_w_tail], axis=1
+        )
 
     def placed(part, whole, start):
         return lax.dynamic_update_slice_in_dim(

time: 1050 us -> 974 us (0.928); the launches traced: 1050 us -> 960 us
  Pallas kernels: 37.6 us -> 191 us
  waiting for transfers between devices: 646 us -> 507 us
  blocking collectives: 78.8 us -> 14.2 us
  other arithmetic: 65 us -> 35.8 us
  local copies, waits for them, and re-layouts: 116 us -> 136 us
  matrix products: 71.8 us -> 52.4 us
    pallas_call x0 -> x2, Pallas kernels: none -> 153 us  [the longest x1 142 us: run_end(): pl.pallas_call(end_kernel, out_shape=jax.ShapeDtypeStruct((reps, 2, shard...]
    all_gather x4 -> x1, waiting for transfers between devices: 233 us -> 109 us  [on_device(): stripes = lax.all_gather(normed_mine.T, ALL).reshape(reps, shards, D, rows)]
    all_to_all x2 -> x0, blocking collectives: 71.6 us -> none  [the longest x1 59.5 us: to_owners(): lax.all_to_all(split, 'rep', split_axis=0, concat_axis=0, tiled=True)]
    psum x1, waiting for transfers between devices: 97.3 us -> 144 us  [on_device(): lax.psum(dot_tn(normed_out, grad_branch_group).astype(BF), 'rep')]
    all_to_all x2 -> x0, waiting for transfers between devices: 35.4 us -> none  [the longest x1 35.4 us: to_owners(): lax.all_to_all(split, 'rep', split_axis=0, concat_axis=0, tiled=True)]
    reduce_scatter x1, waiting for transfers between devices: 32.6 us -> 5.34 us  [on_device(): lax.psum_scatter(dot_nn(normed_out, w_out), 'shard', scatter_dimension=0,...]
    all_gather x0 -> x1, local copies, waits for them, and re-layouts: none -> 22.4 us  [on_device(): stripes = lax.all_gather(normed_mine.T, ALL).reshape(reps, shards, D, rows)]
    dot_general x4 -> x2, matrix products: 28.6 us -> 8.42 us  [dot_tn(): lax.dot_general(a, b, (((0,), (0,)), ((), ())), preferred_element_type=F32)]
  transfers between devices with their start and end apart: 19 -> 15, of which waited for: 11 -> 7; matrix products, arithmetic and copies ran while one was open for 19% -> 19% of each run, Pallas kernels for 1% -> 16%
where the time goes in v2:
time: 974 us; the launch traced here: 960 us
  waiting for transfers between devices  507 us (52%)
  Pallas kernels  191 us (20%)
  local copies, waits for them, and re-layouts  136 us (14%)
  matrix products  52.4 us (5%)
  other arithmetic  35.8 us (4%)
  between operations  19 us (2%)
  blocking collectives  14.2 us (1%)
    psum x1, waiting for transfers between devices, on_device(): lax.psum(dot_tn(normed_out, grad_branch_group).astype(BF), 'rep')  144 us
    pallas_call x1, Pallas kernels, run_end(): pl.pallas_call(end_kernel, out_shape=jax.ShapeDtypeStruct((reps, 2, shard...  142 us
    psum x1, waiting for transfers between devices, on_device(): summed = lax.psum(jnp.concatenate(pieces), ALL)  117 us
    all_gather x1, waiting for transfers between devices, on_device(): stripes = lax.all_gather(normed_mine.T, ALL).reshape(reps, shards, D, rows)  109 us
    ppermute x6, waiting for transfers between devices, exchange(): lax.ppermute(pieces(mine ^ other), axis, [(i, i ^ other) for i in range(c...  86.6 us
    reduce_scatter x1, waiting for transfers between devices, on_device(): lax.psum_scatter(dot_nt(grad_given, w_own), 'shard', scatter_dimension=0,...  44.4 us
    unnamed x66, local copies, waits for them, and re-layouts  32.1 us
    dot_general x5, matrix products, dot_nn(): lax.dot_general(a, b, (((1,), (0,)), ((), ())), preferred_element_type=F32)  26.1 us
  transfers between devices with their start and end apart: 15, of which 7 were waited for; matrix products, arithmetic and copies ran while one was open for 19% of the time, Pallas kernels for 16%

profile of v2, /device:TPU:0, one launch (start us, length us, event | category | flops | bytes accessed | tf_op | source)
XLA Modules:
  0.0 960.5 jit_solution(1321695105291453504)
XLA Ops:
  8.0 5.7 constant_dynamic-slice_fusion.2
  13.7 2.2 pad_maximum_fusion
  16.4 2.5 collective-permute-start.1
  19.0 2.4 copy.83
  22.8 1.9 collective-permute-start.4
  28.8 4.5 compare_select_fusion.2
  34.1 5.7 select_select_fusion
  41.3 2.9 broadcast_in_dim.108
  51.7 2.5 broadcast_in_dim.118
  55.3 2.4 bitcast_dynamic-update-slice_fusion.2
  57.8 66.9 %collective-permute-done.4 = bf16[512,1024]{1,0:T(8,128)(2,1)} collective-permute-done((bf16[512,1024]{1,0:T(8,128)(2,1)}, bf16[512,1024]{1,0:T(8,128)(2,1)}, u32[]{:S(2)}, u32[]{:S(2)}) %collective-permute-start.4) | collective-permute-done | bytes 1048608 | tf_op jit(solution)/shard_map/ppermute | solution.py:702
  124.7 2.3 bitcast_dynamic-update-slice_fusion.1
  126.9 19.7 %collective-permute-done.5 = bf16[512,1024]{1,0:T(8,128)(2,1)S(1)} collective-permute-done((bf16[512,1024]{1,0:T(8,128)(2,1)S(1)}, bf16[512,1024]{1,0:T(8,128)(2,1)S(1)}, u32[]{:S(2)}, u32[]{:S(2)}) %collective-permute-start.5) | collective-permute-done | bytes 1048608 | tf_op jit(solution)/shard_map/ppermute | solution.py:702
  147.7 1.8 copy.64
  149.5 1.8 copy.65
  151.3 2.5 copy.66
  158.2 3.0 multiply_reduce_fusion
  163.1 6.0 convolution_convert_fusion.2
  171.1 13.1 %mixer_forward.1 = (f32[512,1024]{1,0:T(8,128)}, f32[512,1024]{1,0:T(8,128)}) custom-call(bf16[512,1280]{1,0:T(8,128)(2,1)} %slice.146.conv_in_ref, f32[512,128]{1,0:T(8,128)} %pad.14.dt_ref, s32[512,1]{1,0:T(8,128)} %copy.68.position_ref, f32[4,1280]{1,0:T(4,128)} %pad_maximum_fusion.6.conv_w_ref, f32[1,1280]{1,0:T(1,128)} %pad_maximum_fusion.7.conv_b_ref, ...), custom_call_target="tpu_custom_call" | custom-call | flops 1342177280 | bytes 6291456 | tf_op jit(solution)/shard_map/mixer_forward/pallas_call | solution.py:364
  184.2 5.3 fusion.46
  189.6 6.8 multiply_reduce_fusion.3
  196.4 7.1 psum.28
  203.6 4.5 fusion.14
  208.1 24.9 %mixer_backward.1 = (bf16[512,1024]{1,0:T(8,128)(2,1)}, f32[512,256]{1,0:T(8,128)}, f32[512,128]{1,0:T(8,128)}, f32[4,1280]{1,0:T(4,128)}, f32[1,1280]{1,0:T(1,1...) custom-call(bf16[512,1280]{1,0:T(8,128)(2,1)} %slice.146.conv_in_ref, f32[512,128]{1,0:T(8,128)} %pad.14.dt_ref, ...), custom_call_target="tpu_custom_call" | custom-call | flops 2684354560 | bytes 10485760 | tf_op jit(solution)/shard_map/mixer_backward/pallas_call | solution.py:389
  233.0 2.1 copy.81
  235.2 7.9 fusion.39
  243.9 4.6 slice.152
  248.5 2.0 constant_dynamic-slice_fusion.1
  250.5 2.1 constant_dynamic-slice_fusion
  252.6 14.3 %concatenate.51 = bf16[2048,2128]{1,0:T(8,128)(2,1)} concatenate(bf16[2048,1024]{1,0:T(8,128)(2,1)} %bitcast.42, bf16[2048,1024]{1,0:T(8,128)(2,1)} %slice.152, bf16[2048,64]{1,0:T(8,128)(2,1)} %constant_dynamic-slice_fusion.1, bf16[2048,16]{1,0:T(8,128)(2,1)} %constant_dynamic-slice_fusion), dimensions={1} | concatenate | bytes 17432576 | tf_op jit(solution)/shard_map/concatenate | solution.py:854
  269.0 4.4 concatenate.50
  273.3 12.6 %fusion.17 = f32[512,2048]{1,0:T(8,128)} fusion(bf16[2048,2128]{1,0:T(8,128)(2,1)} %concatenate.51, bf16[512,2128]{1,0:T(8,128)(2,1)} %concatenate.50, s32[512]{0:T(512)S(1)} %select_reduce_fusion), kind=kOutput, calls=%fused_computation.49 | convolution fusion | flops 5579776000 | bytes 15091712 | tf_op jit(solution)/shard_map/dot_general | solution.py:33
  287.2 7.0 convolution_convert_fusion.1
  299.0 5.3 reduce-scatter.6.cloned.1.call-done
  304.4 2.5 multiply_reduce_fusion.4
  307.5 44.4 %reduce-scatter.8.cloned.1.call-done = f32[128,2048]{1,0:T(8,128)} async-done(((f32[512,2048]{1,0:T(8,128)}), f32[128,2048]{1,0:T(8,128)}) %reduce-scatter.8.cloned.1.call-update) | async-done | bytes 1048592 | tf_op jit(solution)/shard_map/reduce_scatter | solution.py:863
  351.9 1.6 fusion.13
  353.5 2.7 concatenate.54
  358.2 7.0 all-gather.1
  369.1 143.7 %all-reduce.11.cloned.1.call-done = bf16[1024,2048]{1,0:T(8,128)(2,1)} async-done(((bf16[1024,2048]{1,0:T(8,128)(2,1)}), bf16[1024,2048]{1,0:T(8,128)(2,1)}) %all-reduce.11.cloned.1.call-update) | async-done | bytes 4194320 | tf_op jit(solution)/shard_map/psum | solution.py:818
  512.8 6.8 convert_element_type.72
  519.6 2.3 fusion
  521.9 117.2 %all-reduce.7.cloned.1.call-done = f32[28099]{0:T(1024)} async-done(((f32[28099]{0:T(1024)}), f32[28099]{0:T(1024)}) %all-reduce.7.cloned.1.call-update) | async-done | bytes 112412 | tf_op jit(solution)/shard_map/psum | solution.py:914
  649.4 108.7 %all-gather.10.cloned.1.call-done = bf16[65536,128]{0,1:T(8,128)(2,1)} async-done(((bf16[2048,128]{0,1:T(8,128)(2,1)}), bf16[65536,128]{0,1:T(8,128)(2,1)}) %all-gather.10.cloned.1.call-update) | async-done | bytes 16777232 | tf_op jit(solution)/shard_map/all_gather | solution.py:761
  758.1 22.4 %copy.74 = bf16[65536,128]{1,0:T(8,128)(2,1)} copy(bf16[65536,128]{0,1:T(8,128)(2,1)} %all-gather.10.cloned.1.call-done) | data formatting | bytes 33554432 | tf_op jit(solution)/shard_map/all_gather | solution.py:761
  780.5 142.4 %weight_gradient.1.parts_ref = bf16[8,2,4,512,128]{4,3,2,1,0:T(8,128)(2,1)} custom-call(bf16[512,1024]{1,0:T(8,128)(2,1)} %copy-done.1, bf16[512,1024]{1,0:T(8,128)(2,1)} %get-tuple-element.36.values_ref, bf16[8,4,2048,128]{3,2,1,0:T(8,128)(2,1)} %bitcast.94), custom_call_target="tpu_custom_call" | custom-call | flops 4294967296 | bytes 67108864 | tf_op jit(solution)/shard_map/weight_gradient/pallas_call | solution.py:638
  923.0 10.6 %assemble.1 = f32[512,8512]{1,0:T(8,128)} custom-call(bf16[8,2,4,512,128]{4,3,2,1,0:T(8,128)(2,1)} %weight_gradient.1.parts_ref, f32[512,320]{1,0:T(8,128)} %all-reduce.9.cloned.1.call-done.tail_ref), custom_call_target="tpu_custom_call" | custom-call | tf_op jit(solution)/shard_map/assemble/pallas_call | solution.py:682
  933.6 17.9 %copy.78 = f32[512,8512]{0,1:T(8,128)} copy(f32[512,8512]{1,0:T(8,128)} %assemble.1) | data formatting | bytes 34865152
  (182 shorter events, 50.5 us)
Async XLA Ops:
  7.2 151.0 %all-gather.6.cloned.1.call-start = ((), (), s32[]{:S(2)}) async-start(), calls=%async_computation.3 | async-start | bytes 2621440 | tf_op jit(solution)/shard_map/all_gather | solution.py:745
  7.9 176.3 %all-gather.8.cloned.1.call-start = ((), (), s32[]{:S(2)}) async-start(), calls=%async_computation.4 | async-start | bytes 2621440 | tf_op jit(solution)/shard_map/all_gather | solution.py:749
  8.0 5.7 slice-start
  15.9 131.8 %collective-permute-start = (bf16[512,1344]{0,1:T(8,128)(2,1)}, bf16[512,1344]{0,1:T(8,128)(2,1)}, u32[]{:S(2)}, u32[]{:S(2)}) collective-permute-start(bf16[512,1344]{0,1:T(8,128)(2,1)} %get-tuple-element.132), channel_id=1, source_target_pairs={{0,1},{1,0},{2,3},{3,2},{4,5},{5,4},{6,7},{7,6},{8,9},{9,8},{10,11... | collective-permute-start | bytes 4128776 | tf_op jit(solution)/shard_map/ppermute | solution.py:702
  16.4 133.1 %collective-permute-start.1 = (bf16[512,1344]{0,1:T(8,128)(2,1)}, bf16[512,1344]{0,1:T(8,128)(2,1)}, u32[]{:S(2)}, u32[]{:S(2)}) collective-permute-start(bf16[512,1344]{0,1:T(8,128)(2,1)} %get-tuple-element.133), channel_id=1, source_target_pairs={{0,2},{1,3},{2,0},{3,1},{4,6},{5,7},{6,4},{7,5},{8,10},{9,11},{10,... | collective-permute-start | bytes 4128776 | tf_op jit(solution)/shard_map/ppermute | solution.py:702
  18.9 132.5 %collective-permute-start.2 = (bf16[512,1344]{0,1:T(8,128)(2,1)}, bf16[512,1344]{0,1:T(8,128)(2,1)}, u32[]{:S(2)}, u32[]{:S(2)}) collective-permute-start(bf16[512,1344]{0,1:T(8,128)(2,1)} %get-tuple-element.131), channel_id=1, source_target_pairs={{0,3},{1,2},{2,1},{3,0},{4,7},{5,6},{6,5},{7,4},{8,11},{9,10},{10,... | collective-permute-start | bytes 4128776 | tf_op jit(solution)/shard_map/ppermute | solution.py:702
  19.0 5.7 copy-start.23
  19.0 5.7 copy-start.11
  21.4 4.7 copy-start.18
  21.4 4.7 copy-start.28
  21.4 29.7 %collective-permute-start.3 = (bf16[512,1024]{1,0:T(8,128)(2,1)}, bf16[512,1024]{1,0:T(8,128)(2,1)}, u32[]{:S(2)}, u32[]{:S(2)}) collective-permute-start(bf16[512,1024]{1,0:T(8,128)(2,1)} %copy.83), channel_id=1, source_target_pairs={{0,1},{1,0},{2,3},{3,2},{4,5},{5,4},{6,7},{7,6},{8,9},{9,8},{10,11... | collective-permute-start | bytes 3145736 | tf_op jit(solution)/shard_map/ppermute | solution.py:702
  22.8 101.8 %collective-permute-start.4 = (bf16[512,1024]{1,0:T(8,128)(2,1)}, bf16[512,1024]{1,0:T(8,128)(2,1)}, u32[]{:S(2)}, u32[]{:S(2)}) collective-permute-start(bf16[512,1024]{1,0:T(8,128)(2,1)} %copy.84), channel_id=1, source_target_pairs={{0,2},{1,3},{2,0},{3,1},{4,6},{5,7},{6,4},{7,5},{8,10},{9,11},{10,... | collective-permute-start | bytes 3145736 | tf_op jit(solution)/shard_map/ppermute | solution.py:702
  24.7 3.2 copy-start.14
  24.7 3.2 copy-start.27
  24.7 4.0 copy-start.16
  24.8 8.7 slice-start.1
  25.7 242.2 %reduce-scatter.10.cloned.1.call-start = ((), (), s32[]{:S(2)}) async-start(), calls=%async_computation.11 | async-start | bytes 655360
  26.4 0.5 copy-start.25
  27.1 14.2 %copy-start.21 = (s32[4,1]{0,1:T(1,128)}, s32[4,1]{0,1:T(1,128)S(1)}, u32[]{:S(2)}) copy-start(s32[4,1]{0,1:T(1,128)S(1)} %reduce-window.17) | copy-start | bytes 52
  44.3 1.4 copy-start.26
  44.3 1.5 copy-start.19
  44.3 1.5 copy-start.20
  44.3 4.0 copy-start.5
  44.3 4.5 copy-start.4
  51.1 95.6 %collective-permute-start.5 = (bf16[512,1024]{1,0:T(8,128)(2,1)S(1)}, bf16[512,1024]{1,0:T(8,128)(2,1)S(1)}, u32[]{:S(2)}, u32[]{:S(2)}) collective-permute-start(bf16[512,1024]{1,0:T(8,128)(2,1)S(1)} %copy.85), channel_id=1, source_target_pairs={{0,3},{1,2},{2,1},{3,0},{4,7},{5,6},{6,5},{7,4},{8,11},{9,10},{10,... | collective-permute-start | bytes 3145736 | tf_op jit(solution)/shard_map/ppermute | solution.py:702
  155.1 1.9 copy-start.3
  158.2 3.0 copy-start.12
  161.1 1.9 copy-start
  184.2 5.4 copy-start.7
  189.6 6.8 copy-start.8
  208.1 60.9 %copy-start.1 = (bf16[512,1024]{1,0:T(8,128)(2,1)}, bf16[512,1024]{1,0:T(8,128)(2,1)S(1)}, u32[]{:S(2)}) copy-start(bf16[512,1024]{1,0:T(8,128)(2,1)S(1)} %get-tuple-element.128.gate_ref) | copy-start | bytes 3145732
  235.1 69.2 %reduce-scatter.6.cloned.1.call-start = ((), (), s32[]{:S(2)}) async-start(), calls=%async_computation.5 | async-start | bytes 5242880 | tf_op jit(solution)/shard_map/reduce_scatter | solution.py:808
  243.1 0.7 copy-start.22
  243.2 108.7 %reduce-scatter.8.cloned.1.call-start = ((), (), s32[]{:S(2)}) async-start(), calls=%async_computation.6 | async-start | bytes 5242880 | tf_op jit(solution)/shard_map/reduce_scatter | solution.py:863
  285.9 1.2 copy-start.10
  286.0 226.8 %all-reduce.11.cloned.1.call-start = ((), (), s32[]{:S(2)}) async-start(), calls=%async_computation.9 | async-start | bytes 8388608 | tf_op jit(solution)/shard_map/psum | solution.py:818
  294.2 1.0 copy-start.2
  294.2 1.2 copy-start.13
  294.2 1.4 copy-start.15
  294.2 1.9 copy-start.17
  294.2 12.7 %copy-start.24 = (s32[128]{0:T(128)S(1)}, s32[128]{0:T(128)}, u32[]{:S(2)}) copy-start(s32[128]{0:T(128)} %param.20) | copy-start | bytes 1540
  294.2 344.8 %all-reduce.7.cloned.1.call-start = ((), (), s32[]{:S(2)}) async-start(), calls=%async_computation.7 | async-start | bytes 229376 | tf_op jit(solution)/shard_map/psum | solution.py:914
  356.2 401.9 %all-gather.10.cloned.1.call-start = ((), (), s32[]{:S(2)}) async-start(), calls=%async_computation.10 | async-start | bytes 17301504 | tf_op jit(solution)/shard_map/all_gather | solution.py:761
  357.1 565.8 %all-reduce.9.cloned.1.call-start = ((), (), s32[]{:S(2)}) async-start(), calls=%async_computation.8 | async-start | bytes 1572864 | tf_op jit(solution)/shard_map/psum | solution.py:884
  369.1 150.5 %copy-start.6 = (f32[128,2048]{1,0:T(8,128)S(1)}, f32[128,2048]{1,0:T(8,128)}, u32[]{:S(2)}) copy-start(f32[128,2048]{1,0:T(8,128)} %reduce-scatter.8.cloned.1.call-done) | copy-start | bytes 3145732
  512.8 6.8 copy-start.9
Sparse Core Ops, SparseCore 0:
  9.6 36.6 all-gather.5
  48.4 33.8 all-gather.7
  235.3 21.9 reduce-scatter.9
  259.9 44.4 reduce-scatter.5
  307.3 44.4 reduce-scatter.7
  356.4 156.3 all-reduce.10
  519.3 119.7 all-reduce.6
  642.4 115.6 all-gather.9
  761.9 90.0 all-reduce.8

commit v3 on v1

v3 whole, which is shorter than its diff:
```python
import functools

import jax
import jax.numpy as jnp
from jax import lax
from jax.experimental import pallas as pl
from jax.experimental.pallas import tpu as pltpu
from jax.sharding import PartitionSpec as P

D = 2048
H = 64
P_SIZE = 64
N = 128
KW = 4
SPAN = 128
DI = 4096
CONVW = 4352
PROJ = 8512
TAIL = PROJ - 2 * DI

EPSILON = 1e-05
ALL = ("rep", "shard")
VMEM_BYTES = 56 * 1024 * 1024
BF = jnp.bfloat16
F32 = jnp.float32


def dot_nn(a, b):
    return lax.dot_general(a, b, (((1,), (0,)), ((), ())), preferred_element_type=F32)


def dot_nt(a, b):
    return lax.dot_general(a, b, (((1,), (1,)), ((), ())), preferred_element_type=F32)


def dot_tn(a, b):
    return lax.dot_general(a, b, (((0,), (0,)), ((), ())), preferred_element_type=F32)


def halves(a):
    high = a.astype(BF)
    return high, (a - high.astype(F32)).astype(BF)


def slot_tables(seq_lengths, seq_order, slot_ids):
    seq_count = seq_lengths.shape[0]
    numbers = jnp.arange(seq_count, dtype=jnp.int32)
    chosen = (seq_order[:, None] == numbers[None, :]).astype(jnp.int32)
    given_start = jnp.cumsum(seq_lengths) - seq_lengths
    owner_length = jnp.sum(chosen * seq_lengths[None, :], axis=1)
    owner_start = jnp.cumsum(owner_length) - owner_length
    owner_from = jnp.sum(chosen * given_start[None, :], axis=1)
    placed_at = jnp.sum(chosen * owner_start[:, None], axis=0)
    column = slot_ids[:, None]
    within = (column >= owner_start[None, :]) & (column < (owner_start + owner_length)[None, :])
    offset = column - owner_start[None, :]
    source = jnp.sum(jnp.where(within, offset + owner_from[None, :], 0), axis=1)
    position = jnp.sum(jnp.where(within, offset, 0), axis=1)
    given_within = (column >= given_start[None, :]) & (
        column < (given_start + seq_lengths)[None, :]
    )
    target = jnp.sum(
        jnp.where(given_within, column - given_start[None, :] + placed_at[None, :], 0), axis=1
    )
    return (source, target, position)


def params():
    return pltpu.CompilerParams(vmem_limit_bytes=VMEM_BYTES)


def spread_rows(row):
    return jnp.broadcast_to(row, (16, row.shape[1]))


def sigmoid(v):
    return 1.0 / (1.0 + jnp.exp(-v))


def spread(column, lanes=128):
    return jnp.broadcast_to(column, (column.shape[0], lanes))


MESH = pl.DeviceIdType.MESH
LINE, PLANE = 4, 2
CHUNK = 256
TAIL_PAD = 384


def remote(src, dst, send_sem, recv_sem, device):
    return pltpu.make_async_remote_copy(
        src_ref=src,
        dst_ref=dst,
        send_sem=send_sem,
        recv_sem=recv_sem,
        device_id=device,
        device_id_type=MESH,
    )


def meet(devices):
    barrier = pltpu.get_barrier_semaphore()
    for device in devices:
        pl.semaphore_signal(barrier, inc=1, device_id=device, device_id_type=MESH)
    pl.semaphore_wait(barrier, len(devices))


def tables_in_kernel(lengths_ref, order_ref, slots):
    count = lengths_ref.shape[1]
    lengths = [lengths_ref[0, i] for i in range(count)]
    order = [order_ref[0, i] for i in range(count)]
    given_start, at = [], jnp.int32(0)
    for i in range(count):
        given_start.append(at)
        at = at + lengths[i]
    source = jnp.zeros_like(slots)
    position = jnp.zeros_like(slots)
    placed_at = [jnp.int32(0)] * count
    at = jnp.int32(0)
    for k in range(count):
        length, start = jnp.int32(0), jnp.int32(0)
        for i in range(count):
            chosen = order[k] == i
            length = length + jnp.where(chosen, lengths[i], 0)
            start = start + jnp.where(chosen, given_start[i], 0)
            placed_at[i] = placed_at[i] + jnp.where(chosen, at, 0)
        within = (slots >= at) & (slots < at + length)
        source = source + jnp.where(within, slots - at + start, 0)
        position = position + jnp.where(within, slots - at, 0)
        at = at + length
    target = jnp.zeros_like(slots)
    for i in range(count):
        within = (slots >= given_start[i]) & (slots < given_start[i] + lengths[i])
        target = target + jnp.where(within, slots - given_start[i] + placed_at[i], 0)
    return source, target, position


def start_kernel(
    lengths_ref,
    order_ref,
    x_ref,
    cotangent_ref,
    valid_ref,
    gain_ref,
    w_ref,
    normed_out_ref,
    conv_in_ref,
    gate_ref,
    w_gate_out_ref,
    w_conv_out_ref,
    branch_grad_ref,
    back_ref,
    place_ref,
    resid_ref,
    x_all,
    normed,
    w_gate,
    w_conv,
    grads,
    local_sem,
    row_send,
    row_recv,
    w_send,
    w_recv,
    w_local,
):
    mine, rep = lax.axis_index("shard"), lax.axis_index("rep")
    y, c = mine // 2, lax.rem(mine, 2)
    z, x = rep // PLANE, lax.rem(rep, PLANE)
    sibling, peer, far = y * 2 + (1 - c), (1 - y) * 2 + c, (1 - y) * 2 + (1 - c)
    beside = z * PLANE + (1 - x)
    rows, length = x_ref.shape[0], x_all.shape[0]
    depth, width = w_ref.shape[1], gate_ref.shape[1]
    chunks = width // CHUNK
    tail_half = TAIL // 2
    meet([(rep, sibling), (rep, peer), (rep, far), (beside, mine)])

    def block(ref, shard):
        return ref.at[pl.ds(pl.multiple_of(shard * rows, rows), rows)]

    def row_copies(kind, own, store):
        return (
            remote(own, block(store, mine), row_send.at[kind, 0], row_recv.at[kind, 0], (rep, peer)),
            remote(own, block(store, mine), row_send.at[kind, 1], row_recv.at[kind, 1], (rep, sibling)),
            remote(
                block(store, peer),
                block(store, peer),
                row_send.at[kind, 2],
                row_recv.at[kind, 2],
                (rep, sibling),
            ),
        )

    def lanes(shard):
        return pl.ds(pl.multiple_of(shard * depth, depth), depth)

    def weight_copies(store, index, base, stride, at, half):
        share = pl.ds(pl.multiple_of(at + half * x, 16), half)
        both = pl.ds(pl.multiple_of((1 - y) * 2 * depth, 128), 2 * depth)

        def source(shard, start, count):
            return w_ref.at[pl.ds(pl.multiple_of(base + stride * shard + start, 16), count)]

        def sems(way):
            return w_send.at[way, index], w_recv.at[way, index]

        whole = pl.ds(pl.multiple_of(at, 16), 2 * half)
        near = at if stride else 0
        return (
            lambda: remote(
                source(peer, near + half * x, half), store.at[share, lanes(mine)], *sems(0), (rep, peer)
            ),
            lambda: remote(
                source(far, near + half * x, half), store.at[share, lanes(mine)], *sems(1), (rep, far)
            ),
            lambda: remote(store.at[share, both], store.at[share, both], *sems(2), (beside, mine)),
            lambda: remote(
                source(sibling, near, 2 * half), store.at[whole, lanes(mine)], *sems(3), (rep, sibling)
            ),
            lambda: pltpu.make_async_copy(
                source(mine, near, 2 * half), store.at[whole, lanes(mine)], w_local.at[index]
            ),
        )

    def conv_copies(q):
        return weight_copies(w_conv, q, DI, width, q * CHUNK, CHUNK // 2)

    def tail_copies():
        return weight_copies(w_conv, chunks, 2 * DI, 0, width, tail_half)

    def gate_copies(q):
        return weight_copies(w_gate, chunks + 1 + q, 0, width, q * CHUNK, CHUNK // 2)

    def send_out(copies):
        for i in (0, 1, 3, 4):
            copies[i]().start()

    def pass_on(copies):
        copies[0]().wait_recv()
        copies[1]().wait_recv()
        copies[2]().start()

    def arrived(copies):
        copies[2]().wait_recv()
        copies[3]().wait_recv()
        copies[4]().wait()

    def each(count, body):
        def step(i, unused):
            body(i)
            return unused

        lax.fori_loop(0, count, step, 0)

    x_copies = row_copies(0, x_ref, x_all)
    own_rows = pltpu.make_async_copy(x_ref, block(x_all, mine), local_sem.at[0])
    x_copies[0].start()
    x_copies[1].start()
    own_rows.start()
    each(chunks, lambda q: send_out(conv_copies(q)))
    send_out(tail_copies())
    grads[pl.ds(pl.multiple_of(mine * rows, rows), rows), :] = jnp.where(
        spread(valid_ref[...], D) > 0, cotangent_ref[...].astype(F32), 0.0
    ).astype(BF)
    w_conv[width + TAIL :, :] = jnp.zeros((TAIL_PAD - TAIL, D), BF)

    def table_block(i):
        span = pl.ds(pl.multiple_of(i * rows, rows), rows)
        slots = lax.broadcasted_iota(jnp.int32, (rows, length), 0) + i * rows
        across = lax.broadcasted_iota(jnp.int32, (rows, length), 1)
        target = tables_in_kernel(lengths_ref, order_ref, slots)[1]
        back_ref[span, :] = (target == across).astype(F32).astype(BF)
        few_slots = lax.broadcasted_iota(jnp.int32, (rows, 128), 0) + i * rows
        place_ref[span, :] = tables_in_kernel(lengths_ref, order_ref, few_slots)[2]

    each(length // rows, table_block)
    x_copies[0].wait_recv()
    x_copies[2].start()
    own_rows.wait()
    x_copies[1].wait_recv()
    x_copies[2].wait_recv()

    def picked(i):
        slots = lax.broadcasted_iota(jnp.int32, (rows, length), 0) + i * rows
        across = lax.broadcasted_iota(jnp.int32, (rows, length), 1)
        source = tables_in_kernel(lengths_ref, order_ref, slots)[0]
        return dot_nn((source == across).astype(F32).astype(BF), x_all[...])

    def norm_block(i):
        span = pl.ds(pl.multiple_of(i * rows, rows), rows)
        resid = picked(i)
        inverse = lax.rsqrt(jnp.mean(resid * resid, axis=1, keepdims=True) + EPSILON)
        normed[span, :] = (resid * inverse * gain_ref[...]).astype(BF)

    each(length // rows, norm_block)
    resid_ref[...] = picked(mine).astype(BF)
    normed_store = pltpu.make_async_copy(normed, normed_out_ref, local_sem.at[1])
    normed_store.start()

    each(chunks, lambda q: pass_on(conv_copies(q)))
    pass_on(tail_copies())
    each(chunks, lambda q: send_out(gate_copies(q)))

    def project(store, target, at, count):
        span = pl.ds(pl.multiple_of(at, 128), count)
        target[:, span] = dot_nt(normed[...], store[span, :]).astype(BF)

    def conv_chunk(q):
        arrived(conv_copies(q))
        project(w_conv, conv_in_ref, q * CHUNK, CHUNK)

    each(chunks, conv_chunk)
    arrived(tail_copies())
    project(w_conv, conv_in_ref, width, TAIL_PAD)
    grad_copies = row_copies(1, block(grads, mine), grads)
    grad_copies[0].start()
    grad_copies[1].start()
    conv_store = pltpu.make_async_copy(w_conv, w_conv_out_ref, local_sem.at[2])
    conv_store.start()
    each(chunks, lambda q: pass_on(gate_copies(q)))

    def gate_chunk(q):
        arrived(gate_copies(q))
        project(w_gate, gate_ref, q * CHUNK, CHUNK)

    each(chunks, gate_chunk)
    gate_store = pltpu.make_async_copy(w_gate, w_gate_out_ref, local_sem.at[3])
    gate_store.start()
    grad_copies[0].wait_recv()
    grad_copies[2].start()
    grad_copies[1].wait_recv()
    grad_copies[2].wait_recv()
    branch_grad_ref[...] = grads[...]

    def drain(copies):
        for i in range(4):
            copies[i]().wait_send()

    each(chunks, lambda q: drain(conv_copies(q)))
    drain(tail_copies())
    each(chunks, lambda q: drain(gate_copies(q)))
    for copies in (x_copies, grad_copies):
        for copy in copies:
            copy.wait_send()
    normed_store.wait()
    conv_store.wait()
    gate_store.wait()


def run_start(lengths, order, x_in, cotangent, valid, gain, w_columns, shards):
    rows = x_in.shape[0]
    length, width = rows * shards, DI // shards
    chunks = width // CHUNK
    dma = pltpu.SemaphoreType.DMA
    anywhere = pl.BlockSpec(memory_space=pl.ANY)
    scalars = pl.BlockSpec(memory_space=pltpu.SMEM)
    vector = pl.BlockSpec(memory_space=pltpu.VMEM)
    shape = jax.ShapeDtypeStruct
    return pl.pallas_call(
        start_kernel,
        out_shape=(
            shape((length, D), BF),
            shape((length, width + TAIL_PAD), BF),
            shape((length, width), BF),
            shape((width, D), BF),
            shape((width + TAIL_PAD, D), BF),
            shape((length, D), BF),
            shape((length, length), BF),
            shape((length, 128), jnp.int32),
            shape((rows, D), BF),
        ),
        in_specs=[scalars, scalars, anywhere, vector, vector, vector, anywhere],
        out_specs=(anywhere, vector, vector, anywhere, anywhere, vector, vector, vector, vector),
        scratch_shapes=[
            pltpu.VMEM((length, D), BF),
            pltpu.VMEM((length, D), BF),
            pltpu.VMEM((width, D), BF),
            pltpu.VMEM((width + TAIL_PAD, D), BF),
            pltpu.VMEM((length, D), BF),
            dma((4,)),
            dma((2, 3)),
            dma((2, 3)),
            dma((4, 2 * chunks + 1)),
            dma((4, 2 * chunks + 1)),
            dma((2 * chunks + 1,)),
        ],
        compiler_params=pltpu.CompilerParams(
            vmem_limit_bytes=VMEM_BYTES, collective_id=1, has_side_effects=True
        ),
        cost_estimate=pl.CostEstimate(
            flops=2 * length * D * (2 * width + TAIL_PAD), bytes_accessed=48 << 20, transcendentals=0
        ),
        name="project",
    )(lengths, order, x_in, cotangent, valid, gain, w_columns)


def conv_pre(x, conv_w, conv_b, place):
    pre = conv_b + conv_w[KW - 1 : KW] * x
    for back in range(1, KW):
        moved = pltpu.roll(x, back, 0)
        pre = pre + jnp.where(place >= back, conv_w[KW - 1 - back : KW - back] * moved, 0.0)
    return pre


def conv_lanes(chunk, width, mine):
    if 128 * chunk < width:
        return pl.ds(pl.multiple_of(mine * width + 128 * chunk, 128), 128)
    return pl.ds(DI + 128 * chunk - width, 128)


def block_terms(place):
    local = lax.broadcasted_iota(jnp.int32, (SPAN, 128), 0)
    across = lax.broadcasted_iota(jnp.int32, (SPAN, 128), 1)
    begins = local - place
    causal = (across <= local) & (across >= begins)
    reach_end = local >= begins[SPAN - 1 : SPAN, :]
    entered = place >= local + 1
    carries = place[SPAN - 1 : SPAN, :] >= SPAN
    return causal, reach_end, entered, carries


def pair_terms(pair, run, run_t, step, causal, reach_end, entered, carries):
    left = lax.broadcasted_iota(jnp.int32, (SPAN, 128), 1) < P_SIZE
    runs = [spread(run[:, 2 * pair + i : 2 * pair + i + 1]) for i in range(2)]
    decays = []
    for i in range(2):
        gap = runs[i] - run_t[2 * pair + i : 2 * pair + i + 1, :]
        decays.append(jnp.exp(jnp.where(causal, gap, -jnp.inf)))
    both = jnp.where(left, runs[0], runs[1])
    end = both[SPAN - 1 : SPAN, :]
    entering = jnp.where(entered, jnp.exp(both), 0.0)
    tail = jnp.where(reach_end, jnp.exp(jnp.where(reach_end, end - both, 0.0)), 0.0)
    carried = jnp.where(carries, jnp.exp(end), 0.0)
    size = jnp.where(
        left,
        spread(step[:, 2 * pair : 2 * pair + 1]),
        spread(step[:, 2 * pair + 1 : 2 * pair + 2]),
    )
    return left, decays, entering, tail, carried, size


def stacked(value, left):
    zero = jnp.zeros_like(value)
    return jnp.concatenate([jnp.where(left, value, zero), jnp.where(left, zero, value)], axis=0)


def own_lanes(row, mine, heads):
    return pltpu.roll(row, lax.rem(128 - mine * heads, 128), 1)


def skip_lanes(row, pair):
    left = lax.broadcasted_iota(jnp.int32, (1, 128), 1) < P_SIZE
    return jnp.where(
        left,
        spread(row[:, 2 * pair : 2 * pair + 1]),
        spread(row[:, 2 * pair + 1 : 2 * pair + 2]),
    )


def step_and_run(conv_in_ref, heads_ref, run_ref, step_ref, width, mine):
    length = run_ref.shape[0]
    heads = width // P_SIZE
    lower = (
        lax.broadcasted_iota(jnp.int32, (SPAN, SPAN), 0)
        >= lax.broadcasted_iota(jnp.int32, (SPAN, SPAN), 1)
    ).astype(F32)
    bias = heads_ref[0:1, :]
    rate = jnp.exp(own_lanes(heads_ref[...], mine, heads)[1:2, :])

    def block(b, unused):
        rows = pl.ds(pl.multiple_of(b * SPAN, SPAN), SPAN)
        raw = conv_in_ref[rows, width + 2 * N : width + 2 * N + 128].astype(F32)
        step = own_lanes(jax.nn.softplus(raw + bias), mine, heads)
        step_ref[rows, :] = step
        run_ref[rows, :] = jnp.dot(
            lower, -step * rate, precision=lax.Precision.HIGHEST, preferred_element_type=F32
        )
        return unused

    lax.fori_loop(0, length // SPAN, block, 0)


def forward_kernel(
    conv_in_ref,
    gate_ref,
    branch_grad_ref,
    w_out_ref,
    place_ref,
    conv_w_ref,
    conv_b_ref,
    heads_ref,
    gain_ref,
    mixed_ref,
    starts_ref,
    normed_out_ref,
    grad_mixed_ref,
    grad_gate_ref,
    grad_gain_ref,
    act_ref,
    step_ref,
    run_ref,
    state_ref,
    back_ref,
    sums,
    send_sem,
    recv_sem,
):
    length, width = mixed_ref.shape
    mine, rep, shards = lax.axis_index("shard"), lax.axis_index("rep"), lax.axis_size("shard")
    heads = width // P_SIZE
    peers = [(rep, lax.rem(mine + step, shards)) for step in range(1, shards)]
    barrier = pltpu.get_barrier_semaphore()
    for peer in peers:
        pl.semaphore_signal(barrier, inc=1, device_id=peer, device_id_type=MESH)
    for c in range((width + 2 * N) // 128):
        lanes = slice(128 * c, 128 * c + 128)
        there = conv_lanes(c, width, mine)
        pre = conv_pre(
            conv_in_ref[:, lanes].astype(F32),
            conv_w_ref[:, there],
            conv_b_ref[:, there],
            place_ref[...],
        )
        act_ref[:, lanes] = (pre * sigmoid(pre)).astype(BF)
    step_and_run(conv_in_ref, heads_ref, run_ref, step_ref, width, mine)
    state_ref[...] = jnp.zeros_like(state_ref)
    skips = own_lanes(heads_ref[...], mine, heads)[2:3, :]

    def block(b, unused):
        row = pl.multiple_of(b * SPAN, SPAN)
        rows = pl.ds(row, SPAN)
        starts_ref[pl.ds(pl.multiple_of(b * N, N), N), :] = state_ref[...]
        run = run_ref[rows, :]
        run_t = run.T
        step = step_ref[rows, :]
        masks = block_terms(place_ref[rows, :])
        in_map = act_ref[rows, width : width + N]
        out_map = act_ref[rows, width + N : width + 2 * N]
        products = dot_nt(out_map, in_map)
        in_map_t = in_map.T
        for pair in range(width // 128):
            lanes = slice(128 * pair, 128 * pair + 128)
            left, decays, entering, tail, carried, size = pair_terms(
                pair, run, run_t, step, *masks
            )
            values = act_ref[rows, lanes].astype(F32)
            scaled = values * size
            weights = jnp.concatenate([(d * products).astype(BF) for d in decays], axis=1)
            out = dot_nn(weights, stacked(scaled.astype(BF), left))
            state = state_ref[:, lanes]
            high, low = halves(state)
            out += entering * (dot_nn(out_map, high) + dot_nn(out_map, low))
            mixed_ref[rows, lanes] = out + skip_lanes(skips, pair) * values
            high, low = halves(tail * scaled)
            fresh = dot_nn(in_map_t, high) + dot_nn(in_map_t, low)
            state_ref[:, lanes] = carried * state + fresh
        return unused

    lax.fori_loop(0, length // SPAN, block, 0)

    lane = lax.broadcasted_iota(jnp.int32, (SPAN, 128), 1)

    def gated(rows, c):
        lanes = slice(128 * c, 128 * c + 128)
        gate = gate_ref[rows, lanes].astype(F32)
        opened = sigmoid(gate)
        mixed = mixed_ref[rows, lanes]
        back = back_ref[rows, lanes]
        gain = gain_ref[:, pl.ds(pl.multiple_of(mine * width + 128 * c, 128), 128)]
        return gate, opened, mixed, back, gain, mixed * (gate * opened), back * gain

    def measure(b, unused):
        rows = pl.ds(pl.multiple_of(b * SPAN, SPAN), SPAN)
        back_ref[rows, :] = dot_nt(branch_grad_ref[rows, :], w_out_ref[...])
        squares = jnp.zeros((SPAN, 128), F32)
        crosses = jnp.zeros((SPAN, 128), F32)
        for c in range(width // 128):
            product, weighted = gated(rows, c)[5:]
            squares += product * product
            crosses += weighted * product
        squares = jnp.sum(squares, axis=1, keepdims=True)
        crosses = jnp.sum(crosses, axis=1, keepdims=True)
        both = jnp.where(lane == 0, spread(squares), jnp.where(lane == 1, spread(crosses), 0.0))
        sums[mine, :, rows] = both.T[0:8, :]
        return unused

    lax.fori_loop(0, length // SPAN, measure, 0)

    pl.semaphore_wait(barrier, shards - 1)
    copies = [
        remote(sums.at[mine], sums.at[mine], send_sem.at[i], recv_sem.at[i], peer)
        for i, peer in enumerate(peers)
    ]
    for copy in copies:
        copy.start()
    for copy in copies:
        copy.wait_recv()
    grad_gain_ref[...] = jnp.zeros_like(grad_gain_ref)

    def finish(b, unused):
        rows = pl.ds(pl.multiple_of(b * SPAN, SPAN), SPAN)
        both = sums[0, :, rows]
        for shard in range(1, shards):
            both = both + sums[shard, :, rows]
        both = jnp.concatenate([both, jnp.zeros((SPAN - 8, SPAN), F32)], axis=0).T / DI
        inverse = lax.rsqrt(both[:, 0:1] + EPSILON)
        pull = spread(inverse * inverse * inverse * both[:, 1:2])
        inverse = spread(inverse)
        for c in range(width // 128):
            lanes = slice(128 * c, 128 * c + 128)
            gate, opened, mixed, back, gain, product, weighted = gated(rows, c)
            normalized = product * inverse
            normed_out_ref[rows, lanes] = (normalized * gain).astype(BF)
            grad_product = inverse * weighted - product * pull
            grad_gain_ref[:, lanes] += jnp.sum(back * normalized, axis=0, keepdims=True)
            grad_mixed_ref[rows, lanes] = grad_product * (gate * opened)
            grad_gate_ref[rows, lanes] = (
                grad_product * mixed * (opened * (1.0 + gate * (1.0 - opened)))
            ).astype(BF)
        return unused

    lax.fori_loop(0, length // SPAN, finish, 0)
    for copy in copies:
        copy.wait_send()


def backward_kernel(
    conv_in_ref,
    place_ref,
    conv_w_ref,
    conv_b_ref,
    heads_ref,
    mixed_ref,
    starts_ref,
    grad_ref,
    grad_values_ref,
    grad_tail_ref,
    grad_conv_w_ref,
    grad_conv_b_ref,
    grad_head_ref,
    act_ref,
    pre_ref,
    step_ref,
    run_ref,
    state_ref,
    grad_act_ref,
    joined_ref,
    join_ref,
):
    length, width = mixed_ref.shape
    mine = lax.axis_index("shard")
    heads = width // P_SIZE
    blocks = length // SPAN
    for c in range((width + 2 * N) // 128):
        lanes = slice(128 * c, 128 * c + 128)
        there = conv_lanes(c, width, mine)
        pre = conv_pre(
            conv_in_ref[:, lanes].astype(F32),
            conv_w_ref[:, there],
            conv_b_ref[:, there],
            place_ref[...],
        )
        pre_ref[:, lanes] = pre
        act_ref[:, lanes] = (pre * sigmoid(pre)).astype(BF)
    step_and_run(conv_in_ref, heads_ref, run_ref, step_ref, width, mine)
    state_ref[...] = jnp.zeros_like(state_ref)
    grad_head_ref[...] = jnp.zeros_like(grad_head_ref)
    skips = own_lanes(heads_ref[...], mine, heads)[2:3, :]
    upper = (
        lax.broadcasted_iota(jnp.int32, (SPAN, SPAN), 0)
        <= lax.broadcasted_iota(jnp.int32, (SPAN, SPAN), 1)
    ).astype(F32)
    last_row = lax.broadcasted_iota(jnp.int32, (SPAN, 128), 0) == SPAN - 1
    join_ref[...] = (
        lax.broadcasted_iota(jnp.int32, (width, 128), 0) // P_SIZE + mine * heads
        == lax.broadcasted_iota(jnp.int32, (width, 128), 1)
    ).astype(F32).astype(BF)

    def block(count, unused):
        b = blocks - 1 - count
        row = pl.multiple_of(b * SPAN, SPAN)
        rows = pl.ds(row, SPAN)
        start_rows = pl.ds(pl.multiple_of(b * N, N), N)
        run = run_ref[rows, :]
        run_t = run.T
        step = step_ref[rows, :]
        masks = block_terms(place_ref[rows, :])
        in_map = act_ref[rows, width : width + N]
        out_map = act_ref[rows, width + N : width + 2 * N]
        out_map_t = out_map.T
        products = dot_nt(out_map, in_map)
        grad_products = jnp.zeros((SPAN, SPAN), F32)
        grad_out_map = jnp.zeros((SPAN, N), F32)
        grad_in_map = jnp.zeros((SPAN, N), F32)
        for pair in range(width // 128):
            lanes = slice(128 * pair, 128 * pair + 128)
            left, decays, entering, tail, carried, size = pair_terms(
                pair, run, run_t, step, *masks
            )
            values = act_ref[rows, lanes].astype(F32)
            grad = grad_ref[rows, lanes]
            start = starts_ref[start_rows, lanes]
            later = state_ref[:, lanes]
            scaled = values * size
            scaled_low = scaled.astype(BF)
            grad_low = grad.astype(BF)
            weights = jnp.concatenate([(d * products).astype(BF) for d in decays], axis=0)
            grad_scaled = dot_tn(weights, stacked(grad_low, left))
            grad_pairs = dot_nt(grad_low, stacked(scaled_low, left))
            grad_products += (
                grad_pairs[:, :SPAN] * decays[0] + grad_pairs[:, SPAN:] * decays[1]
            )
            later_high, later_low = halves(later)
            from_later = tail * (dot_nn(in_map, later_high) + dot_nn(in_map, later_low))
            grad_scaled += from_later
            entering_high, entering_low = halves(entering * grad)
            grad_out_map += dot_nt(entering_high, start.astype(BF))
            grad_in_map += dot_nt((tail * scaled).astype(BF), later_high)
            ending = jnp.sum(scaled * from_later, axis=0, keepdims=True) + carried * jnp.sum(
                start * later, axis=0, keepdims=True
            )
            state_ref[:, lanes] = (
                carried * later + dot_nn(out_map_t, entering_high) + dot_nn(out_map_t, entering_low)
            )
            skip = skip_lanes(skips, pair)
            inner = mixed_ref[rows, lanes] - skip * values
            joined_ref[0:SPAN, lanes] = (
                grad_low.astype(F32) * inner
                - scaled_low.astype(F32) * (grad_scaled - from_later)
                - scaled * from_later
                + jnp.where(last_row, ending, 0.0)
            )
            joined_ref[SPAN : 2 * SPAN, lanes] = grad_scaled * values
            joined_ref[2 * SPAN : 2 * SPAN + 16, lanes] = spread_rows(
                jnp.sum(grad * values, axis=0, keepdims=True)
            )
            grad_act_ref[rows, lanes] = grad_scaled * size + skip * grad
        grad_products = grad_products.astype(BF)
        grad_act_ref[rows, width : width + N] = grad_in_map + dot_tn(grad_products, out_map)
        grad_act_ref[rows, width + N : width + 2 * N] = grad_out_map + dot_nn(
            grad_products, in_map
        )
        joined = joined_ref[...]
        first = joined.astype(BF)
        second, third = halves(joined - first.astype(F32))
        join = join_ref[...]
        by_head = dot_nn(first, join) + dot_nn(second, join) + dot_nn(third, join)
        grad_log = jnp.dot(
            upper, by_head[:SPAN], precision=lax.Precision.HIGHEST, preferred_element_type=F32
        )
        rate = jnp.exp(heads_ref[1:2, :])
        raw = conv_in_ref[rows, width + 2 * N : width + 2 * N + 128].astype(F32) + heads_ref[0:1, :]
        grad_dt = (by_head[SPAN : 2 * SPAN] - grad_log * rate) * sigmoid(raw)
        grad_tail_ref[rows, 2 * N : 2 * N + 128] = grad_dt
        grad_head_ref[0:1, :] += jnp.sum(grad_dt, axis=0, keepdims=True)
        grad_head_ref[1:2, :] += jnp.sum(
            -grad_log * jax.nn.softplus(raw) * rate, axis=0, keepdims=True
        )
        grad_head_ref[2:3, :] += by_head[2 * SPAN : 2 * SPAN + 1]
        return unused

    lax.fori_loop(0, blocks, block, 0)

    place = place_ref[...]
    for c in range((width + 2 * N) // 128):
        lanes = slice(128 * c, 128 * c + 128)
        x = conv_in_ref[:, lanes].astype(F32)
        conv_w = conv_w_ref[:, conv_lanes(c, width, mine)]
        pre = pre_ref[:, lanes]
        gain = sigmoid(pre)
        grad_pre = grad_act_ref[:, lanes] * (gain * (1.0 + pre * (1.0 - gain)))
        grad_conv_b_ref[:, lanes] = jnp.sum(grad_pre, axis=0, keepdims=True)
        grad_conv_w_ref[KW - 1 : KW, lanes] = jnp.sum(grad_pre * x, axis=0, keepdims=True)
        grad_x = conv_w[KW - 1 : KW] * grad_pre
        for back in range(1, KW):
            tap = KW - 1 - back
            kept = jnp.where(place >= back, grad_pre, 0.0)
            grad_conv_w_ref[tap : tap + 1, lanes] = jnp.sum(
                kept * pltpu.roll(x, back, 0), axis=0, keepdims=True
            )
            grad_x += conv_w[tap : tap + 1] * pltpu.roll(kept, length - back, 0)
        if c < width // 128:
            grad_values_ref[:, lanes] = grad_x.astype(BF)
        else:
            grad_tail_ref[:, 128 * c - width : 128 * c - width + 128] = grad_x


def run_forward(conv_in, gate, branch_grad, w_out, place, conv_w, conv_b, heads, gain, shards):
    length, width = gate.shape
    blocks = length // SPAN
    shape = jax.ShapeDtypeStruct
    return pl.pallas_call(
        forward_kernel,
        out_shape=(
            shape((length, width), F32),
            shape((blocks * N, width), F32),
            shape((length, width), BF),
            shape((length, width), F32),
            shape((length, width), BF),
            shape((1, width), F32),
        ),
        scratch_shapes=[
            pltpu.VMEM((length, width + 2 * N), BF),
            pltpu.VMEM((length, 128), F32),
            pltpu.VMEM((length, 128), F32),
            pltpu.VMEM((N, width), F32),
            pltpu.VMEM((length, width), F32),
            pltpu.VMEM((shards, 8, length), F32),
            pltpu.SemaphoreType.DMA((shards - 1,)),
            pltpu.SemaphoreType.DMA((shards - 1,)),
        ],
        compiler_params=pltpu.CompilerParams(
            vmem_limit_bytes=VMEM_BYTES, collective_id=2, has_side_effects=True
        ),
        cost_estimate=pl.CostEstimate(
            flops=20 * length * width * 128, bytes_accessed=12 * length * width, transcendentals=0
        ),
        name="mixer_forward",
    )(conv_in, gate, branch_grad, w_out, place, conv_w, conv_b, heads, gain)


def run_backward(conv_in, place, conv_w, conv_b, heads, mixed, starts, grad):
    length, width = mixed.shape
    shape = jax.ShapeDtypeStruct
    return pl.pallas_call(
        backward_kernel,
        out_shape=(
            shape((length, width), BF),
            shape((length, TAIL_PAD), F32),
            shape((KW, width + 2 * N), F32),
            shape((1, width + 2 * N), F32),
            shape((8, 128), F32),
        ),
        scratch_shapes=[
            pltpu.VMEM((length, width + 2 * N), BF),
            pltpu.VMEM((length, width + 2 * N), F32),
            pltpu.VMEM((length, 128), F32),
            pltpu.VMEM((length, 128), F32),
            pltpu.VMEM((N, width), F32),
            pltpu.VMEM((length, width + 2 * N), F32),
            pltpu.VMEM((2 * SPAN + 16, width), F32),
            pltpu.VMEM((width, 128), BF),
        ],
        compiler_params=params(),
        cost_estimate=pl.CostEstimate(
            flops=40 * length * width * 128, bytes_accessed=20 * length * width, transcendentals=0
        ),
        name="mixer_backward",
    )(conv_in, place, conv_w, conv_b, heads, mixed, starts, grad)


def end_kernel(
    gate_ref,
    values_ref,
    tail_ref,
    normed_ref,
    w_gate_hbm,
    w_conv_hbm,
    w_out_hbm,
    normed_out_hbm,
    back_ref,
    branch_grad_hbm,
    x_ref,
    resid_ref,
    valid_ref,
    gain_ref,
    grad_conv_w_ref,
    grad_conv_b_ref,
    grad_head_ref,
    grad_gain_ref,
    parts_ref,
    tails_ref,
    block_out_ref,
    grad_in_ref,
    out_norm_ref,
    out_conv_w_ref,
    out_conv_b_ref,
    out_head_ref,
    out_gain_ref,
    taken,
    group_rows,
    own_columns,
    total,
    low,
    partial,
    pair_in,
    row_in,
    tail_in,
    tail_low,
    tail_sum,
    tail_parts,
    small,
    small_in,
    small_all,
    w_gate_ref,
    w_conv_ref,
    w_out_ref,
    normed_out_ref,
    branch_grad_ref,
    load_sem,
    local_sem,
    group_sem,
    a2a_send,
    a2a_recv,
    swap_send,
    swap_recv,
    line_send,
    line_recv,
    side_send,
    side_recv,
    pair_send,
    pair_recv,
    tail_send,
    tail_recv,
    rep_send,
    rep_recv,
    all_send,
    all_recv,
):
    reps, shards = LINE * PLANE, lax.axis_size("shard")
    mine, rep = lax.axis_index("shard"), lax.axis_index("rep")
    y, c = mine // 2, lax.rem(mine, 2)
    z, x = rep // PLANE, lax.rem(rep, PLANE)
    beside = z * PLANE + (1 - x)
    rows, length = x_ref.shape[0], gate_ref.shape[0]
    width, depth = gate_ref.shape[1], own_columns.shape[1]
    sources = (gate_ref, values_ref)
    sibling, peer = y * 2 + (1 - c), (1 - y) * 2 + c

    def other(step):
        return lax.rem(z + step // PLANE, LINE) * PLANE + lax.rem(x + step % PLANE, PLANE)

    def before(step):
        return lax.rem(z + LINE - step // PLANE, LINE) * PLANE + lax.rem(
            x + PLANE - step % PLANE, PLANE
        )

    def shard_at(step):
        return lax.rem(mine + step, shards)

    def each(count, body):
        def step(i, unused):
            body(i)
            return unused

        lax.fori_loop(0, count, step, 0)

    meet(
        [(other(step), mine) for step in range(1, reps)]
        + [(rep, shard_at(step)) for step in range(1, shards)]
    )

    loads = [
        pltpu.make_async_copy(far_ref, near_ref, load_sem.at[i])
        for i, (far_ref, near_ref) in enumerate(
            [
                (normed_out_hbm, normed_out_ref),
                (w_out_hbm, w_out_ref),
                (w_gate_hbm, w_gate_ref),
                (w_conv_hbm, w_conv_ref),
                (branch_grad_hbm, branch_grad_ref),
            ]
        )
    ]

    def share_copy(part, step):
        to = other(step)
        return remote(
            sources[part].at[:, pl.ds(pl.multiple_of(to * 128, 128), 128)],
            taken.at[part, step],
            a2a_send.at[part, step],
            a2a_recv.at[part, step],
            (to, mine),
        )

    def own_copy(part):
        return pltpu.make_async_copy(
            sources[part].at[:, pl.ds(pl.multiple_of(rep * 128, 128), 128)],
            taken.at[part, 0],
            local_sem.at[part],
        )

    def group_copy(step, slot):
        start = pl.multiple_of(before(step) * length, 128)
        return pltpu.make_async_copy(
            normed_ref.at[pl.ds(start, length)], group_rows.at[slot], group_sem.at[slot]
        )

    own_part = pltpu.make_async_copy(
        normed_ref.at[
            pl.ds(pl.multiple_of(rep * length, 128), length),
            pl.ds(pl.multiple_of(mine * depth, 128), depth),
        ],
        own_columns,
        local_sem.at[4],
    )
    own_part.start()
    group_copy(0, 0).start()
    for part in range(2):
        own_copy(part).start()
        for step in range(1, reps):
            share_copy(part, step).start()

    def row_block(ref, shard):
        return ref.at[pl.ds(pl.multiple_of(shard * rows, rows), rows)]

    def tail_out_copy(step):
        to = shard_at(step)
        return remote(
            row_block(tail_ref, to),
            tail_in.at[step],
            tail_send.at[0, step],
            tail_recv.at[0, step],
            (rep, to),
        )

    def tail_back_copy(step):
        return remote(
            row_block(tail_low, mine),
            row_block(tail_low, mine),
            tail_send.at[1, step],
            tail_recv.at[1, step],
            (rep, shard_at(step)),
        )

    for step in range(1, shards):
        tail_out_copy(step).start()
    for load in loads:
        load.start()

    def pair_copy(kind, side):
        return remote(
            row_block(partial, 2 * side + (1 - c)),
            pair_in.at[kind, side],
            pair_send.at[kind, side],
            pair_recv.at[kind, side],
            (rep, sibling),
        )

    def row_copy(kind):
        return remote(
            pair_in.at[kind, 1 - y],
            row_in.at[kind],
            pair_send.at[kind, 2],
            pair_recv.at[kind, 2],
            (rep, peer),
        )

    def join_pair(kind):
        for side in range(2):
            pair_copy(kind, side).wait_recv()
        for side in range(2):
            span = pl.ds(pl.multiple_of((2 * side + c) * rows, rows), rows)
            pair_in[kind, side] = pair_in[kind, side] + partial[span, :]
        row_copy(kind).start()

    def joined_rows(kind):
        row_copy(kind).wait_recv()
        return pair_in[kind, y] + row_in[kind]

    def branch_rows(i):
        span = pl.ds(pl.multiple_of(i * rows, rows), rows)
        partial[span, :] = dot_nn(normed_out_ref[span, :], w_out_ref[...])

    loads[0].wait()
    loads[1].wait()
    each(shards, branch_rows)
    for side in range(2):
        pair_copy(0, side).start()

    def swap_copy(part, step):
        to = shard_at(step)
        return remote(
            low.at[part, :, pl.ds(pl.multiple_of(to * depth, depth), depth)],
            parts_ref.at[rep, part, mine],
            swap_send.at[part, step],
            swap_recv.at[part, step],
            (rep, to),
        )

    def swap_own(part):
        return pltpu.make_async_copy(
            low.at[part, :, pl.ds(pl.multiple_of(mine * depth, depth), depth)],
            parts_ref.at[rep, part, mine],
            local_sem.at[2 + part],
        )

    def sum_groups(part):
        for step in range(reps):
            slot = step % 2
            last = step == reps - 1
            if not last:
                group_copy(step + 1, 1 - slot).start()
            elif part == 0:
                group_copy(0, 1 - slot).start()
            if step == 0:
                own_copy(part).wait()
            else:
                share_copy(part, step).wait_recv()
            group_copy(step, slot).wait()

            def columns(i, unused, step=step, slot=slot):
                span = pl.ds(pl.multiple_of(i * 512, 512), 512)
                term = dot_tn(taken[part, step], group_rows[slot, :, span])
                if step == 0:
                    total[:, span] = term
                elif step < reps - 1:
                    total[:, span] += term
                else:
                    low[part, :, span] = (total[:, span] + term).astype(BF)
                return unused

            lax.fori_loop(0, D // 512, columns, 0)
        swap_own(part).start()
        for step in range(1, shards):
            swap_copy(part, step).start()

    def line_copy(part, origin, toward, lane):
        block = parts_ref.at[origin * PLANE + x, part]
        return remote(
            block,
            block,
            line_send.at[part, lane, origin],
            line_recv.at[part, origin],
            ((z + toward) * PLANE + x, mine),
        )

    def side_copy(part, origin, from_x):
        block = parts_ref.at[origin * PLANE + from_x, part]
        return remote(
            block, block, side_send.at[part, origin], side_recv.at[part, origin], (beside, mine)
        )

    def spread_own(part):
        swap_own(part).wait()
        for step in range(1, shards):
            swap_copy(part, step).wait_recv()
        side_copy(part, z, x).start()

        @pl.when(z < LINE - 1)
        def _():
            line_copy(part, z, 1, 0).start()

        @pl.when(z > 0)
        def _():
            line_copy(part, z, -1, 1).start()

    def pass_on(part, step):
        @pl.when(z - step >= 0)
        def _():
            origin = z - step
            line_copy(part, origin, 1, 0).wait_recv()

            @pl.when(z < LINE - 1)
            def _():
                line_copy(part, origin, 1, 0).start()

            side_copy(part, origin, x).start()

        @pl.when(z + step < LINE)
        def _():
            origin = z + step
            line_copy(part, origin, -1, 1).wait_recv()

            @pl.when(z > 0)
            def _():
                line_copy(part, origin, -1, 1).start()

            side_copy(part, origin, x).start()

    sum_groups(0)
    join_pair(0)

    for step in range(1, shards):
        tail_out_copy(step).wait_recv()
    span = pl.ds(pl.multiple_of(mine * rows, rows), rows)
    summed_tail = tail_ref[span, :]
    for step in range(1, shards):
        summed_tail = summed_tail + tail_in[step]
    tail_low[span, :] = summed_tail.astype(BF)
    for step in range(1, shards):
        tail_back_copy(step).start()

    spread_own(0)
    sum_groups(1)

    for step in range(1, shards):
        tail_back_copy(step).wait_recv()
    for side in range(2):
        pair_copy(0, side).wait_send()
    heads, share = H // shards, 2 * N // shards
    lane = lax.broadcasted_iota(jnp.int32, (rows, TAIL_PAD), 1)
    owned = ((lane >= mine * share) & (lane < (mine + 1) * share)) | (
        (lane >= 2 * N + mine * heads) & (lane < 2 * N + (mine + 1) * heads)
    )

    def grad_rows(i):
        span = pl.ds(pl.multiple_of(i * rows, rows), rows)
        back = back_ref[span, :]
        tail = dot_nn(back, tail_low[...])
        tail = jnp.where(owned, tail, 0.0).astype(BF)
        partial[span, :] = (
            dot_nn(dot_nn(back, gate_ref[...]).astype(BF), w_gate_ref[...])
            + dot_nn(dot_nn(back, values_ref[...]).astype(BF), w_conv_ref[0:width, :])
            + dot_nn(tail, w_conv_ref[width:, :])
        )

    loads[2].wait()
    loads[3].wait()
    each(shards, grad_rows)
    for side in range(2):
        pair_copy(1, side).start()

    spread_own(1)
    pass_on(0, 1)

    own_part.wait()
    tail_sum[...] = dot_tn(tail_low[...], own_columns[...])
    share_rows = TAIL_PAD // reps

    def tail_rows(ref, owner):
        return ref.at[pl.ds(pl.multiple_of(owner * share_rows, 16), share_rows)]

    def tail_part_copy(step):
        to = other(step)
        return remote(
            tail_rows(tail_sum, to),
            tail_parts.at[step],
            rep_send.at[0, step],
            rep_recv.at[0, step],
            (to, mine),
        )

    def tail_spread_copy(step):
        return remote(
            tail_rows(tails_ref, rep),
            tail_rows(tails_ref, rep),
            rep_send.at[1, step],
            rep_recv.at[1, step],
            (other(step), mine),
        )

    for step in range(1, reps):
        tail_part_copy(step).start()

    branch = joined_rows(0)
    whole = resid_ref[...].astype(F32) + branch
    block_out_ref[...] = whole.astype(BF)
    counts = valid_ref[...].astype(F32)
    square_total = jnp.sum(
        counts * jnp.sum(whole * whole, axis=1, keepdims=True), axis=0, keepdims=True
    )
    square_branch = jnp.sum(
        counts * jnp.sum(branch * branch, axis=1, keepdims=True), axis=0, keepdims=True
    )
    count = jnp.sum(counts, axis=0, keepdims=True)

    pass_on(1, 1)
    join_pair(1)
    pass_on(0, 2)

    for step in range(1, reps):
        tail_part_copy(step).wait_recv()
    span = pl.ds(pl.multiple_of(rep * share_rows, 16), share_rows)
    piece = tail_sum[span, :]
    for step in range(1, reps):
        piece = piece + tail_parts[step]
    tails_ref[span, :] = piece.astype(BF)
    for step in range(1, reps):
        tail_spread_copy(step).start()

    pass_on(1, 2)

    grad_normed = joined_rows(1)
    given = x_ref[...].astype(F32)
    inverse = lax.rsqrt(jnp.mean(given * given, axis=1, keepdims=True) + EPSILON)
    grad_norm_gain = jnp.sum(grad_normed * (given * inverse), axis=0, keepdims=True)
    scaled = grad_normed * gain_ref[...]
    pull = inverse * inverse * inverse * jnp.mean(scaled * given, axis=1, keepdims=True)
    span = pl.ds(pl.multiple_of(mine * rows, rows), rows)
    loads[4].wait()
    kept = dot_nn(back_ref[span, :], branch_grad_ref[...])
    grad_in_ref[...] = (scaled * inverse - given * pull + kept).astype(BF)

    lane = lax.broadcasted_iota(jnp.int32, (1, 128), 1)
    at = 0
    for i in range(D // 128):
        small[at : at + 1, :] = grad_norm_gain[:, 128 * i : 128 * i + 128]
        at += 1
    channels = (width + 2 * N) // 128
    for tap in range(KW):
        for i in range(channels):
            small[at : at + 1, :] = grad_conv_w_ref[tap : tap + 1, 128 * i : 128 * i + 128]
            at += 1
    for i in range(channels):
        small[at : at + 1, :] = grad_conv_b_ref[:, 128 * i : 128 * i + 128]
        at += 1
    for i in range(width // 128):
        small[at : at + 1, :] = grad_gain_ref[:, 128 * i : 128 * i + 128]
        at += 1
    small[at : at + 3, :] = grad_head_ref[0:3, :]
    small[at + 3 : at + 4, :] = jnp.where(
        lane == 0,
        spread(square_total),
        jnp.where(lane == 1, spread(square_branch), jnp.where(lane == 2, spread(count), 0.0)),
    )
    small[at + 4 :, :] = jnp.zeros((small.shape[0] - at - 4, 128), F32)

    def small_rep_copy(step):
        return remote(
            small, small_in.at[rep], rep_send.at[2, step], rep_recv.at[2, step], (other(step), mine)
        )

    def small_rep_arrival(step):
        return remote(
            small,
            small_in.at[before(step)],
            rep_send.at[2, step],
            rep_recv.at[2, step],
            (other(step), mine),
        )

    def small_shard_copy(step):
        return remote(
            small_all.at[mine],
            small_all.at[mine],
            all_send.at[step],
            all_recv.at[step],
            (rep, shard_at(step)),
        )

    for step in range(1, reps):
        small_rep_copy(step).start()
    small_in[rep] = small[...]

    pass_on(0, 3)
    for step in range(1, reps):
        small_rep_arrival(step).wait_recv()
    added = small_in[0]
    for i in range(1, reps):
        added = added + small_in[i]
    small_all[mine] = added
    for step in range(1, shards):
        small_shard_copy(step).start()
    pass_on(1, 3)
    for step in range(1, shards):
        small_shard_copy(step).wait_recv()

    def over_shards(row):
        value = small_all[0, row : row + 1, :]
        for i in range(1, shards):
            value = value + small_all[i, row : row + 1, :]
        return value

    at = 0
    for i in range(D // 128):
        out_norm_ref[:, 128 * i : 128 * i + 128] = over_shards(at)
        at += 1
    for tap in range(KW + 1):
        ref, row = (out_conv_w_ref, tap) if tap < KW else (out_conv_b_ref, 0)
        for i in range(channels):
            if i < width // 128:
                for shard in range(shards):
                    to = shard * width + 128 * i
                    ref[row : row + 1, to : to + 128] = small_all[shard, at : at + 1, :]
            else:
                to = DI + 128 * i - width
                ref[row : row + 1, to : to + 128] = over_shards(at)
            at += 1
    for i in range(width // 128):
        for shard in range(shards):
            to = shard * width + 128 * i
            out_gain_ref[:, to : to + 128] = small_all[shard, at : at + 1, :]
        at += 1
    for i in range(3):
        out_head_ref[i : i + 1, :] = over_shards(at + i)
    stats = over_shards(at + 3)
    per = jnp.maximum(stats[:, 2:3], 1.0) * D
    out_head_ref[3:4, :] = jnp.sqrt(stats / spread(per))
    out_head_ref[4:8, :] = jnp.zeros((4, 128), F32)

    for step in range(1, reps):
        tail_spread_copy(step).wait_recv()
    for part in range(2):
        for origin in range(LINE):
            side_copy(part, origin, 1 - x).wait_recv()
            side_copy(part, origin, x).wait_send()

            @pl.when((origin <= z) & (z < LINE - 1))
            def _(part=part, origin=origin):
                line_copy(part, origin, 1, 0).wait_send()

            @pl.when((origin >= z) & (z > 0))
            def _(part=part, origin=origin):
                line_copy(part, origin, -1, 1).wait_send()

        for step in range(1, shards):
            swap_copy(part, step).wait_send()
        for step in range(1, reps):
            share_copy(part, step).wait_send()
    for side in range(2):
        pair_copy(1, side).wait_send()
    for kind in range(2):
        row_copy(kind).wait_send()
    for step in range(1, shards):
        tail_out_copy(step).wait_send()
        tail_back_copy(step).wait_send()
        small_shard_copy(step).wait_send()
    for step in range(1, reps):
        tail_part_copy(step).wait_send()
        tail_spread_copy(step).wait_send()
        small_rep_copy(step).wait_send()


def run_end(operands, shards):
    gate = operands[0]
    reps = LINE * PLANE
    length, width = gate.shape
    rows, depth = length // shards, D // shards
    dma = pltpu.SemaphoreType.DMA
    vector = pl.BlockSpec(memory_space=pltpu.VMEM)
    anywhere = pl.BlockSpec(memory_space=pl.ANY)
    shape = jax.ShapeDtypeStruct
    channels = width + 2 * N
    small = -(-(D + 5 * channels + width + 4 * 128) // 1024) * 8
    return pl.pallas_call(
        end_kernel,
        out_shape=(
            shape((reps, 2, shards, 128, depth), BF),
            shape((TAIL_PAD, depth), BF),
            shape((rows, D), BF),
            shape((rows, D), BF),
            shape((1, D), F32),
            shape((KW, CONVW), F32),
            shape((1, CONVW), F32),
            shape((8, 128), F32),
            shape((1, DI), F32),
        ),
        in_specs=[vector] * 3 + [anywhere] * 5 + [vector, anywhere] + [vector] * 8,
        out_specs=(anywhere,) + (vector,) * 8,
        scratch_shapes=[
            pltpu.VMEM((2, reps, length, 128), BF),
            pltpu.VMEM((2, length, D), BF),
            pltpu.VMEM((length, depth), BF),
            pltpu.VMEM((128, D), F32),
            pltpu.VMEM((2, 128, D), BF),
            pltpu.VMEM((length, D), F32),
            pltpu.VMEM((2, 2, rows, D), F32),
            pltpu.VMEM((2, rows, D), F32),
            pltpu.VMEM((shards, rows, TAIL_PAD), F32),
            pltpu.VMEM((length, TAIL_PAD), BF),
            pltpu.VMEM((TAIL_PAD, depth), F32),
            pltpu.VMEM((reps, TAIL_PAD // reps, depth), F32),
            pltpu.VMEM((small, 128), F32),
            pltpu.VMEM((reps, small, 128), F32),
            pltpu.VMEM((shards, small, 128), F32),
            pltpu.VMEM((width, D), BF),
            pltpu.VMEM((width + TAIL_PAD, D), BF),
            pltpu.VMEM((width, D), BF),
            pltpu.VMEM((length, width), BF),
            pltpu.VMEM((length, D), BF),
            dma((5,)),
            dma((5,)),
            dma((2,)),
            dma((2, reps)),
            dma((2, reps)),
            dma((2, shards)),
            dma((2, shards)),
            dma((2, 2, LINE)),
            dma((2, LINE)),
            dma((2, LINE)),
            dma((2, LINE)),
            dma((2, 3)),
            dma((2, 3)),
            dma((2, shards)),
            dma((2, shards)),
            dma((3, reps)),
            dma((3, reps)),
            dma((shards,)),
            dma((shards,)),
        ],
        compiler_params=pltpu.CompilerParams(
            vmem_limit_bytes=VMEM_BYTES, collective_id=3, has_side_effects=True
        ),
        cost_estimate=pl.CostEstimate(
            flops=2 * reps * length * D * 256, bytes_accessed=96 << 20, transcendentals=0
        ),
        name="weight_gradient",
    )(*operands)


def assemble_kernel(parts_ref, tail_ref, out_ref):
    step, steps = pl.program_id(0), pl.num_programs(0)
    reps = parts_ref.shape[0]

    @pl.when(step < steps - 1)
    def _():
        for rep in range(reps):
            out_ref[128 * rep : 128 * rep + 128, :] = parts_ref[rep, 0, 0].astype(F32)

    @pl.when(step == steps - 1)
    def _():
        out_ref[0:TAIL, :] = tail_ref[0:TAIL, :].astype(F32)


def run_assemble(parts, tail):
    reps, unused, shards, unused2, depth = parts.shape
    steps = 2 * shards

    def place(i):
        at = jnp.minimum(i, steps - 1)
        return (0, at // shards, lax.rem(at, shards), 0, 0)

    return pl.pallas_call(
        assemble_kernel,
        grid=(steps + 1,),
        out_shape=jax.ShapeDtypeStruct((PROJ, depth), F32),
        in_specs=[
            pl.BlockSpec((reps, 1, 1, 128, depth), place),
            pl.BlockSpec((TAIL_PAD, depth), lambda i: (0, 0)),
        ],
        out_specs=pl.BlockSpec((reps * 128, depth), lambda i: (i, 0)),
        compiler_params=params(),
        name="assemble",
    )(parts, tail)


def exchange(pieces, axis, mine):
    count = lax.axis_size(axis)
    own = pieces(mine)
    gathered = jnp.zeros((count,) + own.shape, own.dtype)
    gathered = lax.dynamic_update_index_in_dim(gathered, own, mine, 0)
    for other in range(1, count):
        arrived = lax.ppermute(
            pieces(mine ^ other), axis, [(i, i ^ other) for i in range(count)]
        )
        gathered = lax.dynamic_update_index_in_dim(gathered, arrived, mine ^ other, 0)
    return gathered


def columns_at(array, start, width):
    return lax.dynamic_slice_in_dim(array, start, width, axis=1)


def plain_device(
    x_in,
    cotangent,
    seq_lengths,
    seq_order,
    valid,
    norm_gain,
    w_in,
    conv_w,
    conv_b,
    head_rows,
    gain_row,
    w_out,
):
    shards, mine = lax.axis_size("shard"), lax.axis_index("shard")
    rows = x_in.shape[0]
    length = rows * shards
    depth = w_in.shape[0]
    heads = H // shards
    width = DI // shards
    share = 2 * N // shards
    w_tail = w_in[:, 2 * DI :]

    def conv_piece(d):
        return jnp.concatenate([columns_at(w_in, DI + d * width, width), w_tail], axis=1)

    x_group = lax.all_gather(x_in, "shard", axis=0, tiled=True)
    w_conv = exchange(conv_piece, "shard", mine).reshape(D, width + TAIL)
    w_gate = exchange(lambda d: columns_at(w_in, d * width, width), "shard", mine).reshape(D, width)
    branch_grad = lax.all_gather(
        jnp.where(valid[:, None] > 0, cotangent, jnp.zeros_like(cotangent)),
        "shard",
        axis=0,
        tiled=True,
    )
    slot_ids = jnp.arange(length, dtype=jnp.int32)
    source, target, position = slot_tables(seq_lengths[0], seq_order[0], slot_ids)
    resid = dot_nn((source[:, None] == slot_ids[None, :]).astype(BF), x_group)
    inverse_rms = lax.rsqrt(jnp.mean(resid * resid, axis=1, keepdims=True) + EPSILON)
    normed = (resid * inverse_rms * norm_gain[None, :]).astype(BF)
    resid_mine = lax.dynamic_slice_in_dim(resid, mine * rows, rows, axis=0)
    gate = dot_nn(normed, w_gate).astype(BF)
    conv_in = jnp.pad(dot_nn(normed, w_conv).astype(BF), ((0, 0), (0, TAIL_PAD - TAIL)))
    place = jnp.broadcast_to(position[:, None], (length, 128))
    mixed, starts, normed_out, grad_mixed, grad_gate, grad_gain = run_forward(
        conv_in, gate, branch_grad, w_out, place, conv_w, conv_b, head_rows, gain_row, shards
    )
    branch = lax.psum_scatter(dot_nn(normed_out, w_out), "shard", scatter_dimension=0, tiled=True)
    total_rows = resid_mine + branch
    weights_valid = valid.astype(F32)
    square_total = jnp.sum(weights_valid * jnp.sum(total_rows * total_rows, axis=1))
    square_branch = jnp.sum(weights_valid * jnp.sum(branch * branch, axis=1))
    grad_w_out = lax.psum(dot_tn(normed_out, branch_grad), "rep")
    grad_values, grad_tail, grad_conv_w, grad_conv_b, grad_head = run_backward(
        conv_in, place, conv_w, conv_b, head_rows, mixed, starts, grad_mixed
    )
    grad_tail = lax.psum(grad_tail, "shard").astype(BF)
    lane = jnp.arange(TAIL, dtype=jnp.int32)
    owned = ((lane >= mine * share) & (lane < (mine + 1) * share)) | (
        (lane >= 2 * N + mine * heads) & (lane < 2 * N + (mine + 1) * heads)
    )
    kept_tail = jnp.where(owned[None, :], grad_tail[:, :TAIL], jnp.zeros((), BF))
    back = (target[:, None] == slot_ids[None, :]).astype(BF)

    def returned(grad):
        return dot_nn(back, grad).astype(BF)

    grad_normed = lax.psum_scatter(
        dot_nt(returned(grad_gate), w_gate)
        + dot_nt(returned(grad_values), w_conv[:, :width])
        + dot_nt(returned(kept_tail), w_conv[:, width:]),
        "shard",
        scatter_dimension=0,
        tiled=True,
    )
    given = x_in.astype(F32)
    given_rms = lax.rsqrt(jnp.mean(given * given, axis=1, keepdims=True) + EPSILON)
    grad_norm_gain = jnp.sum(grad_normed * (given * given_rms), axis=0)
    scaled = grad_normed * norm_gain[None, :]
    grad_resid = scaled * given_rms - given * (
        given_rms**3 * jnp.mean(scaled * given, axis=1, keepdims=True)
    )
    back_mine = lax.dynamic_slice_in_dim(back, mine * rows, rows, axis=0)
    grad_in = (grad_resid + dot_nn(back_mine, branch_grad)).astype(BF)

    def to_owners(columns):
        part = dot_tn(normed, columns).reshape(shards, depth, columns.shape[1])
        swapped = lax.all_to_all(part, "shard", split_axis=0, concat_axis=0, tiled=True)
        summed = lax.psum(swapped, "rep")
        return summed.transpose(1, 0, 2).reshape(depth, shards * columns.shape[1])

    grad_w_tail = lax.psum(
        dot_tn(columns_at(normed, mine * depth, depth), grad_tail[:, :TAIL]), "rep"
    )
    grad_w_in = jnp.concatenate([to_owners(grad_gate), to_owners(grad_values), grad_w_tail], axis=1)

    def placed(part):
        own = lax.dynamic_update_slice_in_dim(
            jnp.zeros((part.shape[0], DI), F32), part[:, :width], mine * width, axis=1
        )
        return jnp.concatenate([own, part[:, width:]], axis=1)

    summed = lax.psum(
        (
            grad_norm_gain,
            placed(grad_conv_w),
            placed(grad_conv_b)[0],
            grad_head,
            placed(grad_gain)[0],
            jnp.stack([square_total, square_branch, jnp.sum(weights_valid)]),
        ),
        ALL,
    )
    roots = jnp.sqrt(summed[5] / (jnp.maximum(summed[5][2], 1.0) * D))
    return (
        total_rows.astype(BF),
        grad_in,
        summed[0],
        grad_w_in,
        summed[1],
        summed[2],
        summed[3][0, :H],
        summed[3][1, :H],
        summed[3][2, :H],
        summed[4],
        grad_w_out,
        roots[0],
        roots[1],
    )


def on_device(
    x_in,
    cotangent,
    seq_lengths,
    seq_order,
    valid,
    norm_gain,
    w_in,
    conv_w,
    conv_b,
    dt_bias,
    a_log,
    d_skip,
    gated_gain,
    w_out,
):
    shards, mine = lax.axis_size("shard"), lax.axis_index("shard")
    reps = lax.axis_size("rep")
    rows = x_in.shape[0]
    length = rows * shards
    depth = w_in.shape[0]
    heads = H // shards
    width = DI // shards

    head_rows = jnp.pad(jnp.stack([dt_bias, a_log, d_skip]), ((0, 5), (0, 128 - H)))
    bias_row, gain_row = conv_b[None, :], gated_gain[None, :]
    spans = reps == LINE * PLANE and shards == 4 and width == reps * 128 and rows == 128
    if not spans:
        return plain_device(
            x_in,
            cotangent,
            seq_lengths,
            seq_order,
            valid,
            norm_gain,
            w_in,
            conv_w,
            bias_row,
            head_rows,
            gain_row,
            w_out,
        )
    norm_row, valid_column = norm_gain[None, :], valid[:, None]
    normed, conv_in, gate, w_gate, w_conv, branch_grad, back, place, resid = run_start(
        seq_lengths, seq_order, x_in, cotangent, valid_column, norm_row, w_in.T, shards
    )
    normed_mine = lax.dynamic_slice_in_dim(normed, mine * rows, rows, axis=0)
    normed_all = lax.all_gather(normed_mine, ALL, axis=0, tiled=True)
    mixed, starts, normed_out, grad_mixed, grad_gate, grad_gain = run_forward(
        conv_in, gate, branch_grad, w_out, place, conv_w, bias_row, head_rows, gain_row, shards
    )
    grad_w_out = lax.psum(dot_tn(normed_out, branch_grad).astype(BF), "rep").astype(F32)
    grad_values, grad_tail, grad_conv_w, grad_conv_b, grad_head = run_backward(
        conv_in, place, conv_w, bias_row, head_rows, mixed, starts, grad_mixed
    )
    operands = (
        grad_gate,
        grad_values,
        grad_tail,
        normed_all,
        w_gate,
        w_conv,
        w_out,
        normed_out,
        back,
        branch_grad,
        x_in,
        resid,
        valid_column,
        norm_row,
        grad_conv_w,
        grad_conv_b,
        grad_head,
        grad_gain,
    )
    parts, tails, block_out, grad_in, out_norm, out_conv_w, out_conv_b, out_head, out_gain = (
        run_end(operands, shards)
    )
    grad_w_in = run_assemble(parts, tails).T
    return (
        block_out,
        grad_in,
        out_norm[0],
        grad_w_in,
        out_conv_w,
        out_conv_b[0],
        out_head[0, :H],
        out_head[1, :H],
        out_head[2, :H],
        out_gain[0],
        grad_w_out,
        out_head[3, 0],
        out_head[3, 1],
    )


def solution(mesh):
    in_specs = (
        P(ALL, None),
        P(ALL, None),
        P("rep", None),
        P("rep", None),
        P(ALL),
        P(),
        P("shard", None),
        P(),
        P(),
        P(),
        P(),
        P(),
        P(),
        P("shard", None),
    )
    out_specs = (
        P(ALL, None),
        P(ALL, None),
        P(),
        P("shard", None),
        P(),
        P(),
        P(),
        P(),
        P(),
        P(),
        P("shard", None),
        P(),
        P(),
    )
    return jax.shard_map(
        on_device, mesh=mesh, in_specs=in_specs, out_specs=out_specs, check_vma=False
    )
```

time: 1050 us -> 563 us (0.54)
  waiting for transfers between devices: 646 us -> 182 us
  Pallas kernels: 37.6 us -> 335 us
  local copies, waits for them, and re-layouts: 116 us -> 10.7 us
  blocking collectives: 78.8 us -> 0 us
  matrix products: 71.8 us -> 5.63 us
  other arithmetic: 65 us -> 9.31 us
  starting transfers between devices: 15.2 us -> 0.08 us
    pallas_call x2 -> x5, Pallas kernels: 37.6 us -> 335 us  [the longest x1 182 us: run_end(): pl.pallas_call(end_kernel, out_shape=(shape((reps, 2, shards, 128, depth)...]
    all_gather x5 -> x0, waiting for transfers between devices: 178 us -> none  [the longest x2 120 us: to_owners(): whole = lax.all_gather(swapped, 'rep')]
    ppermute x6 -> x0, waiting for transfers between devices: 86.6 us -> none  [exchange(): lax.ppermute(pieces(mine ^ other), axis, [(i, i ^ other) for i in range(c...]
    reduce_scatter x2 -> x0, waiting for transfers between devices: 76.8 us -> none  [the longest x1 44.1 us: on_device(): lax.psum_scatter(dot_nt(grad_given, w_own), 'shard', scatter_dimension=0,...]
    all_to_all x2 -> x0, blocking collectives: 71.6 us -> none  [the longest x1 59.5 us: to_owners(): lax.all_to_all(split, 'rep', split_axis=0, concat_axis=0, tiled=True)]
    all_gather x1, waiting for transfers between devices: 55.1 us -> 0.01 us  [on_device(): normed_all = lax.all_gather(normed_mine, ALL, axis=0, tiled=True)]
    dot_general x7 -> x0, matrix products: 43.2 us -> none  [the longest x5 25.2 us: dot_nn(): lax.dot_general(a, b, (((1,), (0,)), ((), ())), preferred_element_type=F32)]
    all_to_all x2 -> x0, waiting for transfers between devices: 35.4 us -> none  [the longest x1 35.4 us: to_owners(): lax.all_to_all(split, 'rep', split_axis=0, concat_axis=0, tiled=True)]
  transfers between devices with their start and end apart: 19 -> 2, of which waited for: 11 -> 1; matrix products, arithmetic and copies ran while one was open for 19% -> 2% of each run, Pallas kernels for 1% -> 5%
where the time goes in v3:
time: 563 us; the launch traced here: 558 us
  Pallas kernels  335 us (60%)
  waiting for transfers between devices  182 us (32%)
  between operations  15.5 us (3%)
  local copies, waits for them, and re-layouts  10.7 us (2%)
  other arithmetic  9.31 us (2%)
  matrix products  5.63 us (1%)
    psum x1, waiting for transfers between devices, on_device(): lax.psum(dot_tn(normed_out, branch_grad).astype(BF), 'rep').astype(F32)  182 us
    pallas_call x1, Pallas kernels, run_end(): pl.pallas_call(end_kernel, out_shape=(shape((reps, 2, shards, 128, depth)...  182 us
    pallas_call x1, Pallas kernels, run_start(): pl.pallas_call(start_kernel, out_shape=(shape((length, D), BF), shape((le...  88 us
    pallas_call x1, Pallas kernels, run_forward(): pl.pallas_call(forward_kernel, out_shape=(shape((length, width), F32), sh...  28.2 us
    pallas_call x1, Pallas kernels, run_backward(): pl.pallas_call(backward_kernel, out_shape=(shape((length, width), BF), sh...  26.3 us
  transfers between devices with their start and end apart: 2, of which 1 were waited for; matrix products, arithmetic and copies ran while one was open for 2% of the time, Pallas kernels for 5%

profile of v3, /device:TPU:0, one launch (start us, length us, event | category | flops | bytes accessed | tf_op | source)
XLA Modules:
  0.0 558.1 jit_solution(8604445611898562581)
XLA Ops:
  8.0 0.0 all-reduce.3.cloned.1.call-start
  8.1 1.3 broadcast_in_dim.14.conv_b_ref
  9.4 1.4 copy.27.valid_ref
  10.8 1.3 select_maximum_fusion.heads_ref
  12.1 88.0 %project.1 = (bf16[512,2048]{1,0:T(8,128)(2,1)}, bf16[512,1408]{1,0:T(8,128)(2,1)}, bf16[512,1024]{1,0:T(8,128)(2,1)}, bf16[1024,2048]{1,0:T(8,128)(2,1)}, bf16[...) custom-call(s32[1,4]{1,0:T(1,128)} %lengths_ref.1, ...), custom_call_target="tpu_custom_call" | custom-call | flops 5100273664 | bytes 50331648 | tf_op jit(solution)/shard_map/project/pallas_call | solution.py:359
  100.1 0.0 copy-start
  100.1 28.2 %mixer_forward.1 = (f32[512,1024]{1,0:T(8,128)}, f32[512,1024]{1,0:T(8,128)}, bf16[512,1024]{1,0:T(8,128)(2,1)}, f32[512,1024]{1,0:T(8,128)}, bf16[512,1024]{1,0:T(8,128)(2,1)}, /*index=5*/f32[1,1024]{1,0:T(1,128)}) custom-call(bf16[512,1408]{1,0:T(8,128)(2,1)} %get-tuple-element.42.conv_in_ref, bf16[512,1024]{1,0:T(8,128)(2,1)} %get-tuple-element.43.gate_ref, ...), custom_call_target="tpu_custom_call" | custom-call | flops 1342177280 | bytes 6291456 | tf_op jit(solution)/shard_map/mixer_forward/pallas_call | solution.py:792
  128.3 0.0 copy-done
  128.3 5.6 %convolution_convert_fusion = bf16[1024,2048]{1,0:T(8,128)(2,1)} fusion(bf16[512,1024]{1,0:T(8,128)(2,1)} %get-tuple-element.55.normed_out_hbm, bf16[512,2048]{1,0:T(8,128)(2,1)S(1)} %copy-done), kind=kOutput, calls=%fused_computation | convolution fusion | flops 2149580800 | bytes 7340032 | tf_op jit(solution)/shard_map/dot_general | solution.py:37
  133.9 0.0 all-reduce.3.cloned.1.call-update
  133.9 0.0 all-gather.2.cloned.1.call-start
  134.0 1.9 constant_dynamic-slice_fusion
  135.9 0.0 all-gather.2.cloned.1.call-update
  135.9 26.3 %mixer_backward.1 = (bf16[512,1024]{1,0:T(8,128)(2,1)}, f32[512,384]{1,0:T(8,128)}, f32[4,1280]{1,0:T(4,128)}, f32[1,1280]{1,0:T(1,128)}, f32[8,128]{1,0:T(8,128)}) custom-call(bf16[512,1408]{1,0:T(8,128)(2,1)} %get-tuple-element.42.conv_in_ref, s32[512,128]{1,0:T(8,128)} %get-tuple-element.45.place_ref, f32[4,4352]{1,0:T(4,128)} %conv_w_ref.3, ...), custom_call_target="tpu_custom_call" | custom-call | flops 2684354560 | bytes 10485760 | tf_op jit(solution)/shard_map/mixer_backward/pallas_call | solution.py:825
  162.1 181.9 %all-reduce.3.cloned.1.call-done = bf16[1024,2048]{1,0:T(8,128)(2,1)} async-done(((bf16[1024,2048]{1,0:T(8,128)(2,1)}), bf16[1024,2048]{1,0:T(8,128)(2,1)}) %all-reduce.3.cloned.1.call-update) | async-done | bytes 4194320 | tf_op jit(solution)/shard_map/psum | solution.py:1727
  344.0 6.7 %convert_element_type.9 = f32[1024,2048]{1,0:T(8,128)} convert(bf16[1024,2048]{1,0:T(8,128)(2,1)} %all-reduce.3.cloned.1.call-done) | non-fusion elementwise | flops 2097152 | bytes 12582912 | tf_op jit(solution)/shard_map/convert_element_type | solution.py:1727
  350.7 0.0 all-gather.2.cloned.1.call-done.normed_ref
  350.7 181.9 %weight_gradient.1 = (bf16[8,2,4,128,512]{4,3,2,1,0:T(8,128)(2,1)}, bf16[384,512]{1,0:T(8,128)(2,1)}, bf16[128,2048]{1,0:T(8,128)(2,1)}, bf16[128,2048]{1,0:T(8,...) custom-call(bf16[512,1024]{1,0:T(8,128)(2,1)} %get-tuple-element.46., ...), custom_call_target="tpu_custom_call" | custom-call | flops 4294967296 | bytes 100663296 | tf_op jit(solution)/shard_map/weight_gradient/pallas_call | solution.py:1426
  532.5 1.3 fusion
  533.9 1.3 slice_bitcast_fusion
  535.2 1.4 reduce
  536.5 0.0 copy-start.2
  536.5 0.0 copy-start.1
  536.5 0.0 copy-start.5
  536.5 0.0 copy-start.3
  536.5 0.0 copy-start.4
  536.6 10.7 %assemble.1 = f32[8512,512]{1,0:T(8,128)} custom-call(bf16[8,2,4,128,512]{4,3,2,1,0:T(8,128)(2,1)} %get-tuple-element.65.parts_ref, bf16[384,512]{1,0:T(8,128)(2,1)} %get-tuple-element.66.tail_ref), custom_call_target="tpu_custom_call" | custom-call | tf_op jit(solution)/shard_map/assemble/pallas_call | solution.py:1514
  547.2 0.0 copy-done.2
  547.2 0.8 copy.35
  548.0 0.0 copy-done.1
  548.0 0.8 copy.36
  548.8 0.0 copy-done.5
  548.8 0.6 copy.37
  549.4 0.0 copy-done.3
  549.4 0.6 copy.38
  550.1 0.0 copy-done.4
  550.1 0.6 copy.39
Async XLA Ops:
  8.0 336.0 %all-reduce.3.cloned.1.call-start = ((), (), s32[]{:S(2)}) async-start(), calls=%async_computation.1 | async-start | bytes 8388608 | tf_op jit(solution)/shard_map/psum | solution.py:1727
  100.1 28.2 %copy-start = (bf16[512,2048]{1,0:T(8,128)(2,1)S(1)}, bf16[512,2048]{1,0:T(8,128)(2,1)}, u32[]{:S(2)}) copy-start(bf16[512,2048]{1,0:T(8,128)(2,1)} %get-tuple-element.44.branch_grad_ref.branch_grad_hbm) | copy-start | bytes 6291460
  133.9 216.8 %all-gather.2.cloned.1.call-start = ((), (), s32[]{:S(2)}) async-start(), calls=%async_computation | async-start | bytes 17301504 | tf_op jit(solution)/shard_map/all_gather | solution.py:1723
  536.5 10.7 %copy-start.2 = (bf16[128,2048]{1,0:T(8,128)(2,1)S(1)}, bf16[128,2048]{1,0:T(8,128)(2,1)}, u32[]{:S(2)}) copy-start(bf16[128,2048]{1,0:T(8,128)(2,1)} %get-tuple-element.89) | copy-start | bytes 1572868
  536.5 11.5 %copy-start.1 = (bf16[128,2048]{1,0:T(8,128)(2,1)S(1)}, bf16[128,2048]{1,0:T(8,128)(2,1)}, u32[]{:S(2)}) copy-start(bf16[128,2048]{1,0:T(8,128)(2,1)} %get-tuple-element.90) | copy-start | bytes 1572868
  536.5 12.3 %copy-start.5 = (f32[1,2048]{1,0:T(1,128)S(1)}, f32[1,2048]{1,0:T(1,128)}, u32[]{:S(2)}) copy-start(f32[1,2048]{1,0:T(1,128)} %get-tuple-element.64) | copy-start | bytes 24580
  536.5 12.9 %copy-start.3 = (f32[4,4352]{1,0:T(4,128)S(1)}, f32[4,4352]{1,0:T(4,128)}, u32[]{:S(2)}) copy-start(f32[4,4352]{1,0:T(4,128)} %get-tuple-element.93) | copy-start | bytes 208900
  536.5 13.5 %copy-start.4 = (f32[1,4096]{1,0:T(1,128)S(1)}, f32[1,4096]{1,0:T(1,128)}, u32[]{:S(2)}) copy-start(f32[1,4096]{1,0:T(1,128)} %get-tuple-element.70) | copy-start | bytes 49156
Sparse Core Ops, SparseCore 0:
  134.0 209.9 all-reduce.2
Sparse Core Ops, SparseCore 1:
  137.8 163.4 all-gather.1

commit v4 on v3

--- a/solution.py
+++ b/solution.py
@@ -103,6 +103,85 @@
     for device in devices:
         pl.semaphore_signal(barrier, inc=1, device_id=device, device_id_type=MESH)
     pl.semaphore_wait(barrier, len(devices))
+
+
+class Line:
+    def __init__(self, store, first, share, send_sem, recv_sem):
+        self.store, self.first, self.share = store, first, share
+        self.send_sem, self.recv_sem = send_sem, recv_sem
+        self.mine, self.rep = lax.axis_index("shard"), lax.axis_index("rep")
+        self.z, self.x = self.rep // PLANE, lax.rem(self.rep, PLANE)
+        self.sibling = self.mine // 2 * 2 + (1 - lax.rem(self.mine, 2))
+
+    def along(self, origin, toward, first=False):
+        block = self.store.at[origin, self.share]
+        lane = (toward + 1) // 2
+        return remote(
+            self.first if first else block,
+            block,
+            self.send_sem.at[lane, origin],
+            self.recv_sem.at[0, origin],
+            ((self.z + toward) * PLANE + self.x, self.mine),
+        )
+
+    def inward(self, origin):
+        block = self.store.at[origin, self.share]
+        return remote(
+            block,
+            block,
+            self.send_sem.at[2, origin],
+            self.recv_sem.at[1, origin],
+            (self.rep, self.sibling),
+        )
+
+    def start(self):
+        for toward in (1, -1):
+            self.guarded(toward, lambda: self.along(self.z, toward, True).start())
+
+    def guarded(self, toward, act):
+        pl.when(self.z < LINE - 1 if toward > 0 else self.z > 0)(act)
+
+    def step(self, distance):
+        for toward in (1, -1):
+            origin = self.z - toward * distance
+
+            @pl.when(origin >= 0 if toward > 0 else origin < LINE)
+            def _():
+                self.along(origin, toward).wait_recv()
+                self.guarded(toward, lambda: self.along(origin, toward).start())
+                self.inward(origin).start()
+
+    def finish(self):
+        for origin in range(LINE):
+
+            @pl.when(origin != self.z)
+            def _():
+                self.inward(origin).wait_recv()
+                self.inward(origin).wait_send()
+
+            for toward in (1, -1):
+                passed = origin <= self.z if toward > 0 else origin >= self.z
+                pl.when(passed)(
+                    lambda: self.guarded(toward, lambda: self.along(origin, toward).wait_send())
+                )
+
+
+def meet_with_line(devices):
+    mine, rep = lax.axis_index("shard"), lax.axis_index("rep")
+    z, x = rep // PLANE, lax.rem(rep, PLANE)
+    barrier = pltpu.get_barrier_semaphore()
+    for device in devices:
+        pl.semaphore_signal(barrier, inc=1, device_id=device, device_id_type=MESH)
+    for toward, there in ((1, z < LINE - 1), (-1, z > 0)):
+
+        @pl.when(there)
+        def _():
+            pl.semaphore_signal(
+                barrier, inc=1, device_id=((z + toward) * PLANE + x, mine), device_id_type=MESH
+            )
+
+    beyond = (z + LINE - 1) // LINE + (2 * (LINE - 1) - z) // LINE
+    pl.semaphore_wait(barrier, len(devices) + beyond)
 
 
 def tables_in_kernel(lengths_ref, order_ref, slots):
@@ -152,6 +231,9 @@
     back_ref,
     place_ref,
     resid_ref,
+    inverse_ref,
+    line_ref,
+    side_ref,
     x_all,
     normed,
     w_gate,
@@ -163,6 +245,10 @@
     w_send,
     w_recv,
     w_local,
+    line_send,
+    line_recv,
+    side_send,
+    side_recv,
 ):
     mine, rep = lax.axis_index("shard"), lax.axis_index("rep")
     y, c = mine // 2, lax.rem(mine, 2)
@@ -173,7 +259,40 @@
     depth, width = w_ref.shape[1], gate_ref.shape[1]
     chunks = width // CHUNK
     tail_half = TAIL // 2
-    meet([(rep, sibling), (rep, peer), (rep, far), (beside, mine)])
+    meet_with_line([(rep, sibling), (rep, peer), (rep, far), (beside, mine)])
+
+    part = pl.ds(pl.multiple_of(y * (D // 2), 128), D // 2)
+    share = pl.ds(pl.multiple_of(c * (length // 2), 16), length // 2)
+    wholes = (x_all, grads)
+
+    lines = [
+        Line(
+            line_ref.at[kind],
+            wholes[kind].at[share, part],
+            share,
+            line_send.at[kind],
+            line_recv.at[kind],
+        )
+        for kind in range(2)
+    ]
+
+    def side_copy(kind):
+        return remote(
+            wholes[kind].at[share, part],
+            side_ref.at[kind, share],
+            side_send.at[kind, 0],
+            side_recv.at[kind, 0],
+            (beside, mine),
+        )
+
+    def side_inward(kind):
+        block = side_ref.at[kind, share]
+        return remote(block, block, side_send.at[kind, 1], side_recv.at[kind, 1], (rep, sibling))
+
+    def line_own(kind):
+        return pltpu.make_async_copy(
+            wholes[kind].at[:, part], line_ref.at[kind, z], local_sem.at[4 + kind]
+        )
 
     def block(ref, shard):
         return ref.at[pl.ds(pl.multiple_of(shard * rows, rows), rows)]
@@ -231,14 +350,20 @@
     def gate_copies(q):
         return weight_copies(w_gate, chunks + 1 + q, 0, width, q * CHUNK, CHUNK // 2)
 
-    def send_out(copies):
-        for i in (0, 1, 3, 4):
-            copies[i]().start()
+    def send_near(copies):
+        copies[3]().start()
+        copies[4]().start()
+
+    def send_far(copies):
+        copies[0]().start()
+        copies[1]().start()
 
     def pass_on(copies):
         copies[0]().wait_recv()
         copies[1]().wait_recv()
         copies[2]().start()
+        copies[0]().wait_send()
+        copies[1]().wait_send()
 
     def arrived(copies):
         copies[2]().wait_recv()
@@ -253,15 +378,21 @@
         lax.fori_loop(0, count, step, 0)
 
     x_copies = row_copies(0, x_ref, x_all)
+    grad_copies = row_copies(1, block(grads, mine), grads)
     own_rows = pltpu.make_async_copy(x_ref, block(x_all, mine), local_sem.at[0])
+    convs = [conv_copies(q) for q in range(chunks)]
+    gates = [gate_copies(q) for q in range(chunks)]
+    tail = tail_copies()
     x_copies[0].start()
     x_copies[1].start()
     own_rows.start()
-    each(chunks, lambda q: send_out(conv_copies(q)))
-    send_out(tail_copies())
+    for copies in convs + [tail] + gates:
+        send_near(copies)
     grads[pl.ds(pl.multiple_of(mine * rows, rows), rows), :] = jnp.where(
         spread(valid_ref[...], D) > 0, cotangent_ref[...].astype(F32), 0.0
     ).astype(BF)
+    grad_copies[0].start()
+    grad_copies[1].start()
     w_conv[width + TAIL :, :] = jnp.zeros((TAIL_PAD - TAIL, D), BF)
 
     def table_block(i):
@@ -276,9 +407,14 @@
     each(length // rows, table_block)
     x_copies[0].wait_recv()
     x_copies[2].start()
+    x_copies[0].wait_send()
+    send_far(convs[0])
     own_rows.wait()
     x_copies[1].wait_recv()
     x_copies[2].wait_recv()
+    line_own(0).start()
+    lines[0].start()
+    side_copy(0).start()
 
     def picked(i):
         slots = lax.broadcasted_iota(jnp.int32, (rows, length), 0) + i * rows
@@ -292,59 +428,99 @@
         inverse = lax.rsqrt(jnp.mean(resid * resid, axis=1, keepdims=True) + EPSILON)
         normed[span, :] = (resid * inverse * gain_ref[...]).astype(BF)
 
-    each(length // rows, norm_block)
+    each(length // rows // 2, norm_block)
+    grad_copies[0].wait_recv()
+    grad_copies[2].start()
+    grad_copies[0].wait_send()
+    send_far(convs[1])
+    each(length // rows // 2, lambda i: norm_block(i + length // rows // 2))
+    lines[0].step(1)
+    grad_copies[1].wait_recv()
+    grad_copies[2].wait_recv()
+    line_own(1).start()
+    lines[1].start()
+    side_copy(1).start()
+    pass_on(convs[0])
+    send_far(convs[2])
     resid_ref[...] = picked(mine).astype(BF)
     normed_store = pltpu.make_async_copy(normed, normed_out_ref, local_sem.at[1])
     normed_store.start()
 
-    each(chunks, lambda q: pass_on(conv_copies(q)))
-    pass_on(tail_copies())
-    each(chunks, lambda q: send_out(gate_copies(q)))
+    def inverse_block(i):
+        span = pl.ds(pl.multiple_of(i * rows, rows), rows)
+        given = x_all[span, :].astype(F32)
+        inverse_ref[span, :] = spread(
+            lax.rsqrt(jnp.mean(given * given, axis=1, keepdims=True) + EPSILON)
+        )
 
     def project(store, target, at, count):
-        span = pl.ds(pl.multiple_of(at, 128), count)
+        span = pl.ds(at, count)
         target[:, span] = dot_nt(normed[...], store[span, :]).astype(BF)
 
     def conv_chunk(q):
-        arrived(conv_copies(q))
+        arrived(convs[q])
         project(w_conv, conv_in_ref, q * CHUNK, CHUNK)
 
-    each(chunks, conv_chunk)
-    arrived(tail_copies())
+    def gate_chunk(q):
+        arrived(gates[q])
+        project(w_gate, gate_ref, q * CHUNK, CHUNK)
+
+    each(length // rows, inverse_block)
+    pass_on(convs[1])
+    send_far(convs[3])
+    lines[0].step(2)
+    conv_chunk(0)
+    pass_on(convs[2])
+    send_far(tail)
+    lines[1].step(1)
+    conv_chunk(1)
+    pass_on(convs[3])
+    send_far(gates[0])
+    lines[0].step(3)
+    conv_chunk(2)
+    pass_on(tail)
+    send_far(gates[1])
+    lines[1].step(2)
+    conv_chunk(3)
+    pass_on(gates[0])
+    send_far(gates[2])
+    arrived(tail)
     project(w_conv, conv_in_ref, width, TAIL_PAD)
-    grad_copies = row_copies(1, block(grads, mine), grads)
-    grad_copies[0].start()
-    grad_copies[1].start()
     conv_store = pltpu.make_async_copy(w_conv, w_conv_out_ref, local_sem.at[2])
     conv_store.start()
-    each(chunks, lambda q: pass_on(gate_copies(q)))
-
-    def gate_chunk(q):
-        arrived(gate_copies(q))
-        project(w_gate, gate_ref, q * CHUNK, CHUNK)
-
-    each(chunks, gate_chunk)
+    pass_on(gates[1])
+    send_far(gates[3])
+    lines[1].step(3)
+    gate_chunk(0)
+    branch_grad_ref[...] = grads[...]
+    pass_on(gates[2])
+    gate_chunk(1)
+    side_copy(0).wait_recv()
+    side_inward(0).start()
+    pass_on(gates[3])
+    gate_chunk(2)
+    side_copy(1).wait_recv()
+    side_inward(1).start()
+    gate_chunk(3)
     gate_store = pltpu.make_async_copy(w_gate, w_gate_out_ref, local_sem.at[3])
     gate_store.start()
-    grad_copies[0].wait_recv()
-    grad_copies[2].start()
-    grad_copies[1].wait_recv()
-    grad_copies[2].wait_recv()
-    branch_grad_ref[...] = grads[...]
-
-    def drain(copies):
-        for i in range(4):
-            copies[i]().wait_send()
-
-    each(chunks, lambda q: drain(conv_copies(q)))
-    drain(tail_copies())
-    each(chunks, lambda q: drain(gate_copies(q)))
-    for copies in (x_copies, grad_copies):
-        for copy in copies:
-            copy.wait_send()
+
+    for copies in convs + [tail] + gates:
+        copies[2]().wait_send()
+        copies[3]().wait_send()
+    x_copies[1].wait_send()
+    x_copies[2].wait_send()
+    grad_copies[1].wait_send()
+    grad_copies[2].wait_send()
     normed_store.wait()
     conv_store.wait()
     gate_store.wait()
+    for kind in range(2):
+        line_own(kind).wait()
+        lines[kind].finish()
+        side_copy(kind).wait_send()
+        side_inward(kind).wait_recv()
+        side_inward(kind).wait_send()
 
 
 def run_start(lengths, order, x_in, cotangent, valid, gain, w_columns, shards):
@@ -368,21 +544,28 @@
             shape((length, length), BF),
             shape((length, 128), jnp.int32),
             shape((rows, D), BF),
+            shape((length, 128), F32),
+            shape((2, LINE, length, D // 2), BF),
+            shape((2, length, D // 2), BF),
         ),
         in_specs=[scalars, scalars, anywhere, vector, vector, vector, anywhere],
-        out_specs=(anywhere, vector, vector, anywhere, anywhere, vector, vector, vector, vector),
+        out_specs=(anywhere, vector, vector, anywhere, anywhere) + (vector,) * 5 + (anywhere,) * 2,
         scratch_shapes=[
             pltpu.VMEM((length, D), BF),
             pltpu.VMEM((length, D), BF),
             pltpu.VMEM((width, D), BF),
             pltpu.VMEM((width + TAIL_PAD, D), BF),
             pltpu.VMEM((length, D), BF),
-            dma((4,)),
+            dma((6,)),
             dma((2, 3)),
             dma((2, 3)),
             dma((4, 2 * chunks + 1)),
             dma((4, 2 * chunks + 1)),
             dma((2 * chunks + 1,)),
+            dma((2, 3, LINE)),
+            dma((2, 2, LINE)),
+            dma((2, 2)),
+            dma((2, 2)),
         ],
         compiler_params=pltpu.CompilerParams(
             vmem_limit_bytes=VMEM_BYTES, collective_id=1, has_side_effects=True
@@ -480,38 +663,100 @@
     lax.fori_loop(0, length // SPAN, block, 0)
 
 
-def forward_kernel(
-    conv_in_ref,
-    gate_ref,
-    branch_grad_ref,
-    w_out_ref,
-    place_ref,
-    conv_w_ref,
-    conv_b_ref,
-    heads_ref,
-    gain_ref,
-    mixed_ref,
-    starts_ref,
-    normed_out_ref,
-    grad_mixed_ref,
-    grad_gate_ref,
-    grad_gain_ref,
-    act_ref,
-    step_ref,
-    run_ref,
-    state_ref,
-    back_ref,
-    sums,
-    send_sem,
-    recv_sem,
-):
+def side_copies(line_ref, side_ref, blocks, send_sem, recv_sem):
+    mine, rep = lax.axis_index("shard"), lax.axis_index("rep")
+    y, c = mine // 2, lax.rem(mine, 2)
+    z, x = rep // PLANE, lax.rem(rep, PLANE)
+    length = side_ref.shape[1]
+    share = pl.ds(pl.multiple_of(c * (length // 2), 16), length // 2)
+    across = [
+        remote(
+            line_ref.at[kind, lax.rem(z + ahead, LINE), share],
+            side_ref.at[i, share],
+            send_sem.at[0, i],
+            recv_sem.at[0, i],
+            (z * PLANE + (1 - x), mine),
+        )
+        for i, (kind, ahead) in enumerate(blocks)
+    ]
+    inward = [
+        remote(
+            side_ref.at[i, share],
+            side_ref.at[i, share],
+            send_sem.at[1, i],
+            recv_sem.at[1, i],
+            (rep, y * 2 + (1 - c)),
+        )
+        for i in range(len(blocks))
+    ]
+    return across, inward
+
+
+SIDE_BLOCKS = ((0, 1), (0, 2), (0, 3))
+
+
+def hand_inward(copies):
+    for over, inner in zip(*copies):
+        over.wait_recv()
+        inner.start()
+
+
+def finish_side(copies):
+    for over, inner in zip(*copies):
+        inner.wait_recv()
+        inner.wait_send()
+        over.wait_send()
+
+
+def forward_kernel(spans, *refs):
+    refs = list(refs)
+    if spans:
+        line_ref, beside_ref = refs[9:11]
+        side_ref, grad_side_ref = refs[17:19]
+        side_send, side_recv, line_send, line_recv = refs[27:]
+        refs = refs[:9] + refs[11:17] + refs[19:27]
+    (
+        conv_in_ref,
+        gate_ref,
+        branch_grad_ref,
+        w_out_ref,
+        place_ref,
+        conv_w_ref,
+        conv_b_ref,
+        heads_ref,
+        gain_ref,
+        mixed_ref,
+        starts_ref,
+        normed_out_ref,
+        grad_mixed_ref,
+        grad_gate_ref,
+        grad_gain_ref,
+        act_ref,
+        step_ref,
+        run_ref,
+        state_ref,
+        back_ref,
+        sums,
+        send_sem,
+        recv_sem,
+    ) = refs
     length, width = mixed_ref.shape
     mine, rep, shards = lax.axis_index("shard"), lax.axis_index("rep"), lax.axis_size("shard")
     heads = width // P_SIZE
     peers = [(rep, lax.rem(mine + step, shards)) for step in range(1, shards)]
-    barrier = pltpu.get_barrier_semaphore()
-    for peer in peers:
-        pl.semaphore_signal(barrier, inc=1, device_id=peer, device_id_type=MESH)
+    if spans:
+        z, x = rep // PLANE, lax.rem(rep, PLANE)
+        meet_with_line(peers + [(z * PLANE + (1 - x), mine)])
+        share = pl.ds(
+            pl.multiple_of(lax.rem(mine, 2) * (length // 2), 16), length // 2
+        )
+        line = Line(grad_side_ref, beside_ref.at[1, share], share, line_send, line_recv)
+        line.start()
+        sides = side_copies(line_ref, side_ref, SIDE_BLOCKS, side_send, side_recv)
+        for copy in sides[0]:
+            copy.start()
+    else:
+        meet(peers)
     for c in range((width + 2 * N) // 128):
         lanes = slice(128 * c, 128 * c + 128)
         there = conv_lanes(c, width, mine)
@@ -523,6 +768,8 @@
         )
         act_ref[:, lanes] = (pre * sigmoid(pre)).astype(BF)
     step_and_run(conv_in_ref, heads_ref, run_ref, step_ref, width, mine)
+    if spans:
+        line.step(1)
     state_ref[...] = jnp.zeros_like(state_ref)
     skips = own_lanes(heads_ref[...], mine, heads)[2:3, :]
 
@@ -557,6 +804,8 @@
         return unused
 
     lax.fori_loop(0, length // SPAN, block, 0)
+    if spans:
+        line.step(2)
 
     lane = lax.broadcasted_iota(jnp.int32, (SPAN, 128), 1)
 
@@ -586,7 +835,6 @@
 
     lax.fori_loop(0, length // SPAN, measure, 0)
 
-    pl.semaphore_wait(barrier, shards - 1)
     copies = [
         remote(sums.at[mine], sums.at[mine], send_sem.at[i], recv_sem.at[i], peer)
         for i, peer in enumerate(peers)
@@ -622,35 +870,188 @@
     lax.fori_loop(0, length // SPAN, finish, 0)
     for copy in copies:
         copy.wait_send()
-
-
-def backward_kernel(
-    conv_in_ref,
-    place_ref,
-    conv_w_ref,
-    conv_b_ref,
-    heads_ref,
-    mixed_ref,
-    starts_ref,
-    grad_ref,
-    grad_values_ref,
-    grad_tail_ref,
-    grad_conv_w_ref,
-    grad_conv_b_ref,
-    grad_head_ref,
-    act_ref,
-    pre_ref,
-    step_ref,
-    run_ref,
-    state_ref,
-    grad_act_ref,
-    joined_ref,
-    join_ref,
-):
+    if spans:
+        line.step(3)
+        hand_inward(sides)
+        finish_side(sides)
+        line.finish()
+
+
+def rep_steps():
+    return [(i // PLANE, i % PLANE) for i in range(1, LINE * PLANE)]
+
+
+def rep_at(step):
+    rep = lax.axis_index("rep")
+    z, x = rep // PLANE, lax.rem(rep, PLANE)
+    return lax.rem(z + step[0], LINE) * PLANE + lax.rem(x + step[1], PLANE)
+
+
+def share_copy(source, taken, send_sem, recv_sem, step):
+    to, z = rep_at(step), lax.axis_index("rep") // PLANE
+    return remote(
+        source.at[:, pl.ds(pl.multiple_of(to * 128, 128), 128)],
+        taken.at[z, step[1]],
+        send_sem.at[step[0], step[1]],
+        recv_sem.at[z, step[1]],
+        (to, lax.axis_index("shard")),
+    )
+
+
+def share_own(source, taken, sem):
+    rep = lax.axis_index("rep")
+    return pltpu.make_async_copy(
+        source.at[:, pl.ds(pl.multiple_of(rep * 128, 128), 128)], taken.at[rep // PLANE, 0], sem
+    )
+
+
+def share_arrival(taken, recv_sem, at, side):
+    block, sem = taken.at[at, side], recv_sem.at[at, side]
+    remote(block, block, sem, sem, (rep_at((0, 1)), lax.axis_index("shard"))).wait_recv()
+
+
+def share_wait(source, taken, recv_sem, own, at, side):
+    z = lax.axis_index("rep") // PLANE
+    if side == 1:
+        share_arrival(taken, recv_sem, at, side)
+    else:
+        pl.when(z != at)(lambda: share_arrival(taken, recv_sem, at, side))
+        pl.when(z == at)(lambda: own.wait())
+
+
+def in_given_order(back_ref, inverse_ref, grad_ref, given_ref, scaled_ref):
+    length, width = grad_ref.shape
+
+    def block(i, unused):
+        span = pl.ds(pl.multiple_of(i * SPAN, SPAN), SPAN)
+        moved = dot_nn(back_ref[span, :], grad_ref[...])
+        if given_ref is not None:
+            given_ref[span, :] = moved.astype(BF)
+        for c in range(width // 128):
+            lanes = slice(128 * c, 128 * c + 128)
+            scaled_ref[span, lanes] = (moved[:, lanes] * inverse_ref[span, :]).astype(BF)
+        return unused
+
+    lax.fori_loop(0, length // SPAN, block, 0)
+
+
+class RowSum:
+    def __init__(self, partial, pair_in, row_in, send_sem, recv_sem):
+        self.partial, self.pair_in, self.row_in = partial, pair_in, row_in
+        self.rows = row_in.shape[0]
+        mine, rep = lax.axis_index("shard"), lax.axis_index("rep")
+        self.y, self.core = mine // 2, lax.rem(mine, 2)
+        sibling, peer = self.y * 2 + (1 - self.core), (1 - self.y) * 2 + self.core
+        self.pairs = [
+            remote(
+                partial.at[self.span(2 * side + (1 - self.core))],
+                pair_in.at[side],
+                send_sem.at[side],
+                recv_sem.at[side],
+                (rep, sibling),
+            )
+            for side in range(2)
+        ]
+        self.across = remote(
+            pair_in.at[1 - self.y], row_in, send_sem.at[2], recv_sem.at[2], (rep, peer)
+        )
+
+    def span(self, shard):
+        return pl.ds(pl.multiple_of(shard * self.rows, self.rows), self.rows)
+
+    def fill(self, rows_of):
+        def block(i, unused):
+            span = self.span(i)
+            self.partial[span, :] = rows_of(span)
+            return unused
+
+        lax.fori_loop(0, self.partial.shape[0] // self.rows, block, 0)
+        for copy in self.pairs:
+            copy.start()
+
+    def join(self):
+        for copy in self.pairs:
+            copy.wait_recv()
+        for side in range(2):
+            self.pair_in[side] = (
+                self.pair_in[side] + self.partial[self.span(2 * side + self.core), :]
+            )
+        self.across.start()
+
+    def result(self):
+        self.across.wait_recv()
+        return self.pair_in[self.y] + self.row_in[...]
+
+    def finish(self):
+        for copy in self.pairs + [self.across]:
+            copy.wait_send()
+
+
+def backward_kernel(spans, *refs):
+    refs = list(refs)
+    if spans:
+        grad_gate_ref, back_ref, inverse_ref, normed_out_ref, w_out_ref = refs[8:13]
+        taken_ref, taken_out_ref, gate_peer_ref, gate_given_ref, branch_ref = refs[18:23]
+        extra = refs[31:]
+        refs = refs[:8] + refs[13:18] + refs[23:31]
+        scaled_ref, partial, pair_in, row_in = extra[:4]
+        share_send, share_recv, own_sem, pair_send, pair_recv, peer_send, peer_recv = extra[4:]
+    (
+        conv_in_ref,
+        place_ref,
+        conv_w_ref,
+        conv_b_ref,
+        heads_ref,
+        mixed_ref,
+        starts_ref,
+        grad_ref,
+        grad_values_ref,
+        grad_tail_ref,
+        grad_conv_w_ref,
+        grad_conv_b_ref,
+        grad_head_ref,
+        act_ref,
+        pre_ref,
+        step_ref,
+        run_ref,
+        state_ref,
+        grad_act_ref,
+        joined_ref,
+        join_ref,
+    ) = refs
     length, width = mixed_ref.shape
     mine = lax.axis_index("shard")
     heads = width // P_SIZE
     blocks = length // SPAN
+    if spans:
+        rep = lax.axis_index("rep")
+        y, core = mine // 2, lax.rem(mine, 2)
+        sibling, peer = y * 2 + (1 - core), (1 - y) * 2 + core
+        meet(
+            [(rep_at(step), mine) for step in rep_steps()] + [(rep, sibling), (rep, peer)]
+        )
+        in_given_order(back_ref, inverse_ref, grad_gate_ref, gate_given_ref, scaled_ref)
+        exchanges = ((scaled_ref, taken_ref), (normed_out_ref, taken_out_ref))
+        own_shares = [share_own(*pair, own_sem.at[i]) for i, pair in enumerate(exchanges)]
+
+        def exchange_start(i):
+            own_shares[i].start()
+            for step in rep_steps():
+                share_copy(*exchanges[i], share_send.at[i], share_recv.at[i], step).start()
+
+        def gate_peer_copy(at, side):
+            return remote(
+                taken_ref.at[at, side],
+                gate_peer_ref.at[at, side],
+                peer_send.at[at, side],
+                peer_recv.at[at, side],
+                (rep, peer),
+            )
+
+        exchange_start(0)
+        rows_sum = RowSum(partial, pair_in, row_in, pair_send, pair_recv)
+        rows_sum.fill(lambda span: dot_nn(normed_out_ref[span, :], w_out_ref[...]))
+        exchange_start(1)
     for c in range((width + 2 * N) // 128):
         lanes = slice(128 * c, 128 * c + 128)
         there = conv_lanes(c, width, mine)
@@ -663,6 +1064,8 @@
         pre_ref[:, lanes] = pre
         act_ref[:, lanes] = (pre * sigmoid(pre)).astype(BF)
     step_and_run(conv_in_ref, heads_ref, run_ref, step_ref, width, mine)
+    if spans:
+        rows_sum.join()
     state_ref[...] = jnp.zeros_like(state_ref)
     grad_head_ref[...] = jnp.zeros_like(grad_head_ref)
     skips = own_lanes(heads_ref[...], mine, heads)[2:3, :]
@@ -760,6 +1163,11 @@
         return unused
 
     lax.fori_loop(0, blocks, block, 0)
+    if spans:
+        for at in range(LINE):
+            for side in range(PLANE):
+                share_wait(scaled_ref, taken_ref, share_recv.at[0], own_shares[0], at, side)
+                gate_peer_copy(at, side).start()
 
     place = place_ref[...]
     for c in range((width + 2 * N) // 128):
@@ -783,14 +1191,35 @@
             grad_values_ref[:, lanes] = grad_x.astype(BF)
         else:
             grad_tail_ref[:, 128 * c - width : 128 * c - width + 128] = grad_x
-
-
-def run_forward(conv_in, gate, branch_grad, w_out, place, conv_w, conv_b, heads, gain, shards):
+    if spans:
+        branch_ref[...] = rows_sum.result()
+        for at in range(LINE):
+            for side in range(PLANE):
+                share_wait(
+                    normed_out_ref, taken_out_ref, share_recv.at[1], own_shares[1], at, side
+                )
+        for i, pair in enumerate(exchanges):
+            for step in rep_steps():
+                share_copy(*pair, share_send.at[i], share_recv.at[i], step).wait_send()
+        for at in range(LINE):
+            for side in range(PLANE):
+                gate_peer_copy(at, side).wait()
+        rows_sum.finish()
+
+
+def run_forward(
+    conv_in, gate, branch_grad, w_out, place, conv_w, conv_b, heads, gain, shards, extra=()
+):
     length, width = gate.shape
     blocks = length // SPAN
     shape = jax.ShapeDtypeStruct
+    vector = pl.BlockSpec(memory_space=pltpu.VMEM)
+    anywhere = pl.BlockSpec(memory_space=pl.ANY)
+    dma = pltpu.SemaphoreType.DMA
+    spans = len(extra) > 0
+    side = (len(SIDE_BLOCKS), length, D // 2)
     return pl.pallas_call(
-        forward_kernel,
+        functools.partial(forward_kernel, spans),
         out_shape=(
             shape((length, width), F32),
             shape((blocks * N, width), F32),
@@ -798,7 +1227,10 @@
             shape((length, width), F32),
             shape((length, width), BF),
             shape((1, width), F32),
-        ),
+        )
+        + ((shape(side, BF), shape((LINE, length, D // 2), BF)) if spans else ()),
+        in_specs=[vector] * 9 + [anywhere] * (2 * spans),
+        out_specs=(vector,) * 6 + (anywhere,) * (2 * spans),
         scratch_shapes=[
             pltpu.VMEM((length, width + 2 * N), BF),
             pltpu.VMEM((length, 128), F32),
@@ -806,9 +1238,16 @@
             pltpu.VMEM((N, width), F32),
             pltpu.VMEM((length, width), F32),
             pltpu.VMEM((shards, 8, length), F32),
-            pltpu.SemaphoreType.DMA((shards - 1,)),
-            pltpu.SemaphoreType.DMA((shards - 1,)),
-        ],
+            dma((shards - 1,)),
+            dma((shards - 1,)),
+        ]
+        + [
+            dma((2, len(SIDE_BLOCKS))),
+            dma((2, len(SIDE_BLOCKS))),
+            dma((3, LINE)),
+            dma((2, LINE)),
+        ]
+        * spans,
         compiler_params=pltpu.CompilerParams(
             vmem_limit_bytes=VMEM_BYTES, collective_id=2, has_side_effects=True
         ),
@@ -816,21 +1255,38 @@
             flops=20 * length * width * 128, bytes_accessed=12 * length * width, transcendentals=0
         ),
         name="mixer_forward",
-    )(conv_in, gate, branch_grad, w_out, place, conv_w, conv_b, heads, gain)
-
-
-def run_backward(conv_in, place, conv_w, conv_b, heads, mixed, starts, grad):
+    )(conv_in, gate, branch_grad, w_out, place, conv_w, conv_b, heads, gain, *extra)
+
+
+def run_backward(conv_in, place, conv_w, conv_b, heads, mixed, starts, grad, extra=()):
     length, width = mixed.shape
     shape = jax.ShapeDtypeStruct
+    vector = pl.BlockSpec(memory_space=pltpu.VMEM)
+    anywhere = pl.BlockSpec(memory_space=pl.ANY)
+    dma = pltpu.SemaphoreType.DMA
+    spans = len(extra) > 0
     return pl.pallas_call(
-        backward_kernel,
+        functools.partial(backward_kernel, spans),
         out_shape=(
             shape((length, width), BF),
             shape((length, TAIL_PAD), F32),
             shape((KW, width + 2 * N), F32),
             shape((1, width + 2 * N), F32),
             shape((8, 128), F32),
+        )
+        + (
+            (
+                shape((LINE, PLANE, length, 128), BF),
+                shape((LINE, PLANE, length, 128), BF),
+                shape((LINE, PLANE, length, 128), BF),
+                shape((length, width), BF),
+                shape((length // 4, D), F32),
+            )
+            if spans
+            else ()
         ),
+        in_specs=[vector] * (8 + 5 * spans),
+        out_specs=(vector,) * 5 + ((anywhere,) * 3 + (vector,) * 2) * spans,
         scratch_shapes=[
             pltpu.VMEM((length, width + 2 * N), BF),
             pltpu.VMEM((length, width + 2 * N), F32),
@@ -840,24 +1296,49 @@
             pltpu.VMEM((length, width + 2 * N), F32),
             pltpu.VMEM((2 * SPAN + 16, width), F32),
             pltpu.VMEM((width, 128), BF),
-        ],
-        compiler_params=params(),
+        ]
+        + [
+            pltpu.VMEM((length, width), BF),
+            pltpu.VMEM((length, D), F32),
+            pltpu.VMEM((2, length // 4, D), F32),
+            pltpu.VMEM((length // 4, D), F32),
+            dma((2, LINE, PLANE)),
+            dma((2, LINE, PLANE)),
+            dma((2,)),
+            dma((3,)),
+            dma((3,)),
+            dma((LINE, PLANE)),
+            dma((LINE, PLANE)),
+        ]
+        * spans,
+        compiler_params=pltpu.CompilerParams(
+            vmem_limit_bytes=VMEM_BYTES, collective_id=4, has_side_effects=True
+        )
+        if spans
+        else params(),
         cost_estimate=pl.CostEstimate(
             flops=40 * length * width * 128, bytes_accessed=20 * length * width, transcendentals=0
         ),
         name="mixer_backward",
-    )(conv_in, place, conv_w, conv_b, heads, mixed, starts, grad)
+    )(conv_in, place, conv_w, conv_b, heads, mixed, starts, grad, *extra)
 
 
 def end_kernel(
-    gate_ref,
+    gate_taken_hbm,
+    gate_peer_hbm,
+    out_taken_hbm,
+    gate_given_ref,
     values_ref,
     tail_ref,
     normed_ref,
+    line_ref,
+    beside_ref,
+    side_a_ref,
+    side_b_ref,
+    inverse_ref,
     w_gate_hbm,
     w_conv_hbm,
-    w_out_hbm,
-    normed_out_hbm,
+    branch_ref,
     back_ref,
     branch_grad_hbm,
     x_ref,
@@ -869,6 +1350,7 @@
     grad_head_ref,
     grad_gain_ref,
     parts_ref,
+    w_out_grad_ref,
     tails_ref,
     block_out_ref,
     grad_in_ref,
@@ -878,6 +1360,9 @@
     out_head_ref,
     out_gain_ref,
     taken,
+    taken_peer,
+    values_given_ref,
+    scaled_ref,
     group_rows,
     own_columns,
     total,
@@ -894,14 +1379,14 @@
     small_all,
     w_gate_ref,
     w_conv_ref,
-    w_out_ref,
-    normed_out_ref,
     branch_grad_ref,
     load_sem,
     local_sem,
     group_sem,
-    a2a_send,
-    a2a_recv,
+    share_send,
+    share_recv,
+    peer_send,
+    peer_recv,
     swap_send,
     swap_recv,
     line_send,
@@ -922,9 +1407,9 @@
     y, c = mine // 2, lax.rem(mine, 2)
     z, x = rep // PLANE, lax.rem(rep, PLANE)
     beside = z * PLANE + (1 - x)
-    rows, length = x_ref.shape[0], gate_ref.shape[0]
-    width, depth = gate_ref.shape[1], own_columns.shape[1]
-    sources = (gate_ref, values_ref)
+    rows, length = x_ref.shape[0], values_ref.shape[0]
+    width, depth = values_ref.shape[1], own_columns.shape[1]
+    half = D // 2
     sibling, peer = y * 2 + (1 - c), (1 - y) * 2 + c
 
     def other(step):
@@ -954,8 +1439,6 @@
         pltpu.make_async_copy(far_ref, near_ref, load_sem.at[i])
         for i, (far_ref, near_ref) in enumerate(
             [
-                (normed_out_hbm, normed_out_ref),
-                (w_out_hbm, w_out_ref),
                 (w_gate_hbm, w_gate_ref),
                 (w_conv_hbm, w_conv_ref),
                 (branch_grad_hbm, branch_grad_ref),
@@ -963,43 +1446,47 @@
         )
     ]
 
-    def share_copy(part, step):
-        to = other(step)
+    def place_of(i):
+        return lax.rem(z + i // PLANE, LINE), i % PLANE
+
+    def group_copy(part, i, slot):
+        at, side = place_of(i)
+        kind = part // 2
+        if side == 0:
+            source = line_ref.at[kind, at]
+        elif i // PLANE == 0:
+            source = beside_ref.at[kind]
+        elif kind == 0:
+            source = side_a_ref.at[i // PLANE - 1]
+        else:
+            source = side_b_ref.at[at]
+        return pltpu.make_async_copy(source, group_rows.at[slot], group_sem.at[slot])
+
+    def peer_copy(part, at, side):
         return remote(
-            sources[part].at[:, pl.ds(pl.multiple_of(to * 128, 128), 128)],
-            taken.at[part, step],
-            a2a_send.at[part, step],
-            a2a_recv.at[part, step],
-            (to, mine),
-        )
-
-    def own_copy(part):
-        return pltpu.make_async_copy(
-            sources[part].at[:, pl.ds(pl.multiple_of(rep * 128, 128), 128)],
-            taken.at[part, 0],
-            local_sem.at[part],
-        )
-
-    def group_copy(step, slot):
-        start = pl.multiple_of(before(step) * length, 128)
-        return pltpu.make_async_copy(
-            normed_ref.at[pl.ds(start, length)], group_rows.at[slot], group_sem.at[slot]
+            taken.at[part, at, side],
+            taken_peer.at[part, at, side],
+            peer_send.at[part, at, side],
+            peer_recv.at[part, at, side],
+            (rep, peer),
         )
 
     own_part = pltpu.make_async_copy(
-        normed_ref.at[
-            pl.ds(pl.multiple_of(rep * length, 128), length),
-            pl.ds(pl.multiple_of(mine * depth, 128), depth),
-        ],
+        normed_ref.at[:, pl.ds(pl.multiple_of(mine * depth, depth), depth)],
         own_columns,
         local_sem.at[4],
     )
     own_part.start()
-    group_copy(0, 0).start()
-    for part in range(2):
-        own_copy(part).start()
-        for step in range(1, reps):
-            share_copy(part, step).start()
+    gate_load = pltpu.make_async_copy(gate_taken_hbm, taken.at[0], local_sem.at[0])
+    gate_load.start()
+    peer_load = pltpu.make_async_copy(gate_peer_hbm, taken_peer.at[0], local_sem.at[7])
+    peer_load.start()
+    out_load = pltpu.make_async_copy(out_taken_hbm, taken.at[2], local_sem.at[5])
+    out_load.start()
+    group_copy(0, 0, 0).start()
+    out_load.wait()
+    for i in range(reps):
+        peer_copy(2, *place_of(i)).start()
 
     def row_block(ref, shard):
         return ref.at[pl.ds(pl.multiple_of(shard * rows, rows), rows)]
@@ -1028,95 +1515,71 @@
     for load in loads:
         load.start()
 
-    def pair_copy(kind, side):
+    rows_sum = RowSum(partial, pair_in, row_in, pair_send, pair_recv)
+
+    def swap_copy(part):
+        if part == 2:
+            return remote(
+                low.at[2, pl.ds(pl.multiple_of((1 - y) * 128, 128), 128), :],
+                w_out_grad_ref.at[rep, :, pl.ds(pl.multiple_of(y * half, 128), half)],
+                swap_send.at[2],
+                swap_recv.at[2],
+                (rep, peer),
+            )
         return remote(
-            row_block(partial, 2 * side + (1 - c)),
-            pair_in.at[kind, side],
-            pair_send.at[kind, side],
-            pair_recv.at[kind, side],
+            low.at[part, :, pl.ds(pl.multiple_of((1 - c) * depth, depth), depth)],
+            parts_ref.at[rep, part, c],
+            swap_send.at[part],
+            swap_recv.at[part],
             (rep, sibling),
         )
 
-    def row_copy(kind):
-        return remote(
-            pair_in.at[kind, 1 - y],
-            row_in.at[kind],
-            pair_send.at[kind, 2],
-            pair_recv.at[kind, 2],
-            (rep, peer),
-        )
-
-    def join_pair(kind):
-        for side in range(2):
-            pair_copy(kind, side).wait_recv()
-        for side in range(2):
-            span = pl.ds(pl.multiple_of((2 * side + c) * rows, rows), rows)
-            pair_in[kind, side] = pair_in[kind, side] + partial[span, :]
-        row_copy(kind).start()
-
-    def joined_rows(kind):
-        row_copy(kind).wait_recv()
-        return pair_in[kind, y] + row_in[kind]
-
-    def branch_rows(i):
-        span = pl.ds(pl.multiple_of(i * rows, rows), rows)
-        partial[span, :] = dot_nn(normed_out_ref[span, :], w_out_ref[...])
-
-    loads[0].wait()
-    loads[1].wait()
-    each(shards, branch_rows)
-    for side in range(2):
-        pair_copy(0, side).start()
-
-    def swap_copy(part, step):
-        to = shard_at(step)
-        return remote(
-            low.at[part, :, pl.ds(pl.multiple_of(to * depth, depth), depth)],
-            parts_ref.at[rep, part, mine],
-            swap_send.at[part, step],
-            swap_recv.at[part, step],
-            (rep, to),
-        )
-
     def swap_own(part):
+        if part == 2:
+            return pltpu.make_async_copy(
+                low.at[2, pl.ds(pl.multiple_of(y * 128, 128), 128), :],
+                w_out_grad_ref.at[rep, :, pl.ds(pl.multiple_of(y * half, 128), half)],
+                local_sem.at[6],
+            )
         return pltpu.make_async_copy(
-            low.at[part, :, pl.ds(pl.multiple_of(mine * depth, depth), depth)],
-            parts_ref.at[rep, part, mine],
+            low.at[part, :, pl.ds(pl.multiple_of(c * depth, depth), depth)],
+            parts_ref.at[rep, part, c],
             local_sem.at[2 + part],
         )
 
-    def sum_groups(part):
-        for step in range(reps):
-            slot = step % 2
-            last = step == reps - 1
-            if not last:
-                group_copy(step + 1, 1 - slot).start()
-            elif part == 0:
-                group_copy(0, 1 - slot).start()
-            if step == 0:
-                own_copy(part).wait()
+    def sum_groups(part, then=None):
+        gains = gain_ref[:, pl.ds(pl.multiple_of(y * half, 128), half)] if part < 2 else 1.0
+        for i in range(reps):
+            slot = i % 2
+            at, side = place_of(i)
+            if i < reps - 1:
+                group_copy(part, i + 1, 1 - slot).start()
+            elif then is not None:
+                group_copy(then, 0, 1 - slot).start()
+            if part > 0:
+                peer_copy(part, at, side).wait_recv()
+            elif i == 0:
+                gate_load.wait()
+                peer_load.wait()
+            group_copy(part, i, slot).wait()
+            both = jnp.concatenate([taken[part, at, side], taken_peer[part, at, side]], axis=1)
+            term = dot_tn(both, group_rows[slot])
+            if i == 0:
+                total[...] = term
+            elif i < reps - 1:
+                total[...] += term
             else:
-                share_copy(part, step).wait_recv()
-            group_copy(step, slot).wait()
-
-            def columns(i, unused, step=step, slot=slot):
-                span = pl.ds(pl.multiple_of(i * 512, 512), 512)
-                term = dot_tn(taken[part, step], group_rows[slot, :, span])
-                if step == 0:
-                    total[:, span] = term
-                elif step < reps - 1:
-                    total[:, span] += term
-                else:
-                    low[part, :, span] = (total[:, span] + term).astype(BF)
-                return unused
-
-            lax.fori_loop(0, D // 512, columns, 0)
+                term = ((total[...] + term) * gains).astype(BF)
+                for place, half_rows in ((y, term[:128]), (1 - y, term[128:])):
+                    low[part, pl.ds(pl.multiple_of(place * 128, 128), 128), :] = half_rows
         swap_own(part).start()
-        for step in range(1, shards):
-            swap_copy(part, step).start()
+        swap_copy(part).start()
+
+    def sum_block(part, owner):
+        return w_out_grad_ref.at[owner] if part == 2 else parts_ref.at[owner, part]
 
     def line_copy(part, origin, toward, lane):
-        block = parts_ref.at[origin * PLANE + x, part]
+        block = sum_block(part, origin * PLANE + x)
         return remote(
             block,
             block,
@@ -1126,15 +1589,14 @@
         )
 
     def side_copy(part, origin, from_x):
-        block = parts_ref.at[origin * PLANE + from_x, part]
+        block = sum_block(part, origin * PLANE + from_x)
         return remote(
             block, block, side_send.at[part, origin], side_recv.at[part, origin], (beside, mine)
         )
 
     def spread_own(part):
         swap_own(part).wait()
-        for step in range(1, shards):
-            swap_copy(part, step).wait_recv()
+        swap_copy(part).wait_recv()
         side_copy(part, z, x).start()
 
         @pl.when(z < LINE - 1)
@@ -1168,9 +1630,13 @@
 
             side_copy(part, origin, x).start()
 
-    sum_groups(0)
-    join_pair(0)
-
+    sum_groups(0, 2)
+    in_given_order(back_ref, inverse_ref, values_ref, values_given_ref, scaled_ref)
+    own_share = share_own(scaled_ref, taken.at[1], local_sem.at[1])
+    own_share.start()
+    for step in rep_steps():
+        share_copy(scaled_ref, taken.at[1], share_send, share_recv, step).start()
+    spread_own(0)
     for step in range(1, shards):
         tail_out_copy(step).wait_recv()
     span = pl.ds(pl.multiple_of(mine * rows, rows), rows)
@@ -1180,39 +1646,44 @@
     tail_low[span, :] = summed_tail.astype(BF)
     for step in range(1, shards):
         tail_back_copy(step).start()
-
-    spread_own(0)
-    sum_groups(1)
+    sum_groups(2, 1)
+    pass_on(0, 1)
+    spread_own(2)
+    for i in range(reps):
+        at, side = place_of(i)
+        if i == 0:
+            own_share.wait()
+        else:
+            share_arrival(taken.at[1], share_recv, at, side)
+        peer_copy(1, at, side).start()
+    pass_on(0, 2)
 
     for step in range(1, shards):
         tail_back_copy(step).wait_recv()
-    for side in range(2):
-        pair_copy(0, side).wait_send()
     heads, share = H // shards, 2 * N // shards
     lane = lax.broadcasted_iota(jnp.int32, (rows, TAIL_PAD), 1)
     owned = ((lane >= mine * share) & (lane < (mine + 1) * share)) | (
         (lane >= 2 * N + mine * heads) & (lane < 2 * N + (mine + 1) * heads)
     )
 
-    def grad_rows(i):
-        span = pl.ds(pl.multiple_of(i * rows, rows), rows)
-        back = back_ref[span, :]
-        tail = dot_nn(back, tail_low[...])
+    def grad_rows(span):
+        tail = dot_nn(back_ref[span, :], tail_low[...])
         tail = jnp.where(owned, tail, 0.0).astype(BF)
-        partial[span, :] = (
-            dot_nn(dot_nn(back, gate_ref[...]).astype(BF), w_gate_ref[...])
-            + dot_nn(dot_nn(back, values_ref[...]).astype(BF), w_conv_ref[0:width, :])
+        return (
+            dot_nn(gate_given_ref[span, :], w_gate_ref[...])
+            + dot_nn(values_given_ref[span, :], w_conv_ref[0:width, :])
             + dot_nn(tail, w_conv_ref[width:, :])
         )
 
-    loads[2].wait()
-    loads[3].wait()
-    each(shards, grad_rows)
-    for side in range(2):
-        pair_copy(1, side).start()
-
+    loads[0].wait()
+    loads[1].wait()
+    rows_sum.fill(grad_rows)
+    pass_on(0, 3)
+    pass_on(2, 1)
+    rows_sum.join()
+    sum_groups(1)
+    pass_on(2, 2)
     spread_own(1)
-    pass_on(0, 1)
 
     own_part.wait()
     tail_sum[...] = dot_tn(tail_low[...], own_columns[...])
@@ -1243,7 +1714,7 @@
     for step in range(1, reps):
         tail_part_copy(step).start()
 
-    branch = joined_rows(0)
+    branch = branch_ref[...]
     whole = resid_ref[...].astype(F32) + branch
     block_out_ref[...] = whole.astype(BF)
     counts = valid_ref[...].astype(F32)
@@ -1255,9 +1726,8 @@
     )
     count = jnp.sum(counts, axis=0, keepdims=True)
 
+    pass_on(2, 3)
     pass_on(1, 1)
-    join_pair(1)
-    pass_on(0, 2)
 
     for step in range(1, reps):
         tail_part_copy(step).wait_recv()
@@ -1271,14 +1741,14 @@
 
     pass_on(1, 2)
 
-    grad_normed = joined_rows(1)
+    grad_normed = rows_sum.result()
     given = x_ref[...].astype(F32)
     inverse = lax.rsqrt(jnp.mean(given * given, axis=1, keepdims=True) + EPSILON)
     grad_norm_gain = jnp.sum(grad_normed * (given * inverse), axis=0, keepdims=True)
     scaled = grad_normed * gain_ref[...]
     pull = inverse * inverse * inverse * jnp.mean(scaled * given, axis=1, keepdims=True)
     span = pl.ds(pl.multiple_of(mine * rows, rows), rows)
-    loads[4].wait()
+    loads[2].wait()
     kept = dot_nn(back_ref[span, :], branch_grad_ref[...])
     grad_in_ref[...] = (scaled * inverse - given * pull + kept).astype(BF)
 
@@ -1333,7 +1803,6 @@
         small_rep_copy(step).start()
     small_in[rep] = small[...]
 
-    pass_on(0, 3)
     for step in range(1, reps):
         small_rep_arrival(step).wait_recv()
     added = small_in[0]
@@ -1381,7 +1850,7 @@
 
     for step in range(1, reps):
         tail_spread_copy(step).wait_recv()
-    for part in range(2):
+    for part in range(3):
         for origin in range(LINE):
             side_copy(part, origin, 1 - x).wait_recv()
             side_copy(part, origin, x).wait_send()
@@ -1394,14 +1863,13 @@
             def _(part=part, origin=origin):
                 line_copy(part, origin, -1, 1).wait_send()
 
-        for step in range(1, shards):
-            swap_copy(part, step).wait_send()
-        for step in range(1, reps):
-            share_copy(part, step).wait_send()
-    for side in range(2):
-        pair_copy(1, side).wait_send()
-    for kind in range(2):
-        row_copy(kind).wait_send()
+        swap_copy(part).wait_send()
+        if part > 0:
+            for i in range(reps):
+                peer_copy(part, *place_of(i)).wait_send()
+    for step in rep_steps():
+        share_copy(scaled_ref, taken.at[1], share_send, share_recv, step).wait_send()
+    rows_sum.finish()
     for step in range(1, shards):
         tail_out_copy(step).wait_send()
         tail_back_copy(step).wait_send()
@@ -1413,9 +1881,8 @@
 
 
 def run_end(operands, shards):
-    gate = operands[0]
     reps = LINE * PLANE
-    length, width = gate.shape
+    length, width = operands[4].shape
     rows, depth = length // shards, D // shards
     dma = pltpu.SemaphoreType.DMA
     vector = pl.BlockSpec(memory_space=pltpu.VMEM)
@@ -1426,7 +1893,8 @@
     return pl.pallas_call(
         end_kernel,
         out_shape=(
-            shape((reps, 2, shards, 128, depth), BF),
+            shape((reps, 2, 2, 256, depth), BF),
+            shape((reps, 128, D), BF),
             shape((TAIL_PAD, depth), BF),
             shape((rows, D), BF),
             shape((rows, D), BF),
@@ -1436,17 +1904,20 @@
             shape((8, 128), F32),
             shape((1, DI), F32),
         ),
-        in_specs=[vector] * 3 + [anywhere] * 5 + [vector, anywhere] + [vector] * 8,
-        out_specs=(anywhere,) + (vector,) * 8,
+        in_specs=[anywhere] * 3 + [vector] * 3 + [anywhere] * 5 + [vector] + [anywhere] * 2 + [vector] * 2 + [anywhere] + [vector] * 8,
+        out_specs=(anywhere,) * 2 + (vector,) * 8,
         scratch_shapes=[
-            pltpu.VMEM((2, reps, length, 128), BF),
-            pltpu.VMEM((2, length, D), BF),
+            pltpu.VMEM((3, LINE, PLANE, length, 128), BF),
+            pltpu.VMEM((3, LINE, PLANE, length, 128), BF),
+            pltpu.VMEM((length, width), BF),
+            pltpu.VMEM((length, width), BF),
+            pltpu.VMEM((2, length, D // 2), BF),
             pltpu.VMEM((length, depth), BF),
-            pltpu.VMEM((128, D), F32),
-            pltpu.VMEM((2, 128, D), BF),
+            pltpu.VMEM((256, D // 2), F32),
+            pltpu.VMEM((3, 256, D // 2), BF),
             pltpu.VMEM((length, D), F32),
-            pltpu.VMEM((2, 2, rows, D), F32),
             pltpu.VMEM((2, rows, D), F32),
+            pltpu.VMEM((rows, D), F32),
             pltpu.VMEM((shards, rows, TAIL_PAD), F32),
             pltpu.VMEM((length, TAIL_PAD), BF),
             pltpu.VMEM((TAIL_PAD, depth), F32),
@@ -1456,22 +1927,22 @@
             pltpu.VMEM((shards, small, 128), F32),
             pltpu.VMEM((width, D), BF),
             pltpu.VMEM((width + TAIL_PAD, D), BF),
-            pltpu.VMEM((width, D), BF),
-            pltpu.VMEM((length, width), BF),
             pltpu.VMEM((length, D), BF),
-            dma((5,)),
-            dma((5,)),
+            dma((3,)),
+            dma((8,)),
             dma((2,)),
-            dma((2, reps)),
-            dma((2, reps)),
-            dma((2, shards)),
-            dma((2, shards)),
-            dma((2, 2, LINE)),
-            dma((2, LINE)),
-            dma((2, LINE)),
-            dma((2, LINE)),
-            dma((2, 3)),
-            dma((2, 3)),
+            dma((LINE, PLANE)),
+            dma((LINE, PLANE)),
+            dma((3, LINE, PLANE)),
+            dma((3, LINE, PLANE)),
+            dma((3,)),
+            dma((3,)),
+            dma((3, 2, LINE)),
+            dma((3, LINE)),
+            dma((3, LINE)),
+            dma((3, LINE)),
+            dma((3,)),
+            dma((3,)),
             dma((2, shards)),
             dma((2, shards)),
             dma((3, reps)),
@@ -1504,12 +1975,14 @@
 
 
 def run_assemble(parts, tail):
-    reps, unused, shards, unused2, depth = parts.shape
+    reps, unused, cores, stack, depth = parts.shape
+    shards = cores * stack // 128
     steps = 2 * shards
 
     def place(i):
         at = jnp.minimum(i, steps - 1)
-        return (0, at // shards, lax.rem(at, shards), 0, 0)
+        shard = lax.rem(at, shards)
+        return (0, at // shards, lax.rem(shard, cores), shard // cores, 0)
 
     return pl.pallas_call(
         assemble_kernel,
@@ -1716,27 +2189,50 @@
             w_out,
         )
     norm_row, valid_column = norm_gain[None, :], valid[:, None]
-    normed, conv_in, gate, w_gate, w_conv, branch_grad, back, place, resid = run_start(
-        seq_lengths, seq_order, x_in, cotangent, valid_column, norm_row, w_in.T, shards
-    )
-    normed_mine = lax.dynamic_slice_in_dim(normed, mine * rows, rows, axis=0)
-    normed_all = lax.all_gather(normed_mine, ALL, axis=0, tiled=True)
-    mixed, starts, normed_out, grad_mixed, grad_gate, grad_gain = run_forward(
-        conv_in, gate, branch_grad, w_out, place, conv_w, bias_row, head_rows, gain_row, shards
-    )
-    grad_w_out = lax.psum(dot_tn(normed_out, branch_grad).astype(BF), "rep").astype(F32)
-    grad_values, grad_tail, grad_conv_w, grad_conv_b, grad_head = run_backward(
-        conv_in, place, conv_w, bias_row, head_rows, mixed, starts, grad_mixed
-    )
-    operands = (
-        grad_gate,
+    normed, conv_in, gate, w_gate, w_conv, branch_grad, back, place, resid, inverse, line, beside = (
+        run_start(seq_lengths, seq_order, x_in, cotangent, valid_column, norm_row, w_in.T, shards)
+    )
+    mixed, starts, normed_out, grad_mixed, grad_gate, grad_gain, side_a, side_b = run_forward(
+        conv_in, gate, branch_grad, w_out, place, conv_w, bias_row, head_rows, gain_row, shards, (line, beside)
+    )
+    (
         grad_values,
         grad_tail,
-        normed_all,
+        grad_conv_w,
+        grad_conv_b,
+        grad_head,
+        gate_taken,
+        out_taken,
+        gate_peer,
+        gate_given,
+        branch,
+    ) = run_backward(
+        conv_in,
+        place,
+        conv_w,
+        bias_row,
+        head_rows,
+        mixed,
+        starts,
+        grad_mixed,
+        (grad_gate, back, inverse, normed_out, w_out),
+    )
+    operands = (
+        gate_taken,
+        gate_peer,
+        out_taken,
+        gate_given,
+        grad_values,
+        grad_tail,
+        normed,
+        line,
+        beside,
+        side_a,
+        side_b,
+        inverse,
         w_gate,
         w_conv,
-        w_out,
-        normed_out,
+        branch,
         back,
         branch_grad,
         x_in,
@@ -1748,9 +2244,19 @@
         grad_head,
         grad_gain,
     )
-    parts, tails, block_out, grad_in, out_norm, out_conv_w, out_conv_b, out_head, out_gain = (
-        run_end(operands, shards)
-    )
+    (
+        parts,
+        w_out_parts,
+        tails,
+        block_out,
+        grad_in,
+        out_norm,
+        out_conv_w,
+        out_conv_b,
+        out_head,
+        out_gain,
+    ) = run_end(operands, shards)
+    grad_w_out = w_out_parts.reshape(width, D).astype(F32)
     grad_w_in = run_assemble(parts, tails).T
     return (
         block_out,

time: 563 us -> 466 us (0.83)
  waiting for transfers between devices: 182 us -> 0 us
  Pallas kernels: 335 us -> 439 us
  between operations: 15.5 us -> 0.93 us
  matrix products: 5.63 us -> 0 us
    psum x1 -> x0, waiting for transfers between devices: 182 us -> none  [on_device(): lax.psum(dot_tn(normed_out, branch_grad).astype(BF), 'rep').astype(F32)]
    pallas_call x3, Pallas kernels: 236 us -> 316 us  [the longest x1 198 us: run_end(): pl.pallas_call(end_kernel, out_shape=(shape((reps, 2, 2, 256, depth), BF)...]
    pallas_call x1, Pallas kernels: 88 us -> 113 us  [run_start(): pl.pallas_call(start_kernel, out_shape=(shape((length, D), BF), shape((le...]
  transfers between devices with their start and end apart: 2 -> 0, of which waited for: 1 -> 0; matrix products, arithmetic and copies ran while one was open for 2% -> 0% of each run, Pallas kernels for 5% -> 0%
where the time goes in v4:
time: 466 us; the launch traced here: 458 us
  Pallas kernels  439 us (94%)
  other arithmetic  9.31 us (2%)
  local copies, waits for them, and re-layouts  8.83 us (2%)
    pallas_call x1, Pallas kernels, run_end(): pl.pallas_call(end_kernel, out_shape=(shape((reps, 2, 2, 256, depth), BF)...  198 us
    pallas_call x1, Pallas kernels, run_start(): pl.pallas_call(start_kernel, out_shape=(shape((length, D), BF), shape((le...  113 us
    pallas_call x1, Pallas kernels, run_backward(): pl.pallas_call(functools.partial(backward_kernel, spans), out_shape=(shap...  66.6 us
    pallas_call x1, Pallas kernels, run_forward(): pl.pallas_call(functools.partial(forward_kernel, spans), out_shape=(shape...  51.4 us
    pallas_call x1, Pallas kernels, run_assemble(): pl.pallas_call(assemble_kernel, grid=(steps + 1,), out_shape=jax.ShapeDty...  10.7 us

profile of v4, /device:TPU:0, one launch (start us, length us, event | category | flops | bytes accessed | tf_op | source)
XLA Modules:
  0.0 458.1 jit_solution(12229626572861021506)
XLA Ops:
  0.6 1.3 select_maximum_fusion.refs_7_.refs_4_
  1.9 1.3 broadcast_in_dim.14.refs_6_.refs_3_
  3.3 1.4 copy.27.valid_ref
  4.7 112.5 %project.1 = (bf16[512,2048]{1,0:T(8,128)(2,1)}, bf16[512,1408]{1,0:T(8,128)(2,1)}, bf16[512,1024]{1,0:T(8,128)(2,1)}, bf16[1024,2048]{1,0:T(8,128)(2,1)}, bf16[...) custom-call(s32[1,4]{1,0:T(1,128)} %lengths_ref.1, ...), custom_call_target="tpu_custom_call" | custom-call | flops 5100273664 | bytes 50331648 | tf_op jit(solution)/shard_map/project/pallas_call | solution.py:535
  117.2 51.4 %mixer_forward.1 = (f32[512,1024]{1,0:T(8,128)}, f32[512,1024]{1,0:T(8,128)}, bf16[512,1024]{1,0:T(8,128)(2,1)}, f32[512,1024]{1,0:T(8,128)}, bf16[512,1024]{1,0...) custom-call(bf16[512,1408]{1,0:T(8,128)(2,1)} %get-tuple-element.53.refs_0_, ...), custom_call_target="tpu_custom_call" | custom-call | flops 1342177280 | bytes 6291456 | tf_op jit(solution)/shard_map/mixer_forward/pallas_call | solution.py:1221
  168.6 66.6 %mixer_backward.1 = (bf16[512,1024]{1,0:T(8,128)(2,1)}, f32[512,384]{1,0:T(8,128)}, f32[4,1280]{1,0:T(4,128)}, f32[1,1280]{1,0:T(1,128)}, f32[8,128]{1,0:T(8,128...) custom-call(bf16[512,1408]{1,0:T(8,128)(2,1)} %get-tuple-element.53., ...), custom_call_target="tpu_custom_call" | custom-call | flops 2684354560 | bytes 10485760 | tf_op jit(solution)/shard_map/mixer_backward/pallas_call | solution.py:1268
  235.3 197.6 %weight_gradient.1 = (bf16[8,2,2,256,512]{4,3,2,1,0:T(8,128)(2,1)}, bf16[8,128,2048]{2,1,0:T(8,128)(2,1)}, bf16[384,512]{1,0:T(8,128)(2,1)}, bf16[128,2048]{1,0:...) custom-call(bf16[4,2,512,128]{3,2,1,0:T(8,128)(2,1)} %get-tuple-elem, ...), custom_call_target="tpu_custom_call" | custom-call | flops 4294967296 | bytes 100663296 | tf_op jit(solution)/shard_map/weight_gradient/pallas_call | solution.py:1893
  432.9 1.3 fusion
  434.3 1.3 slice_bitcast_fusion
  435.6 1.4 reduce
  437.0 6.7 %bitcast_convert_fusion = f32[1024,2048]{1,0:T(8,128)} fusion(bf16[8,128,2048]{2,1,0:T(8,128)(2,1)} %get-tuple-element.92), kind=kLoop, calls=%fused_computation | loop fusion | flops 2097152 | bytes 12582912 | tf_op jit(solution)/shard_map/convert_element_type | solution.py:2259
  443.6 0.0 copy-start.1
  443.6 0.0 copy-start
  443.6 0.0 copy-start.4
  443.6 0.0 copy-start.2
  443.6 0.0 copy-start.3
  443.6 10.7 %assemble.1 = f32[8512,512]{1,0:T(8,128)} custom-call(bf16[8,2,2,256,512]{4,3,2,1,0:T(8,128)(2,1)} %get-tuple-element.86.parts_ref, bf16[384,512]{1,0:T(8,128)(2,1)} %get-tuple-element.87.tail_ref), custom_call_target="tpu_custom_call" | custom-call | tf_op jit(solution)/shard_map/assemble/pallas_call | solution.py:1987
  454.4 0.0 copy-done.1
  454.4 0.8 copy.34
  455.2 0.0 copy-done
  455.2 0.8 copy.35
  456.0 0.0 copy-done.4
  456.0 0.6 copy.36
  456.6 0.0 copy-done.2
  456.6 0.6 copy.37
  457.2 0.0 copy-done.3
  457.2 0.6 copy.38
Async XLA Ops:
  443.6 10.8 %copy-start.1 = (bf16[128,2048]{1,0:T(8,128)(2,1)S(1)}, bf16[128,2048]{1,0:T(8,128)(2,1)}, u32[]{:S(2)}) copy-start(bf16[128,2048]{1,0:T(8,128)(2,1)} %get-tuple-element.111) | copy-start | bytes 1572868
  443.6 11.6 %copy-start = (bf16[128,2048]{1,0:T(8,128)(2,1)S(1)}, bf16[128,2048]{1,0:T(8,128)(2,1)}, u32[]{:S(2)}) copy-start(bf16[128,2048]{1,0:T(8,128)(2,1)} %get-tuple-element.112) | copy-start | bytes 1572868
  443.6 12.4 %copy-start.4 = (f32[1,2048]{1,0:T(1,128)S(1)}, f32[1,2048]{1,0:T(1,128)}, u32[]{:S(2)}) copy-start(f32[1,2048]{1,0:T(1,128)} %get-tuple-element.85) | copy-start | bytes 24580
  443.6 13.0 %copy-start.2 = (f32[4,4352]{1,0:T(4,128)S(1)}, f32[4,4352]{1,0:T(4,128)}, u32[]{:S(2)}) copy-start(f32[4,4352]{1,0:T(4,128)} %get-tuple-element.115) | copy-start | bytes 208900
  443.6 13.6 %copy-start.3 = (f32[1,4096]{1,0:T(1,128)S(1)}, f32[1,4096]{1,0:T(1,128)}, u32[]{:S(2)}) copy-start(f32[1,4096]{1,0:T(1,128)} %get-tuple-element.91) | copy-start | bytes 49156
